TPU v7x, 128 devices: a whole 4x4x4 slice. The times are simulated.
128 devices in a mesh: dp: 4 (over x), seq: 32 (over z, y, core).
Axes of the slice: x: 4, y: 4, z: 4, core: 2. Of those that a mesh axis runs over, the one named last changes fastest.
Arguments:
- ssm_input: bfloat16 [4, 8192, 3072], P('dp', 'seq'), may hold values from -6 to 6
- gate_input: bfloat16 [4, 8192, 3072], P('dp', 'seq'), may hold values from -6 to 6
- input_map: bfloat16 [4, 8192, 128], P('dp', 'seq'), may hold values from -0.52734375 to 0.52734375
- output_map: bfloat16 [4, 8192, 128], P('dp', 'seq'), may hold values from -6 to 6
- step_logit: bfloat16 [4, 8192, 48], P('dp', 'seq'), may hold values from -5 to 5
- step_bias: float32 [48], replicated, may hold values from -1 to 1
- decay_rate: float32 [48], replicated, may hold values from 6.1035156e-07 to 0.05
- skip_gain: float32 [48], replicated, may hold values from 0.5 to 1.5
- norm_gain: float32 [3072], replicated, may hold values from 0.1 to 1.9
- out_weight: bfloat16 [3072, 1536], replicated, may hold values from -0.109375 to 0.109375
- resets: int32 [4, 4], P('dp'), may hold values from 1 to 8191
- out_grad: bfloat16 [4, 8192, 1536], P('dp', 'seq'), may hold values from -6 to 6
Outputs:
- mixed_out: bfloat16 [4, 8192, 1536], P('dp', 'seq')
- grad_input: bfloat16 [4, 8192, 3072], P('dp', 'seq')
- grad_gate: bfloat16 [4, 8192, 3072], P('dp', 'seq')
- grad_inmap: bfloat16 [4, 8192, 128], P('dp', 'seq')
- grad_outmap: bfloat16 [4, 8192, 128], P('dp', 'seq')
- grad_step: bfloat16 [4, 8192, 48], P('dp', 'seq')
- grad_bias: float32 [48], replicated
- grad_rate: float32 [48], replicated
- grad_skip: float32 [48], replicated
- grad_gain: float32 [3072], replicated
- grad_weight: float32 [3072, 1536], P('seq')
All inputs are finite; a program needn't handle non-finite values.
Results may differ from a plain program's by a relative error of at most 0.0049.
Values sent between devices are 32-bit elements; how exact they have to be, the bound alone decides.
A program may use at most 384 MiB of HBM per device.

v0:
```python
import jax
import jax.numpy as jnp
from jax import lax
from jax.sharding import PartitionSpec as P

SPAN = 128


highest = lax.Precision.HIGHEST


def prefix(shard, axis, combine, identity, reverse):
    count, place = (lax.axis_size(axis), lax.axis_index(axis))
    everything = jax.tree.map(lambda part: lax.all_gather(part, axis), shard)
    start = jax.tree.map(
        lambda part, zero: jnp.broadcast_to(jnp.asarray(zero, part.dtype), part.shape),
        shard,
        identity,
    )

    def hop(k, before):
        at = count - 1 - k if reverse else k
        reached = at > place if reverse else at < place
        new = combine(before, jax.tree.map(lambda part: part[at], everything))
        return jax.tree.map(lambda a, b: jnp.where(reached, a, b), new, before)

    return lax.fori_loop(0, count, hop, start)


def block_step(state_in, inputs):
    x_blk, b_blk, c_blk, step_blk, decay_blk, flag_blk = inputs
    cumulative = jnp.cumsum(decay_blk, axis=0)
    counts = jnp.cumsum(flag_blk)
    block_len = flag_blk.shape[0]
    row_ids = lax.broadcasted_iota(jnp.int32, (block_len, block_len), 0)
    col_ids = lax.broadcasted_iota(jnp.int32, (block_len, block_len), 1)
    in_mask = ((row_ids >= col_ids) & (counts[:, None] == counts[None, :]))[:, :, None]
    gap_vals = cumulative[:, None, :] - cumulative[None, :, :]
    decay_mat = jnp.where(in_mask, jnp.exp(jnp.where(in_mask, gap_vals, 0.0)), 0.0)
    gram_mat = jnp.einsum("in,jn->ij", c_blk, b_blk, precision=highest)
    mixing = gram_mat[:, :, None] * decay_mat * step_blk[None, :, :]
    y_blk = jnp.einsum("ijh,jhp->ihp", mixing, x_blk, precision=highest)
    opened = (counts == 0)[:, None]
    from_start = jnp.where(opened, jnp.exp(jnp.where(opened, cumulative, 0.0)), 0.0)
    y_blk = y_blk + from_start[:, :, None] * jnp.einsum(
        "in,hpn->ihp", c_blk, state_in, precision=highest
    )
    keep_mask = (counts == counts[-1])[:, None]
    tail_weights = (
        jnp.where(
            keep_mask, jnp.exp(jnp.where(keep_mask, cumulative[-1][None, :] - cumulative, 0.0)), 0.0
        )
        * step_blk
    )
    whole_decay = jnp.where(counts[-1] == 0, jnp.exp(cumulative[-1]), 0.0)
    new_state = whole_decay[:, None, None] * state_in + jnp.einsum(
        "jhp,jn->hpn", tail_weights[:, :, None] * x_blk, b_blk, precision=highest
    )
    return (new_state, y_blk)


def ssd_blocks(x_heads, b_float, c_float, step_vals, log_decay, flags, state_in):
    num_blocks = x_heads.shape[0] // SPAN

    def to_blocks(values):
        return values.reshape((num_blocks, SPAN) + values.shape[1:])

    final_state, y_blocks = lax.scan(
        block_step,
        state_in,
        (
            to_blocks(x_heads),
            to_blocks(b_float),
            to_blocks(c_float),
            to_blocks(step_vals),
            to_blocks(log_decay),
            to_blocks(flags),
        ),
    )
    return (final_state, y_blocks.reshape(x_heads.shape))


def gate_norm(y_ssd, x_float, z_float, skip_gain, norm_gain):
    num_heads = skip_gain.shape[0]
    rows_here = x_float.shape[0]
    y_full = y_ssd.reshape(rows_here, -1) + (
        x_float.reshape(rows_here, num_heads, -1) * skip_gain[None, :, None]
    ).reshape(x_float.shape)
    gated_vals = y_full * jax.nn.silu(z_float)
    scale_inv = lax.rsqrt(jnp.mean(gated_vals * gated_vals, axis=-1, keepdims=True) + 1e-05)
    return gated_vals * scale_inv * norm_gain


def step_sizes(logit_vals, bias_in, rate_in):
    step_vals = jax.nn.softplus(logit_vals + bias_in)
    return (step_vals, -rate_in * step_vals)


def combine(earlier, later):
    return (earlier[0] * later[0], later[0][:, None, None] * earlier[1] + later[1])


def per_device(
    ssm_input,
    gate_input,
    input_map,
    output_map,
    step_logit,
    step_bias,
    decay_rate,
    skip_gain,
    norm_gain,
    out_weight,
    resets,
    out_grad,
):
    rows_here = ssm_input.shape[1]
    num_heads = step_bias.shape[0]
    x_float = ssm_input[0].astype(jnp.float32)
    z_float = gate_input[0].astype(jnp.float32)
    b_float = input_map[0].astype(jnp.float32)
    c_float = output_map[0].astype(jnp.float32)
    logit_float = step_logit[0].astype(jnp.float32)
    inner_width = x_float.shape[1]
    head_size = inner_width // num_heads
    x_heads = x_float.reshape(rows_here, num_heads, head_size)
    positions = lax.axis_index("seq") * rows_here + lax.iota(jnp.int32, rows_here)
    flags = jnp.max((positions[:, None] == resets[0][None, :]).astype(jnp.int32), axis=1)
    counts = jnp.cumsum(flags)
    opened = (counts == 0)[:, None]
    clean_shard = counts[-1] == 0
    empty_state = jnp.zeros((num_heads, head_size, b_float.shape[1]), jnp.float32)
    identity = (jnp.ones((num_heads,), jnp.float32), empty_state)
    step_vals, log_decay = step_sizes(logit_float, step_bias, decay_rate)
    cumulative = jnp.cumsum(log_decay, axis=0)
    from_start = jnp.where(opened, jnp.exp(jnp.where(opened, cumulative, 0.0)), 0.0)
    shard_through = jnp.where(clean_shard, jnp.exp(cumulative[-1]), 0.0)
    step_vals, cumulative, from_start, through = (step_vals, cumulative, from_start, shard_through)
    keep_mask = (counts == counts[-1])[:, None]
    tail_weights = (
        jnp.where(
            keep_mask, jnp.exp(jnp.where(keep_mask, cumulative[-1][None, :] - cumulative, 0.0)), 0.0
        )
        * step_vals
    )
    shard_state = jnp.einsum(
        "thp,tn->hpn", tail_weights[:, :, None] * x_heads, b_float, precision=highest
    )
    incoming = prefix((through, shard_state), "seq", combine, identity, False)[1]

    def from_incoming(x_part, b_part, c_part, logit_vals, bias_in, rate_in):
        step_part, decay_part = step_sizes(logit_vals, bias_in, rate_in)
        return ssd_blocks(x_part, b_part, c_part, step_part, decay_part, flags, incoming)

    (final_state, y_ssd), ssd_pullback = jax.vjp(
        from_incoming, x_heads, b_float, c_float, logit_float, step_bias, decay_rate
    )
    normed_f, post_pullback = jax.vjp(gate_norm, y_ssd, x_float, z_float, skip_gain, norm_gain)
    normed = normed_f.astype(jnp.bfloat16)
    mixed = jnp.dot(normed, out_weight, preferred_element_type=jnp.float32).astype(jnp.bfloat16)
    grad_rows = out_grad[0]
    normed_grad = lax.dot_general(
        grad_rows, out_weight, (((1,), (1,)), ((), ())), preferred_element_type=jnp.float32
    )
    y_grad, x_grad_skip, z_grad, skip_grad, gain_grad = post_pullback(normed_grad)
    start_grad = jnp.einsum(
        "thp,tn->hpn", from_start[:, :, None] * y_grad, c_float, precision=highest
    )
    later_grad = prefix((through, start_grad), "seq", combine, identity, True)[1]
    x_grad, b_grad, c_grad, logit_grad, bias_grad, rate_grad = ssd_pullback((later_grad, y_grad))
    bias_sum, rate_sum, skip_sum, gain_sum = lax.psum(
        (bias_grad, rate_grad, skip_grad, gain_grad), ("dp", "seq")
    )
    seq_rows = lax.psum_scatter(
        lax.dot_general(
            normed, grad_rows, (((0,), (0,)), ((), ())), preferred_element_type=jnp.float32
        ),
        "seq",
        scatter_dimension=0,
        tiled=True,
    )
    weight_grad = lax.psum(seq_rows, "dp")
    grad_input = (x_grad.reshape(rows_here, inner_width) + x_grad_skip).astype(jnp.bfloat16)
    return (
        mixed[None],
        grad_input[None],
        z_grad.astype(jnp.bfloat16)[None],
        b_grad.astype(jnp.bfloat16)[None],
        c_grad.astype(jnp.bfloat16)[None],
        logit_grad.astype(jnp.bfloat16)[None],
        bias_sum,
        rate_sum,
        skip_sum,
        gain_sum,
        weight_grad,
    )


def solution(mesh):
    placed = (
        P("dp", "seq", None),
        P("dp", "seq", None),
        P("dp", "seq", None),
        P("dp", "seq", None),
        P("dp", "seq", None),
        P(),
        P(),
        P(),
        P(),
        P(),
        P("dp", None),
        P("dp", "seq", None),
    )
    return jax.shard_map(
        per_device,
        mesh=mesh,
        in_specs=placed,
        out_specs=(
            P("dp", "seq", None),
            P("dp", "seq", None),
            P("dp", "seq", None),
            P("dp", "seq", None),
            P("dp", "seq", None),
            P("dp", "seq", None),
            P(),
            P(),
            P(),
            P(),
            P("seq", None),
        ),
        check_vma=False,
    )
```

profile of v0, /device:TPU:0, one launch (start us, length us, event | category | flops | bytes accessed | tf_op | source)
XLA Modules:
  0.0 972.9 jit_solution(15452090480564412764)
XLA Ops:
  21.5 4.1 convert_multiply_fusion
  29.2 4.5 fusion.162
  37.1 5.3 reshape.1003
  49.7 5.2 reshape.1008
  55.6 22.9 %all-gather.2 = f32[32,1,48]{2,1,0:T(1,128)S(1)} all-gather(f32[1,1,48]{2,1,0:T(1,128)S(1)} %bitcast.581), channel_id=1, replica_groups=mesh['dp'=4,'seq'=32] {'seq'}, dimensions={0}, use_global_device_ids=true | all-gather | bytes 6336 | tf_op jit(solution)/shard_map/all_gather | solution.py:14
  78.7 115.3 %all-gather.6.cloned.1.call-done = f32[1536,64,128]{2,1,0:T(8,128)} async-done(((f32[48,64,128]{2,1,0:T(8,128)}), f32[1536,64,128]{2,1,0:T(8,128)}) %all-gather.6.cloned.1.call-update) | async-done | bytes 50331664 | tf_op jit(solution)/shard_map/all_gather | solution.py:14
  193.9 58.0 %while.116 = (s32[]{:T(128)}, f32[48,64,128]{2,1,0:T(8,128)S(1)}, s32[]{:T(128)}, f32[32,48]{1,0:T(8,128)S(1)}, f32[32,48,64,128]{3,2,1,0:T(8,128)}, /*index=5*/s32[]{:T(128)}, s32[]{:T(128)}) while((s32[]{:T(128)}, f32[48,64,128]{2,1,0:T(8,128)S(1)}, s32[]{:T(128)}, f32[32,48]{1,0:T(8,128)S(1)}, f32[32,48,64,128]{3,2,1,0:T(8,128)}, ...), condition=%wide.region_6.7_spmd.clone, body=%wide.region_5.6_spmd.clone.sunk | while | flops 1572868 | bytes 4719273 | solution.py:27
  258.1 154.5 %while.115 = (s32[]{:T(128)}, f32[48,64,128]{2,1,0:T(8,128)S(1)}, f32[2,128,48,64]{1,3,2,0:T(8,128)}, pred[2,128,128,48]{2,1,3,0:T(32,128)(4,1)}, f32[2,128,128,...) while((s32[]{:T(128)}, f32[48,64,128]{2,1,0:T(8,128)S(1)}, ...), condition=%wide.region_10.11_spmd.clone, body=%wide.region_7.10_spmd.clone.sunk | while | flops 1848273152 | bytes 111490832 | solution.py:68
  261.7 11.3 %broadcast_multiply_fusion.4 = (f32[1,128,128,48]{3,2,1,0:T(8,128)}, f32[1,128,128,48]{3,2,1,0:T(8,128)}, f32[1,128,128,48]{3,2,1,0:T(8,128)}, f32[1,128,128,48]{3,2,1,0:T(8,128)}) fusion(f32[128,48]{1,0:T(8,128)S(1)} %get-tuple-element.2450, f32[128,48]{1,0:T(8,128)S(1)} %reduce_window_sum.92, pred[128,128]{1,0:T(8,128)(4,1)S(1)} %fusion.251, ...), kind=kLoop, calls=%fused_computation.99.clone.1 | loop fusion | flops 3932160 | bytes 12713984 | tf_op jit(solution)/shard_map/jvp()/while/body/eval_jaxpr/mul | solution.py:41
  273.0 6.9 copy.272
  279.9 6.8 copy.273
  286.8 6.3 constant_dynamic-update-slice_fusion.23
  293.0 6.9 copy.269
  299.9 6.8 copy.270
  306.7 6.4 constant_dynamic-update-slice_fusion.21
  315.9 7.6 bitcast_dynamic-update-slice_fusion.13
  338.8 11.3 %broadcast_multiply_fusion.4 = (f32[1,128,128,48]{3,2,1,0:T(8,128)}, f32[1,128,128,48]{3,2,1,0:T(8,128)}, f32[1,128,128,48]{3,2,1,0:T(8,128)}, f32[1,128,128,48]{3,2,1,0:T(8,128)}) fusion(f32[128,48]{1,0:T(8,128)S(1)} %get-tuple-element.2450, f32[128,48]{1,0:T(8,128)S(1)} %reduce_window_sum.92, pred[128,128]{1,0:T(8,128)(4,1)S(1)} %fusion.251, ...), kind=kLoop, calls=%fused_computation.99.clone.1 | loop fusion | flops 3932160 | bytes 12713984 | tf_op jit(solution)/shard_map/jvp()/while/body/eval_jaxpr/mul | solution.py:41
  350.1 6.9 copy.272
  356.9 6.8 copy.273
  363.8 6.3 constant_dynamic-update-slice_fusion.23
  370.1 6.9 copy.269
  376.9 6.8 copy.270
  383.8 6.4 constant_dynamic-update-slice_fusion.21
  393.0 7.6 bitcast_dynamic-update-slice_fusion.13
  412.6 7.7 multiply_reduce_fusion.2
  424.2 7.8 fusion.146
  438.4 6.5 copy.180
  444.9 6.3 reshape.1022
  451.3 10.8 %multiply_reduce_fusion = (f32[3072]{0:T(1024)}, f32[256]{0:T(256)S(1)}, f32[256,3072]{1,0:T(8,128)S(1)}) fusion(f32[256]{0:T(256)S(1)} %bitcast_rsqrt_fusion, bf16[1,256,3072]{2,1,0:T(8,128)(2,1)} %param.21, f32[256,3072]{1,0:T(8,128)} %reshape.1022, f32[3072]{0:T(1024)S(1)} %mul.708, bf16[1,256,3072]{2,1,0:T(8,128)(2,1)S(1)} %copy-done.8, ...), kind=kOutput, calls=%fused_computation.207 | convolution fusion | flops 2427712256 | bytes 19699712 | tf_op jit(solution)/shard_map/dot_general | solution.py:162
  469.8 4.1 copy.154
  473.9 4.6 fusion.160
  479.3 6.1 reshape.1023
  485.4 7.0 copy.158
  493.1 9.9 %fusion.143 = bf16[1,256,1536]{2,1,0:T(8,128)(2,1)} fusion(bf16[3072,1536]{1,0:T(8,128)(2,1)} %param.29, f32[3072]{0:T(1024)S(1)} %copy-done.27, f32[256]{0:T(256)S(1)} %bitcast_rsqrt_fusion, f32[256,3072]{1,0:T(8,128)} %reshape.1022, bf16[1,256,3072]{2,1,0:T(8,128)(2,1)} %param.20, f32[3072]{0:T(1024)S(1)} %mul.708, bf16[1,256,3072]{2,1,0:T(8,128)(2,1)} %param.21), kind=kOutput, calls=%fused_computation.213 | convolution fusion | flops 2425749504 | bytes 16540672 | tf_op jit(solution)/shard_map/dot_general | solution.py:160
  503.0 49.9 %reduce-scatter.2.cloned.1.call-done = f32[96,1536]{1,0:T(8,128)} async-done(((f32[3072,1536]{1,0:T(8,128)}), f32[96,1536]{1,0:T(8,128)}) %reduce-scatter.2.cloned.1.call-update) | async-done | bytes 589840 | tf_op jit(solution)/shard_map/reduce_scatter | solution.py:174
  552.9 159.7 %all-gather.8.cloned.1.call-done = f32[1536,64,128]{2,1,0:T(8,128)} async-done(((f32[48,64,128]{2,1,0:T(8,128)}), f32[1536,64,128]{2,1,0:T(8,128)}) %all-gather.8.cloned.1.call-update) | async-done | bytes 50331664 | tf_op jit(solution)/shard_map/all_gather | solution.py:14
  712.7 79.8 %while.117 = (s32[]{:T(128)}, f32[48,64,128]{2,1,0:T(8,128)S(1)}, s32[]{:T(128)}, f32[32,48]{1,0:T(8,128)}, f32[32,48,64,128]{3,2,1,0:T(8,128)}, /*index=5*/s32[]{:T(128)}, s32[]{:T(128)}, s32[]{:T(128)}, s32[]{:T(128)}) while((s32[]{:T(128)}, f32[48,64,128]{2,1,0:T(8,128)S(1)}, s32[]{:T(128)}, f32[32,48]{1,0:T(8,128)}, ...), condition=%wide.region_14.15_spmd.clone, body=%wide.region_13.14_spmd.clone.sunk | while | flops 1572872 | bytes 4719335 | solution.py:27
  796.7 83.0 %while.114 = (s32[]{:T(128)}, f32[48,64,128]{2,1,0:T(8,128)S(1)}, f32[2,128,48,64]{1,3,2,0:T(8,128)}, bf16[2,128,128]{2,1,0:T(8,128)(2,1)}, bf16[2,128,128]{2,1,...) while((s32[]{:T(128)}, f32[48,64,128]{2,1,0:T(8,128)S(1)}, ...), condition=%wide.region_25.26_spmd, body=%wide.region_15.25_spmd.sunk | while | flops 3688450048 | bytes 77251128 | solution.py:68
  797.6 11.1 %fusion.235 = (f32[128,48]{0,1:T(8,128)S(1)}, f32[128,48]{0,1:T(8,128)S(1)}, f32[128,128]{1,0:T(8,128)S(1)}, f32[128,48]{0,1:T(8,128)S(1)}) fusion(f32[2,128,128,48]{2,1,3,0:T(8,128)} %get-tuple-element.2728, s32[]{:T(128)S(6)} %sub.274, f32[128,48]{0,1:T(8,128)S(1)} %dynamic-slice_bitcast_fusion.18, ...), kind=kOutput, calls=%fused_computation.91.clone.1 | convolution fusion | flops 612595712 | bytes 13600256 | tf_op jit(solution)/shard_map/transpose(jvp())/while/body/eval_jaxpr/ijh,jhp->ihp/dot_general | solution.py:42
  820.6 4.7 fusion.237
  830.6 5.5 bitcast_dynamic-update-slice_fusion.10
  839.0 11.1 %fusion.235 = (f32[128,48]{0,1:T(8,128)S(1)}, f32[128,48]{0,1:T(8,128)S(1)}, f32[128,128]{1,0:T(8,128)S(1)}, f32[128,48]{0,1:T(8,128)S(1)}) fusion(f32[2,128,128,48]{2,1,3,0:T(8,128)} %get-tuple-element.2728, s32[]{:T(128)S(6)} %sub.274, f32[128,48]{0,1:T(8,128)S(1)} %dynamic-slice_bitcast_fusion.18, ...), kind=kOutput, calls=%fused_computation.91.clone.1 | convolution fusion | flops 612595712 | bytes 13600256 | tf_op jit(solution)/shard_map/transpose(jvp())/while/body/eval_jaxpr/ijh,jhp->ihp/dot_general | solution.py:42
  862.0 4.7 fusion.237
  871.9 5.4 bitcast_dynamic-update-slice_fusion.10
  881.8 6.1 copy.183
  887.9 5.8 reshape.1024
  894.5 65.2 %all-reduce.2 = (f32[48]{0:T(128)}, f32[48]{0:T(128)}, f32[48]{0:T(128)}, f32[3072]{0:T(1024)}) all-reduce(f32[48]{0:T(128)S(1)} %get-tuple-element.1778, f32[48]{0:T(128)S(1)} %neg.49, f32[48]{0:T(128)S(1)} %copy-done.36, f32[3072]{0:T(1024)S(1)} %copy-done.32), channel_id=1, replica_groups=mesh['dp'=4,'seq'=32] {'dp','seq'}, use_global_device_ids=true, to_apply=%region_27.28 | all-reduce | flops 3216 | bytes 25728 | tf_op jit(solution)/shard_map/psum | solution.py:171
  959.7 4.6 fusion.145
  (465 shorter events, 273.0 us)
Async XLA Ops:
  7.2 417.0 %copy-start = (bf16[1,256,1536]{2,1,0:T(8,128)(2,1)S(1)}, bf16[1,256,1536]{2,1,0:T(8,128)(2,1)}, u32[]{:S(2)}) copy-start(bf16[1,256,1536]{2,1,0:T(8,128)(2,1)} %param.31) | copy-start | bytes 2359300
  7.2 186.8 %all-gather.6.cloned.1.call-start = ((), (), s32[]{:S(2)}) async-start(), calls=%async_computation.3 | async-start | bytes 51904512 | tf_op jit(solution)/shard_map/all_gather | solution.py:14
  12.5 66.1 %copy-start.33 = (f32[48]{0:T(128)}, f32[48]{0:T(128)S(1)}, u32[]{:S(2)}) copy-start(f32[48]{0:T(128)S(1)} %neg.43) | copy-start | bytes 580
  17.8 3.7 copy-start.7
  25.6 3.6 copy-start.16
  29.2 4.6 copy-start.14
  33.8 519.1 %reduce-scatter.2.cloned.1.call-start = ((), (), s32[]{:S(2)}) async-start(), calls=%async_computation.1 | async-start | bytes 19464192 | tf_op jit(solution)/shard_map/reduce_scatter | solution.py:174
  33.9 44.6 %copy-start.12 = (f32[1,256,48]{2,1,0:T(8,128)}, f32[1,256,48]{2,1,0:T(8,128)S(1)}, u32[]{:S(2)}) copy-start(f32[1,256,48]{2,1,0:T(8,128)S(1)} %copy.179) | copy-start | bytes 147460
  42.5 4.0 copy-start.17
  49.7 5.2 copy-start.26
  49.7 28.9 %copy-start.29 = (f32[48]{0:T(128)S(1)}, f32[48]{0:T(128)}, u32[]{:S(2)}) copy-start(f32[48]{0:T(128)} %param.25) | copy-start | bytes 580
  252.0 4.1 copy-start.28
  329.6 3.5 copy-start.40
  329.6 3.6 copy-start.31
  329.6 3.6 copy-start.37
  329.6 4.9 copy-start.43
  406.6 3.5 copy-start.31
  406.6 3.6 copy-start.37
  406.6 4.9 copy-start.43
  412.5 7.7 copy-start.20
  432.0 280.7 %all-gather.8.cloned.1.call-start = ((), (), s32[]{:S(2)}) async-start(), calls=%async_computation.4 | async-start | bytes 51904512 | tf_op jit(solution)/shard_map/all_gather | solution.py:14
  444.9 6.3 copy-start.8
  444.9 6.4 copy-start.27
  451.3 10.8 %copy-start.10 = (f32[256,3072]{1,0:T(8,128)S(1)}, f32[256,3072]{1,0:T(8,128)}, u32[]{:S(2)}) copy-start(f32[256,3072]{1,0:T(8,128)} %reshape.1022) | copy-start | bytes 9437188
  451.3 10.8 %copy-start.11 = (bf16[1,256,3072]{2,1,0:T(8,128)(2,1)S(1)}, bf16[1,256,3072]{2,1,0:T(8,128)(2,1)}, u32[]{:S(2)}) copy-start(bf16[1,256,3072]{2,1,0:T(8,128)(2,1)} %param.21) | copy-start | bytes 4718596
  462.1 5.6 copy-start.9
  469.8 4.1 copy-start.18
  478.6 485.7 %all-reduce.5.cloned.1.call-start = ((), (), s32[]{:S(2)}) async-start(), calls=%async_computation.2 | async-start | bytes 1179648 | tf_op jit(solution)/shard_map/psum | solution.py:182
  792.5 4.2 copy-start.23
  792.5 4.1 copy-start.39
  792.5 4.1 copy-start.42
  792.5 4.1 copy-start.45
  796.6 84.8 %copy-start.13 = (f32[1,256,48]{2,1,0:T(8,128)S(1)}, f32[1,256,48]{2,1,0:T(8,128)}, u32[]{:S(2)}) copy-start(f32[1,256,48]{2,1,0:T(8,128)} %copy-done.12) | copy-start | bytes 147460
  796.7 84.8 %copy-start.30 = (f32[48]{0:T(128)S(1)}, f32[48]{0:T(128)}, u32[]{:S(2)}) copy-start(f32[48]{0:T(128)} %param.25) | copy-start | bytes 580
  796.7 84.8 %copy-start.34 = (f32[48]{0:T(128)S(1)}, f32[48]{0:T(128)}, u32[]{:S(2)}) copy-start(f32[48]{0:T(128)} %copy-done.33) | copy-start | bytes 580
  797.6 11.2 %copy-start.5 = (f32[2,48,64,128]{3,2,1,0:T(8,128)S(1)}, f32[2,48,64,128]{3,2,1,0:T(8,128)}, u32[]{:S(2)}) copy-start(f32[2,48,64,128]{3,2,1,0:T(8,128)} %get-tuple-element.2715) | copy-start | bytes 9437188 | tf_op jit(solution)/shard_map/transpose(jvp())/while
  820.6 9.6 copy-start.24
  820.6 9.9 %copy-start.1 = (f32[2,128,48,64]{1,3,2,0:T(8,128)S(1)}, f32[2,128,48,64]{1,3,2,0:T(8,128)}, u32[]{:S(2)}) copy-start(f32[2,128,48,64]{1,3,2,0:T(8,128)} %get-tuple-element.2706) | copy-start | bytes 9437188 | tf_op jit(solution)/shard_map/transpose(jvp())/while
  820.6 9.9 %copy-start.4 = (f32[128,48,64]{0,2,1:T(8,128)S(1)}, f32[128,48,64]{0,2,1:T(8,128)}, u32[]{:S(2)}) copy-start(f32[128,48,64]{0,2,1:T(8,128)} %get-tuple-element.2407) | copy-start | bytes 4718596 | tf_op jit(solution)/shard_map/transpose(jvp())/while
  830.5 5.5 copy-start.25
  839.0 11.2 %copy-start.5 = (f32[2,48,64,128]{3,2,1,0:T(8,128)S(1)}, f32[2,48,64,128]{3,2,1,0:T(8,128)}, u32[]{:S(2)}) copy-start(f32[2,48,64,128]{3,2,1,0:T(8,128)} %get-tuple-element.2715) | copy-start | bytes 9437188 | tf_op jit(solution)/shard_map/transpose(jvp())/while
  862.0 9.6 copy-start.24
  862.0 9.9 %copy-start.1 = (f32[2,128,48,64]{1,3,2,0:T(8,128)S(1)}, f32[2,128,48,64]{1,3,2,0:T(8,128)}, u32[]{:S(2)}) copy-start(f32[2,128,48,64]{1,3,2,0:T(8,128)} %get-tuple-element.2706) | copy-start | bytes 9437188 | tf_op jit(solution)/shard_map/transpose(jvp())/while
  862.0 9.9 %copy-start.4 = (f32[128,48,64]{0,2,1:T(8,128)S(1)}, f32[128,48,64]{0,2,1:T(8,128)}, u32[]{:S(2)}) copy-start(f32[128,48,64]{0,2,1:T(8,128)} %get-tuple-element.2407) | copy-start | bytes 4718596 | tf_op jit(solution)/shard_map/transpose(jvp())/while
  871.9 5.4 copy-start.25
  887.9 5.9 copy-start.15
  887.9 6.6 copy-start.32
  887.9 6.6 copy-start.36
  (18 other events, 37.9 us)
Sparse Core Ops, SparseCore 0:
  33.9 160.0 all-gather.5
  432.1 120.7 reduce-scatter.1
  556.0 156.6 all-gather.7
  715.0 42.3 all-reduce.4
where the time goes:
time: 984 us; the launch traced here: 973 us
  waiting for transfers between devices  325 us (33%)
  local copies, waits for them, and re-layouts  220 us (22%)
  other arithmetic  192 us (20%)
  matrix products  128 us (13%)
  blocking collectives  88.2 us (9%)
  between operations  15.1 us (2%)
    all_gather x2, waiting for transfers between devices, prefix(): everything = jax.tree.map(lambda part: lax.all_gather(part, axis), shard)  275 us
    select_n x64, other arithmetic, hop(): return jax.tree.map(lambda a, b: jnp.where(reached, a, b), new, before)  113 us
    dynamic_update_slice x44, local copies, waits for them, and re-layouts, ssd_blocks(): lax.scan(block_step, state_in, (to_blocks(x_heads), to_blocks(b_float), t...  89 us
    psum x1, blocking collectives, per_device(): lax.psum((bias_grad, rate_grad, skip_grad, gain_grad), ('dp', 'seq'))  65.2 us
    reduce_scatter x1, waiting for transfers between devices, per_device(): lax.psum_scatter(lax.dot_general(normed, grad_rows, (((0,), (0,)), ((), (...  49.9 us
    dot_general x6, matrix products, block_step(): y_blk = jnp.einsum('ijh,jhp->ihp', mixing, x_blk, precision=highest)  48.3 us
    all_gather x1, blocking collectives, prefix(): everything = jax.tree.map(lambda part: lax.all_gather(part, axis), shard)  22.9 us
    mul x2, other arithmetic, block_step(): mixing = gram_mat[:, :, None] * decay_mat * step_blk[None, :, :]  22.6 us
  transfers between devices with their start and end apart: 4, of which 3 were waited for; matrix products, arithmetic and copies ran while one was open for 28% of the time, Pallas kernels for 0%

commit v1 on v0

v1 whole, which is shorter than its diff:
```python
import functools

import jax
import jax.numpy as jnp
from jax import lax
from jax.experimental import pallas as pl
from jax.experimental.pallas import tpu as pltpu
from jax.sharding import PartitionSpec as P

MESH = pl.DeviceIdType.MESH
HIGHEST = lax.Precision.HIGHEST
VMEM_LIMIT = 60 * 1024 * 1024


def bdot(a, b, ca, cb):
    return lax.dot_general(
        a, b, (((ca,), (cb,)), ((), ())), preferred_element_type=jnp.float32
    )


def split(v):
    hi = v.astype(jnp.bfloat16)
    return hi, (v - hi.astype(jnp.float32)).astype(jnp.bfloat16)


def dot2(a, b, ca, cb):
    if isinstance(a, tuple) and isinstance(b, tuple):
        return bdot(a[0], b[0], ca, cb) + (bdot(a[0], b[1], ca, cb) + bdot(a[1], b[0], ca, cb))
    if isinstance(a, tuple):
        return bdot(a[0], b, ca, cb) + bdot(a[1], b, ca, cb)
    if isinstance(b, tuple):
        return bdot(a, b[0], ca, cb) + bdot(a, b[1], ca, cb)
    return bdot(a, b, ca, cb)


def exact(a, b):
    return jnp.dot(a, b, precision=HIGHEST, preferred_element_type=jnp.float32)


def scan_kernel(n, reverse, s_ref, thr_ref, spread_ref, out_ref, recv, stage, thr_buf, thr_wide,
                s_send, s_recv, t_send, t_recv, o_send, o_recv):
    me = lax.axis_index("seq")
    ns, width = s_ref.shape
    rows = ns // (n // 2)
    half = width // 2

    def place(k):
        r0 = pl.multiple_of(lax.div(k, 2) * rows, 8)
        l0 = pl.multiple_of(lax.rem(k, 2) * half, 128)
        return pl.ds(r0, rows), pl.ds(l0, half)

    barrier = pltpu.get_barrier_semaphore()

    def greet(i, _):
        peer = lax.rem(me + 1 + i, n)
        pl.semaphore_signal(barrier, inc=1, device_id={"seq": peer}, device_id_type=MESH)
        return 0

    lax.fori_loop(0, n - 1, greet, 0)
    pl.semaphore_wait(barrier, n - 1)

    def thr_copy(k, slot):
        return pltpu.make_async_remote_copy(
            src_ref=thr_ref, dst_ref=thr_buf.at[slot], send_sem=t_send.at[k],
            recv_sem=t_recv.at[slot], device_id={"seq": k}, device_id_type=MESH)

    def s_copy(k, slot):
        r, l = place(k)
        return pltpu.make_async_remote_copy(
            src_ref=s_ref.at[r, l], dst_ref=recv.at[slot], send_sem=s_send.at[k],
            recv_sem=s_recv.at[slot], device_id={"seq": k}, device_id_type=MESH)

    def o_copy(k, owner):
        r, l = place(owner)
        return pltpu.make_async_remote_copy(
            src_ref=stage.at[k], dst_ref=out_ref.at[r, l], send_sem=o_send.at[k],
            recv_sem=o_recv.at[owner], device_id={"seq": k}, device_id_type=MESH)

    def send(i, _):
        k = lax.rem(me + 1 + i, n)
        thr_copy(k, me).start()
        s_copy(k, me).start()
        return 0

    lax.fori_loop(0, n - 1, send, 0)
    my_r, my_l = place(me)
    recv[me] = s_ref[my_r, my_l]
    thr_buf[me] = thr_ref[...]

    def arrive(i, _):
        thr_copy(me, lax.rem(me + 1 + i, n)).wait_recv()
        return 0

    lax.fori_loop(0, n - 1, arrive, 0)
    thr_wide[...] = jnp.dot(thr_buf[:, 0, :], spread_ref[:, my_l], precision=HIGHEST,
                            preferred_element_type=jnp.float32)

    def hop(i, state):
        j = n - 1 - i if reverse else i

        @pl.when(j != me)
        def _():
            s_copy(me, j).wait_recv()

        stage[j] = state

        @pl.when(j != me)
        def _():
            o_copy(j, me).start()

        return thr_wide[pl.ds(j, 1), :] * state + recv[j]

    lax.fori_loop(0, n, hop, jnp.zeros((rows, half), jnp.float32))
    out_ref[my_r, my_l] = stage[me]

    def finish(i, _):
        k = lax.rem(me + 1 + i, n)
        o_copy(me, k).wait_recv()
        thr_copy(k, me).wait_send()
        s_copy(k, me).wait_send()
        o_copy(k, me).wait_send()
        return 0

    lax.fori_loop(0, n - 1, finish, 0)


def state_scan(n, state, thr, spread, reverse):
    ns, width = state.shape
    rows, half = ns // (n // 2), width // 2
    vmem = pl.BlockSpec(memory_space=pltpu.VMEM)
    return pl.pallas_call(
        functools.partial(scan_kernel, n, reverse),
        out_shape=jax.ShapeDtypeStruct((ns, width), jnp.float32),
        in_specs=[vmem] * 3,
        out_specs=vmem,
        scratch_shapes=[
            pltpu.VMEM((n, rows, half), jnp.float32),
            pltpu.VMEM((n, rows, half), jnp.float32),
            pltpu.VMEM((n, 8, 128), jnp.float32),
            pltpu.VMEM((n, half), jnp.float32),
        ] + [pltpu.SemaphoreType.DMA((n,))] * 6,
        compiler_params=pltpu.CompilerParams(
            collective_id=2 if reverse else 1, has_side_effects=True,
            vmem_limit_bytes=VMEM_LIMIT),
        name="scan_back" if reverse else "scan_ahead",
    )(state, thr, spread)


ORDERS = ((2, 1, 0), (1, 0, 2), (0, 2, 1))


def reduce_kernel(nt_ref, og_ref, small_ref, out_ref, small_out, part, nt_got, og_got,
                  agg1, full1, agg2, full2, agg3, full3, slots_c, slots_a, total,
                  c_send, c_recv, r_send, r_recv, x_send, x_recv, m_send, m_recv):
    xi = lax.axis_index("dp")
    s = lax.axis_index("seq")
    zi, yi, core = lax.div(s, 8), lax.rem(lax.div(s, 2), 4), lax.rem(s, 2)
    here = (zi, yi, xi)
    cols = part.shape[-1]
    third = cols // 3
    half = third // 2

    def at(axis, index):
        if axis == 2:
            return {"dp": index}
        z, y = (index, yi) if axis == 0 else (zi, index)
        return {"seq": (z * 4 + y) * 2 + core}

    sibling = {"seq": s + 1 - 2 * core}
    barrier = pltpu.get_barrier_semaphore()
    pl.semaphore_signal(barrier, inc=1, device_id=sibling, device_id_type=MESH)
    for axis in range(3):
        for d in range(1, 4):
            pl.semaphore_signal(barrier, inc=1, device_id=at(axis, lax.rem(here[axis] + d, 4)),
                                device_id_type=MESH)
    pl.semaphore_wait(barrier, 10)

    def remote(src, dst, ss, rs, to):
        return pltpu.make_async_remote_copy(src_ref=src, dst_ref=dst, send_sem=ss, recv_sem=rs,
                                            device_id=to, device_id_type=MESH)

    started = []

    copies = [
        remote(og_ref, og_got, c_send.at[0], c_recv.at[0], sibling),
        remote(nt_ref.at[:, 1 - core], nt_got, c_send.at[1], c_recv.at[1], sibling),
        remote(small_ref, slots_c.at[core], c_send.at[2], c_recv.at[2], sibling),
    ]
    for c in copies:
        c.start()
    slots_c[core] = small_ref[...]
    og = og_ref[...].astype(jnp.bfloat16)

    def own(b, _):
        z, y = lax.div(b, 4), lax.rem(b, 4)
        lhs = nt_ref[b, core].astype(jnp.bfloat16)
        part[z, y] = bdot(lhs, og, 1, 0).reshape(part.shape[2:])
        return 0

    lax.fori_loop(0, 16, own, 0)
    for c in copies:
        c.wait_recv()
    og2 = og_got[...].astype(jnp.bfloat16)

    def theirs(b, _):
        z, y = lax.div(b, 4), lax.rem(b, 4)
        lhs = nt_got[b].astype(jnp.bfloat16)
        part[z, y] += bdot(lhs, og2, 1, 0).reshape(part.shape[2:])
        return 0

    lax.fori_loop(0, 16, theirs, 0)
    total[...] = slots_c[0] + slots_c[1]

    bufs = ((agg1, full1), (agg2, full2), (agg3, full3))
    small_axes = (2, 1, 0)
    for step in range(3):
        agg, full = bufs[step]

        def small_copy(d):
            axis = small_axes[step]
            return remote(total, slots_a.at[step, here[axis]], m_send.at[step, d - 1],
                          m_recv.at[step, d - 1], at(axis, lax.rem(here[axis] + d, 4)))

        smalls = [small_copy(d) for d in (1, 2, 3)]
        for c in smalls:
            c.start()
        slots_a[step, here[small_axes[step]]] = total[...]

        def region(p, t, h=None):
            order = ORDERS[p]
            index = [slice(None)] * 3
            for done in order[:step]:
                index[done] = here[done]
            index[order[step]] = t
            lo = p * third + (0 if h in (None, 0) else half)
            return (*index, slice(None), pl.ds(lo, third if h is None else half))

        def sem(p, k):
            return r_send.at[step, p, k], r_recv.at[step, p, k]

        first, second, last = [], [], []
        for p in range(3):
            axis = ORDERS[p][step]
            me = here[axis]
            up, down, far = lax.rem(me + 1, 4), lax.rem(me + 3, 4), lax.rem(me + 2, 4)
            a = [
                remote(part.at[region(p, far, 0)], agg.at[p, 0], *sem(p, 0), at(axis, up)),
                remote(part.at[region(p, far, 1)], agg.at[p, 1], *sem(p, 1), at(axis, down)),
            ]
            b = [
                remote(part.at[region(p, up, 1)], full.at[p, 0, ..., pl.ds(half, half)], *sem(p, 2), at(axis, up)),
                remote(part.at[region(p, down, 0)], full.at[p, 1, ..., pl.ds(0, half)], *sem(p, 3), at(axis, down)),
            ]
            c = [
                remote(part.at[region(p, up, 0)], full.at[p, 0, ..., pl.ds(0, half)], *sem(p, 4), at(axis, up)),
                remote(part.at[region(p, down, 1)], full.at[p, 1, ..., pl.ds(half, half)], *sem(p, 5), at(axis, down)),
            ]
            first.append(a)
            second.append(b)
            last.append(c)
        for p in range(3):
            for c in first[p]:
                c.start()
        for p in range(3):
            for c in second[p]:
                c.start()
        for p in range(3):
            axis = ORDERS[p][step]
            me = here[axis]
            up, down = lax.rem(me + 1, 4), lax.rem(me + 3, 4)
            first[p][0].wait_recv()
            part[region(p, up, 0)] += agg[p, 0]
            last[p][0].start()
            first[p][1].wait_recv()
            part[region(p, down, 1)] += agg[p, 1]
            last[p][1].start()
        for p in range(3):
            axis = ORDERS[p][step]
            for c in second[p] + last[p]:
                c.wait_recv()
            part[region(p, here[axis])] += full[p, 0] + full[p, 1]
        for c in smalls:
            c.wait_recv()
            c.wait_send()
        for p in range(3):
            started += first[p] + second[p] + last[p]
        total_now = (slots_a[step, 0] + slots_a[step, 1]) + (slots_a[step, 2] + slots_a[step, 3])
        if step < 2:
            total[...] = total_now
        else:
            small_out[...] = total_now

    mine = part[zi, yi, xi]
    out_ref[xi] = mine
    spread = []
    for d in (1, 2, 3):
        c = remote(out_ref.at[xi], out_ref.at[xi], x_send.at[d - 1], x_recv.at[d - 1],
                   {"dp": lax.rem(xi + d, 4)})
        c.start()
        spread.append(c)
    for d in (1, 2, 3):
        came = lax.rem(xi + 4 - d, 4)
        remote(out_ref.at[came], out_ref.at[came], x_send.at[d - 1], x_recv.at[d - 1],
               {"dp": came}).wait_recv()
    for c in spread + copies + started:
        c.wait_send()


def reduce_weight(nt, og, small):
    rows = nt.shape[2]
    cols = og.shape[1]
    quarter = rows // 4
    third, half = cols // 3, cols // 6
    vmem = pl.BlockSpec(memory_space=pltpu.VMEM)
    f32 = jnp.float32
    out, sums = pl.pallas_call(
        reduce_kernel,
        out_shape=(jax.ShapeDtypeStruct((4, quarter, cols), f32), jax.ShapeDtypeStruct(small.shape, f32)),
        in_specs=[vmem] * 3,
        out_specs=(vmem, vmem),
        scratch_shapes=[
            pltpu.VMEM((4, 4, 4, quarter, cols), f32),
            pltpu.VMEM((16, rows, nt.shape[3]), f32),
            pltpu.VMEM(og.shape, f32),
            pltpu.VMEM((3, 2, 4, 4, quarter, half), f32),
            pltpu.VMEM((3, 2, 4, 4, quarter, third), f32),
            pltpu.VMEM((3, 2, 4, quarter, half), f32),
            pltpu.VMEM((3, 2, 4, quarter, third), f32),
            pltpu.VMEM((3, 2, quarter, half), f32),
            pltpu.VMEM((3, 2, quarter, third), f32),
            pltpu.VMEM((2, *small.shape), f32),
            pltpu.VMEM((3, 4, *small.shape), f32),
            pltpu.VMEM(small.shape, f32),
            pltpu.SemaphoreType.DMA((3,)),
            pltpu.SemaphoreType.DMA((3,)),
            pltpu.SemaphoreType.DMA((3, 3, 6)),
            pltpu.SemaphoreType.DMA((3, 3, 6)),
            pltpu.SemaphoreType.DMA((3,)),
            pltpu.SemaphoreType.DMA((3,)),
            pltpu.SemaphoreType.DMA((3, 3)),
            pltpu.SemaphoreType.DMA((3, 3)),
        ],
        compiler_params=pltpu.CompilerParams(
            collective_id=3, has_side_effects=True, vmem_limit_bytes=VMEM_LIMIT),
        name="reduce_weight",
    )(nt, og, small)
    return out.reshape(rows, cols), sums


def per_device(scan, reduce_all, ssm_input, gate_input, input_map, output_map, step_logit, step_bias,
               decay_rate, skip_gain, norm_gain, out_weight, resets, out_grad):
    f32, bf16 = jnp.float32, jnp.bfloat16
    x, z, bmap, cmap, og = ssm_input[0], gate_input[0], input_map[0], output_map[0], out_grad[0]
    rows, width = x.shape
    heads = step_bias.shape[0]
    per_head = width // heads

    start = lax.axis_index("seq") * rows
    ri = lax.broadcasted_iota(jnp.int32, (rows, rows), 0)
    ci = lax.broadcasted_iota(jnp.int32, (rows, rows), 1)
    below = ri >= ci
    tri = below.astype(f32)
    at_col = start + lax.broadcasted_iota(jnp.int32, (rows, 1), 0)
    at_row = start + lax.broadcasted_iota(jnp.int32, (1, rows), 1)
    flag_col = jnp.zeros((rows, 1), jnp.bool_)
    flag_row = jnp.zeros((1, rows), jnp.bool_)
    for k in range(resets.shape[1]):
        flag_col |= at_col == resets[0, k]
        flag_row |= at_row == resets[0, k]
    count_col = jnp.sum(jnp.where(below & flag_row, 1.0, 0.0), axis=1, keepdims=True)
    count_row = jnp.sum(jnp.where((ri <= ci) & flag_col, 1.0, 0.0), axis=0, keepdims=True)
    count_all = jnp.sum(flag_row.astype(f32))
    mask = below & (count_col == count_row)
    opened = count_col == 0
    keep = count_col == count_all

    spread = (
        lax.broadcasted_iota(jnp.int32, (heads, width), 0)
        == lax.broadcasted_iota(jnp.int32, (heads, width), 1) // per_head
    ).astype(f32)
    gather = spread.T

    raw = step_logit[0].astype(f32) + step_bias
    step = jax.nn.softplus(raw)
    cum = exact(tri, -decay_rate * step)
    last = cum[rows - 1 :]
    mid = cum[rows // 2 : rows // 2 + 1]
    through = jnp.where(count_all == 0, jnp.exp(last), 0.0)
    e_head = jnp.exp(cum - mid)
    f_head = step * jnp.exp(mid - cum)
    wide = exact(
        jnp.concatenate([e_head, f_head, jnp.exp(last - mid), jnp.exp(mid), skip_gain[None], through], axis=0),
        spread,
    )
    e, f = wide[:rows], wide[rows : 2 * rows]
    tail, lead, skip, through_wide = (wide[2 * rows + k : 2 * rows + k + 1] for k in range(4))

    xf = x.astype(f32)
    fx_f = f * xf
    fx2 = split(fx_f)
    fx = fx2[0]
    gm2 = split(jnp.where(mask, bdot(cmap, bmap, 1, 1), 0.0))
    gm = gm2[0]
    b_keep = jnp.where(keep, bmap, jnp.zeros_like(bmap))
    c_open = jnp.where(opened, cmap, jnp.zeros_like(cmap))
    s_own = dot2(b_keep, fx2, 0, 0)
    thr = jnp.zeros((8, 128), f32).at[:, :heads].set(jnp.broadcast_to(through, (8, heads)))
    spread_pad = jnp.zeros((128, width), f32).at[:heads].set(spread)
    incoming = scan(tail * s_own, thr, spread_pad, False)
    s_in2 = split(lead * incoming)
    s_in = s_in2[0]

    u = dot2(gm2, fx2, 1, 0) + dot2(c_open, s_in2, 1, 0)
    y = e * u + skip * xf
    zf = z.astype(f32)
    sig = jax.nn.sigmoid(zf)
    silu = zf * sig
    g = y * silu
    r = lax.rsqrt(jnp.mean(g * g, axis=1, keepdims=True) + 1e-05)
    ghat = g * r
    normed = (ghat * norm_gain).astype(bf16)
    mixed = bdot(normed, out_weight, 1, 0).astype(bf16)
    dn = bdot(og, out_weight, 1, 1)
    gain_grad = jnp.sum(dn * ghat, axis=0)
    q = dn * norm_gain
    dg = r * (q - ghat * jnp.mean(q * ghat, axis=1, keepdims=True))
    dy = dg * silu
    dz = (dg * y * (sig * (1.0 + zf * (1.0 - sig)))).astype(bf16)
    du_f = e * dy
    du2 = split(du_f)
    du = du2[0]
    later = scan(lead * dot2(c_open, du2, 0, 0), thr, spread_pad, True)
    ds_f = tail * later
    ds2 = split(ds_f)
    ds = ds2[0]

    dfx = dot2(gm2, du2, 0, 0) + dot2(b_keep, ds2, 1, 0)
    dx = (f * dfx + skip * dy).astype(bf16)
    dgm2 = split(jnp.where(mask, bdot(du, fx, 1, 1), 0.0))
    dc = dot2(dgm2, bmap, 1, 0) + jnp.where(opened, bdot(du, s_in, 1, 1), 0.0)
    db = dot2(dgm2, cmap, 0, 0) + jnp.where(keep, bdot(fx, ds, 1, 1), 0.0)
    skip_row = jnp.sum(dy * xf, axis=0, keepdims=True)
    end_row = jnp.sum(ds_f * s_own + through_wide * later * incoming, axis=0, keepdims=True)
    a_wide = fx_f * dfx
    per = exact(jnp.concatenate([a_wide, du_f * u - a_wide, skip_row, end_row], axis=0), gather)
    a, ba = per[:rows], per[rows : 2 * rows]
    skip_grad, end = per[2 * rows], per[2 * rows + 1 :]
    d_decay = exact((ri <= ci).astype(f32), ba) + end
    dlogit = (a / step - decay_rate * d_decay) * jax.nn.sigmoid(raw)
    bias_grad = jnp.sum(dlogit, axis=0)
    rate_grad = jnp.sum(-step * d_decay, axis=0)

    small = jnp.concatenate([gain_grad, bias_grad, rate_grad, skip_grad])
    size = small.shape[0]
    lines = -(-size // 1024) * 8
    small = jnp.pad(small, (0, lines * 128 - size)).reshape(lines, 128)
    weight_grad, sums = reduce_all(normed, og, small)
    sums = sums.reshape(-1)
    gain_sum = sums[:width]
    bias_sum, rate_sum, skip_sum = (sums[width + k * heads : width + (k + 1) * heads] for k in range(3))
    return (
        mixed[None],
        dx[None],
        dz[None],
        dc_cast(db)[None],
        dc_cast(dc)[None],
        dc_cast(dlogit)[None],
        bias_sum,
        rate_sum,
        skip_sum,
        gain_sum,
        weight_grad,
    )


def dc_cast(values):
    return values.astype(jnp.bfloat16)


def solution(mesh):
    n = mesh.shape["seq"]

    def scan(state, thr, spread, reverse):
        return state_scan(n, state, thr, spread, reverse)

    def reduce_all(normed, og, small):
        rows, width = normed.shape
        nt = normed.T.astype(jnp.float32).reshape(16, 2, width // 32, rows)
        return reduce_weight(nt, og.astype(jnp.float32), small)

    by_rows = P("dp", "seq", None)
    return jax.shard_map(
        functools.partial(per_device, scan, reduce_all),
        mesh=mesh,
        in_specs=(by_rows,) * 5 + (P(),) * 5 + (P("dp", None), by_rows),
        out_specs=(by_rows,) * 6 + (P(),) * 4 + (P("seq", None),),
        check_vma=False,
    )
```

time: 984 us -> 298 us (0.30); the launches traced: 973 us -> 297 us
  waiting for transfers between devices: 325 us -> 0 us
  local copies, waits for them, and re-layouts: 220 us -> 18.7 us
  Pallas kernels: 0 us -> 195 us
  other arithmetic: 192 us -> 21 us
  blocking collectives: 88.2 us -> 0 us
  matrix products: 128 us -> 60.7 us
  between operations: 15.1 us -> 1.76 us
    all_gather x2 -> x0, waiting for transfers between devices: 275 us -> none  [prefix(): everything = jax.tree.map(lambda part: lax.all_gather(part, axis), shard)]
    pallas_call x0 -> x3, Pallas kernels: none -> 195 us  [the longest x2 125 us: state_scan(): pl.pallas_call(functools.partial(scan_kernel, n, reverse), out_shape=jax....]
    select_n x72 -> x0, other arithmetic: 116 us -> none  [the longest x64 113 us: hop(): return jax.tree.map(lambda a, b: jnp.where(reached, a, b), new, before)]
    dynamic_update_slice x44 -> x0, local copies, waits for them, and re-layouts: 89 us -> none  [ssd_blocks(): lax.scan(block_step, state_in, (to_blocks(x_heads), to_blocks(b_float), t...]
    dot_general x29 -> x28, matrix products: 128 us -> 60.7 us  [the longest x24 49.9 us: bdot(): lax.dot_general(a, b, (((ca,), (cb,)), ((), ())), preferred_element_type=...]
    psum x1 -> x0, blocking collectives: 65.2 us -> none  [per_device(): lax.psum((bias_grad, rate_grad, skip_grad, gain_grad), ('dp', 'seq'))]
    reduce_scatter x1 -> x0, waiting for transfers between devices: 49.9 us -> none  [per_device(): lax.psum_scatter(lax.dot_general(normed, grad_rows, (((0,), (0,)), ((), (...]
    mul x83 -> x0, local copies, waits for them, and re-layouts: 45.4 us -> none  [the longest x64 22.6 us: combine(): later[0][:, None, None] * earlier[1] + later[1]]
  transfers between devices with their start and end apart: 4 -> 0, of which waited for: 3 -> 0; matrix products, arithmetic and copies ran while one was open for 28% -> 0% of each run, Pallas kernels for 0% -> 0%
where the time goes in v1:
time: 298 us; the launch traced here: 297 us
  Pallas kernels  195 us (65%)
  matrix products  60.7 us (20%)
  other arithmetic  21 us (7%)
  local copies, waits for them, and re-layouts  18.7 us (6%)
    pallas_call x2, Pallas kernels, state_scan(): pl.pallas_call(functools.partial(scan_kernel, n, reverse), out_shape=jax....  125 us
    pallas_call x1, Pallas kernels, reduce_weight(): pl.pallas_call(reduce_kernel, out_shape=(jax.ShapeDtypeStruct((4, quarter...  70 us
    dot_general x24, matrix products, bdot(): lax.dot_general(a, b, (((ca,), (cb,)), ((), ())), preferred_element_type=...  49.9 us
    dot_general x4, matrix products, exact(): return jnp.dot(a, b, precision=HIGHEST, preferred_element_type=jnp.float32)  10.9 us
    unnamed x49, local copies, waits for them, and re-layouts  9.9 us

profile of v1, /device:TPU:0, one launch (start us, length us, event | category | flops | bytes accessed | tf_op | source)
XLA Modules:
  0.0 297.4 jit_solution(1505205697397863642)
XLA Ops:
  0.7 0.6 compare_reduce_fusion
  1.3 0.7 neg.16
  2.0 1.4 fusion.103
  3.3 3.2 %fusion.71 = f32[]{:T(128)} fusion(s32[]{:T(128)} %bitcast.5, s32[]{:T(128)} %bitcast.4, s32[]{:T(128)} %bitcast.3, s32[]{:T(128)} %bitcast.2, s32[]{:T(128)S(6)} %mul.182), kind=kLoop, calls=%fused_computation.143 | loop fusion | flops 2559 | bytes 24 | tf_op jit(solution)/shard_map/reduce_sum | solution.py:372
  7.2 2.6 compare_or_fusion
  10.0 0.7 broadcast_compare_fusion.1
  10.6 0.7 copy.27
  11.4 1.0 fusion.44
  12.4 0.8 select_reduce_fusion.2
  13.3 0.6 scatter.15.thr_ref
  13.9 0.9 exponential_multiply_fusion
  14.9 1.1 convolution_select_fusion
  16.0 1.3 pad_convert_fusion.spread_ref
  17.3 1.4 bitcast_convert_fusion.og_ref
  18.7 2.7 fusion.94
  21.5 0.6 subtract_convert_fusion.1
  22.1 2.0 copy-done
  24.6 2.2 broadcast_multiply_fusion
  26.8 60.2 %scan_ahead.1 = f32[128,3072]{1,0:T(8,128)} custom-call(f32[128,3072]{1,0:T(8,128)} %get-tuple-element.79.s_ref, f32[8,128]{1,0:T(8,128)} %scatter.15.thr_ref, f32[128,3072]{1,0:T(8,128)} %pad_convert_fusion.spread_ref), custom_call_target="tpu_custom_call" | custom-call | tf_op jit(solution)/shard_map/scan_ahead/pallas_call | solution.py:131
  87.6 0.8 copy-done.7
  88.4 0.6 fusion.40
  89.6 0.6 fusion.11
  90.3 0.9 slice-done
  91.2 0.9 slice-done.1
  92.9 3.6 %multiply_reduce_fusion.2 = (f32[256]{0:T(256)S(1)}, f32[256,3072]{1,0:T(8,128)S(1)}, f32[256,3072]{1,0:T(8,128)}) fusion(bf16[1,256,3072]{2,1,0:T(8,128)(2,1)S(1)} %copy-done.13, bf16[1,256,3072]{2,1,0:T(8,128)(2,1)S(1)} %copy-done.9, f32[3072]{0:T(1024)S(1)} %bitcast.136, f32[516,3072]{1,0:T(8,128)S(1)} %bitcast.124, f32[256,3072]{1,0:T(8,128)S(1)} %fusion.11, ...), kind=kOutput, calls=%fused_computation.42 | convolution fusion | flops 214335232 | bytes 20538624 | tf_op jit(solution)/shard_map/dot_general | solution.py:16
  96.5 8.4 %fusion.22 = bf16[1,256,1536]{2,1,0:T(8,128)(2,1)} fusion(bf16[3072,1536]{1,0:T(8,128)(2,1)} %param.25, f32[256,3072]{1,0:T(8,128)S(1)} %get-tuple-element.52, f32[3072]{0:T(1024)S(1)} %copy-done.18, f32[256]{0:T(256)S(1)} %add_rsqrt_fusion), kind=kOutput, calls=%fused_computation.46 | convolution fusion | flops 2418671616 | bytes 13382656 | tf_op jit(solution)/shard_map/dot_general | solution.py:16
  104.8 5.5 %multiply_reduce_fusion = (f32[3072]{0:T(1024)S(1)}, f32[256]{0:T(256)S(1)}, f32[256,3072]{1,0:T(8,128)S(1)}) fusion(f32[256,3072]{1,0:T(8,128)S(1)} %get-tuple-element.52, f32[256]{0:T(256)S(1)} %add_rsqrt_fusion, f32[3072]{0:T(1024)S(1)} %copy-done.18, bf16[3072,1536]{1,0:T(8,128)(2,1)} %param.25, bf16[1,256,1536]{2,1,0:T(8,128)(2,1)S(1)} %copy-done.17), kind=kOutput, calls=%fused_computation.35 | convolution fusion | flops 2420634368 | bytes 16541696 | tf_op jit(solution)/shard_map/dot_general | solution.py:16
  110.4 4.6 %fusion.14 = (f32[3072]{0:T(1024)S(1)}, f32[256,3072]{1,0:T(8,128)S(1)}) fusion(bf16[1,256,3072]{2,1,0:T(8,128)(2,1)S(1)} %copy-done.9, bf16[1,256,3072]{2,1,0:T(8,128)(2,1)} %param.17, f32[256]{0:T(256)S(1)} %broadcast_multiply_fusion.1, f32[256,3072]{1,0:T(8,128)S(1)} %get-tuple-element.52, f32[256,3072]{1,0:T(8,128)S(1)} %get-tuple-element.82, ...), kind=kLoop, calls=%fused_computation.26 | loop fusion | flops 11006976 | bytes 12609536 | tf_op jit(solution)/shard_map/reduce_sum | solution.py:442
  115.5 1.2 copy-done.5
  116.7 0.9 copy-done.2
  117.6 0.7 convolution_select_fusion.1
  118.6 1.3 fusion.31
  120.9 1.7 fusion.12.s_ref
  122.5 65.1 %scan_back.1 = f32[128,3072]{1,0:T(8,128)} custom-call(f32[128,3072]{1,0:T(8,128)} %fusion.12.s_ref, f32[8,128]{1,0:T(8,128)} %scatter.15.thr_ref, f32[128,3072]{1,0:T(8,128)} %pad_convert_fusion.spread_ref), custom_call_target="tpu_custom_call" | custom-call | tf_op jit(solution)/shard_map/scan_back/pallas_call | solution.py:131
  187.7 2.9 add_reduce_fusion
  191.0 1.2 fusion.32
  192.2 2.3 fusion.39
  195.1 0.6 fusion.78
  195.7 2.4 fusion.9
  198.0 14.3 %multiply_subtract_fusion = (f32[256,3072]{1,0:T(8,128)}, f32[256,3072]{1,0:T(8,128)}, bf16[1,256,3072]{2,1,0:T(8,128)(2,1)}, bf16[1,256,3072]{2,1,0:T(8,128)(2,1)}, f32[3072,256]{0,1:T(8,128)}) fusion(f32[256,3072]{1,0:T(8,128)S(1)} %slice_multiply_fusion, f32[256,3072]{1,0:T(8,128)} %get-tuple-element.81, bf16[1,256,3072]{2,1,0:T(8,128)(2,1)} %param.16, ...), kind=kOutput, calls=%fused_computation.36 | convolution fusion | flops 229277696 | bytes 45717760 | tf_op jit(solution)/shard_map/dot_general | solution.py:16
  212.4 6.1 %fusion = f32[514,48]{0,1:T(8,128)S(1)} fusion(f32[1,3072]{1,0:T(1,128)S(1)} %bitcast.140, f32[1,3072]{1,0:T(1,128)S(1)} %bitcast.139, f32[256,3072]{1,0:T(8,128)} %get-tuple-element.47, f32[256,3072]{1,0:T(8,128)} %get-tuple-element.48, s32[3072]{0:T(1024)S(1)} %get-tuple-element.83, s32[3072]{0:T(1024)S(1)} %get-tuple-element.84, pred[3072]{0:T(1024)(128)(4,1)S(1)} %fusion.70), kind=kOutput, calls=%fused_computation | convolution fusion | flops 914540544 | bytes 6442368 | tf_op jit(solution)/shard_map/dot_general | solution.py:37
  218.7 1.0 fusion.95
  219.8 0.6 pad_bitcast_fusion.small_ref
  220.4 2.4 copy.28
  222.8 70.0 %reduce_weight.1 = (f32[4,24,1536]{2,1,0:T(8,128)}, f32[32,128]{1,0:T(8,128)}) custom-call(f32[16,2,96,256]{3,2,1,0:T(8,128)} %bitcast.125, f32[256,1536]{1,0:T(8,128)} %bitcast_convert_fusion.og_ref, f32[32,128]{1,0:T(8,128)} %pad_bitcast_fusion.small_ref), custom_call_target="tpu_custom_call" | custom-call | tf_op jit(solution)/shard_map/reduce_weight/pallas_call | solution.py:316
  292.8 1.4 fusion.102
  294.2 1.3 slice_bitcast_fusion
  295.5 1.9 copy.30
  (64 shorter events, 5.9 us)
Async XLA Ops:
  0.6 16.6 %copy-start.16 = (bf16[1,256,1536]{2,1,0:T(8,128)(2,1)S(1)}, bf16[1,256,1536]{2,1,0:T(8,128)(2,1)}, u32[]{:S(2)}) copy-start(bf16[1,256,1536]{2,1,0:T(8,128)(2,1)} %param.27) | copy-start | bytes 2359300
  18.7 2.8 copy-start.8
  21.4 2.7 copy-start
  21.5 2.6 copy-start.14
  24.1 65.5 %copy-start.1 = (bf16[256,3072]{1,0:T(8,128)(2,1)}, bf16[256,3072]{1,0:T(8,128)(2,1)S(1)}, u32[]{:S(2)}) copy-start(bf16[256,3072]{1,0:T(8,128)(2,1)S(1)} %get-tuple-element.56) | copy-start | bytes 4718596
  87.0 1.4 copy-start.7
  87.0 1.4 copy-start.15
  89.0 2.2 slice-start
  89.6 2.4 slice-start.1
  89.6 2.9 copy-start.9
  89.6 3.3 %copy-start.13 = (bf16[1,256,3072]{2,1,0:T(8,128)(2,1)S(1)}, bf16[1,256,3072]{2,1,0:T(8,128)(2,1)}, u32[]{:S(2)}) copy-start(bf16[1,256,3072]{2,1,0:T(8,128)(2,1)} %param.17) | copy-start | bytes 4718596
  92.9 3.6 %copy-start.18 = (f32[3072]{0:T(1024)S(1)}, f32[3072]{0:T(1024)}, u32[]{:S(2)}) copy-start(f32[3072]{0:T(1024)} %param.24) | copy-start | bytes 36868
  96.5 13.9 %copy-start.11 = (f32[256,3072]{1,0:T(8,128)}, f32[256,3072]{1,0:T(8,128)S(1)}, u32[]{:S(2)}) copy-start(f32[256,3072]{1,0:T(8,128)S(1)} %get-tuple-element.52) | copy-start | bytes 9437188
  96.5 8.4 %copy-start.17 = (bf16[1,256,1536]{2,1,0:T(8,128)(2,1)S(1)}, bf16[1,256,1536]{2,1,0:T(8,128)(2,1)}, u32[]{:S(2)}) copy-start(bf16[1,256,1536]{2,1,0:T(8,128)(2,1)} %param.27) | copy-start | bytes 2359300
  110.4 4.7 %copy-start.12 = (f32[256,3072]{1,0:T(8,128)}, f32[256,3072]{1,0:T(8,128)S(1)}, u32[]{:S(2)}) copy-start(f32[256,3072]{1,0:T(8,128)S(1)} %get-tuple-element.82) | copy-start | bytes 9437188
  115.1 1.7 copy-start.5
  115.1 2.5 copy-start.2
  187.7 3.0 copy-start.3
  187.7 3.3 %copy-start.4 = (f32[128,3072]{1,0:T(8,128)S(1)}, f32[128,3072]{1,0:T(8,128)}, u32[]{:S(2)}) copy-start(f32[128,3072]{1,0:T(8,128)} %scan_back.1) | copy-start | bytes 4718596
  195.7 2.4 copy-start.6
  212.3 6.4 %copy-start.19 = (bf16[1,256,48]{1,2,0:T(8,128)(2,1)S(1)}, bf16[1,256,48]{1,2,0:T(8,128)(2,1)}, u32[]{:S(2)}) copy-start(bf16[1,256,48]{1,2,0:T(8,128)(2,1)} %param.20) | copy-start | bytes 73732
  212.4 6.4 %copy-start.20 = (f32[48]{0:T(128)S(1)}, f32[48]{0:T(128)}, u32[]{:S(2)}) copy-start(f32[48]{0:T(128)} %param.21) | copy-start | bytes 580
  212.4 6.4 %copy-start.21 = (f32[48]{0:T(128)S(1)}, f32[48]{0:T(128)}, u32[]{:S(2)}) copy-start(f32[48]{0:T(128)} %param.22) | copy-start | bytes 580
  212.4 8.1 %copy-start.10 = (f32[3072,256]{0,1:T(8,128)S(1)}, f32[3072,256]{0,1:T(8,128)}, u32[]{:S(2)}) copy-start(f32[3072,256]{0,1:T(8,128)} %get-tuple-element.63) | copy-start | bytes 9437188

commit v2 on v1

--- a/solution.py
+++ b/solution.py
@@ -37,108 +37,226 @@
     return jnp.dot(a, b, precision=HIGHEST, preferred_element_type=jnp.float32)
 
 
-def scan_kernel(n, reverse, s_ref, thr_ref, spread_ref, out_ref, recv, stage, thr_buf, thr_wide,
-                s_send, s_recv, t_send, t_recv, o_send, o_recv):
-    me = lax.axis_index("seq")
-    ns, width = s_ref.shape
-    rows = ns // (n // 2)
-    half = width // 2
-
-    def place(k):
-        r0 = pl.multiple_of(lax.div(k, 2) * rows, 8)
-        l0 = pl.multiple_of(lax.rem(k, 2) * half, 128)
-        return pl.ds(r0, rows), pl.ds(l0, half)
-
+class Scan:
+    def __init__(self, n, reverse, s_ref, thr_ref, spread_ref, out_ref, pair, mine, recv, stage, back, give,
+                 thr_pair, thr_own, thr_buf, thr_wide, first_wide, sems):
+        me = lax.axis_index("seq")
+        self.chips, self.reverse = n // 2, reverse
+        self.core, self.chip = lax.rem(me, 2), lax.div(me, 2)
+        self.s_ref, self.thr_ref, self.spread_ref, self.out_ref = s_ref, thr_ref, spread_ref, out_ref
+        self.pair, self.mine, self.recv, self.stage, self.back, self.give = pair, mine, recv, stage, back, give
+        self.thr_pair, self.thr_own, self.thr_buf = thr_pair, thr_own, thr_buf
+        self.thr_wide, self.first_wide = thr_wide, first_wide
+        (self.ps, self.pr, self.ss, self.sr, self.ts, self.tr, self.bs, self.br, self.gs, self.gr, self.qs, self.qr) = sems
+        ns, width = s_ref.shape
+        self.rows, self.half = ns // self.chips, width // 2
+
+    def lanes(self, core):
+        return pl.ds(pl.multiple_of(core * self.half, 128), self.half)
+
+    def band(self, k):
+        return pl.ds(pl.multiple_of(k * self.rows, 8), self.rows)
+
+    def copy(self, src, dst, ss, rs, to):
+        return pltpu.make_async_remote_copy(src_ref=src, dst_ref=dst, send_sem=ss, recv_sem=rs,
+                                            device_id={"seq": to}, device_id_type=MESH)
+
+    def sibling(self):
+        return self.chip * 2 + 1 - self.core
+
+    def peer(self, k):
+        return k * 2 + self.core
+
+    def greet(self, barrier):
+        pl.semaphore_signal(barrier, inc=1, device_id={"seq": self.sibling()}, device_id_type=MESH)
+
+        def one(i, _):
+            k = lax.rem(self.chip + 1 + i, self.chips)
+            pl.semaphore_signal(barrier, inc=1, device_id={"seq": self.peer(k)}, device_id_type=MESH)
+            return 0
+
+        lax.fori_loop(0, self.chips - 1, one, 0)
+        return self.chips
+
+    def pair_copy(self, k):
+        return self.copy(self.s_ref.at[self.band(k), self.lanes(1 - self.core)], self.pair.at[k],
+                         self.ps.at[k], self.pr.at[k], self.sibling())
+
+    def thr_pair_copy(self):
+        return self.copy(self.thr_ref, self.thr_pair, self.qs, self.qr, self.sibling())
+
+    def thr_copy(self, k, slot):
+        return self.copy(self.thr_own, self.thr_buf.at[slot], self.ts.at[k], self.tr.at[slot], self.peer(k))
+
+    def chunk_copy(self, k, slot):
+        return self.copy(self.mine.at[k], self.recv.at[slot], self.ss.at[k], self.sr.at[slot], self.peer(k))
+
+    def back_copy(self, k, slot):
+        return self.copy(self.stage.at[k], self.back.at[slot], self.bs.at[k], self.br.at[slot], self.peer(k))
+
+    def give_copy(self, k, core):
+        return self.copy(self.give.at[k], self.out_ref.at[self.band(k), self.lanes(core)], self.gs.at[k], self.gr.at[k],
+                         self.sibling())
+
+    def begin(self):
+        self.thr_pair_copy().start()
+
+        def one(i, _):
+            self.pair_copy(lax.rem(self.chip + 1 + i, self.chips)).start()
+            return 0
+
+        lax.fori_loop(0, self.chips, one, 0)
+
+    def exchange(self):
+        first = 1 if self.reverse else 0
+        self.thr_pair_copy().wait_recv()
+        mine_first = self.core == first
+        thr_first = jnp.where(mine_first, self.thr_ref[...], self.thr_pair[...])
+        thr_second = jnp.where(mine_first, self.thr_pair[...], self.thr_ref[...])
+        self.thr_own[...] = thr_first * thr_second
+        self.thr_buf[self.chip] = thr_first * thr_second
+
+        def tell(i, _):
+            self.thr_copy(lax.rem(self.chip + 1 + i, self.chips), self.chip).start()
+            return 0
+
+        lax.fori_loop(0, self.chips - 1, tell, 0)
+        both = jnp.concatenate([thr_first, thr_second], axis=0)
+        wide = jnp.dot(both, self.spread_ref[:, self.lanes(self.core)], precision=HIGHEST,
+                       preferred_element_type=jnp.float32)
+        self.first_wide[...] = wide[0:8]
+        second_wide = wide[8:16]
+
+        def one(i, _):
+            k = lax.rem(self.chip + 1 + i, self.chips)
+            self.pair_copy(k).wait_recv()
+            own = self.s_ref[self.band(k), self.lanes(self.core)]
+            other = self.pair[k]
+            early = jnp.where(mine_first, own, other)
+            late = jnp.where(mine_first, other, own)
+            self.mine[k] = second_wide * early + late
+
+            @pl.when(k != self.chip)
+            def _():
+                self.chunk_copy(k, self.chip).start()
+
+            return 0
+
+        lax.fori_loop(0, self.chips, one, 0)
+        self.recv[self.chip] = self.mine[self.chip]
+
+    def hops(self):
+        def arrive(i, _):
+            self.thr_copy(self.chip, lax.rem(self.chip + 1 + i, self.chips)).wait_recv()
+            return 0
+
+        lax.fori_loop(0, self.chips - 1, arrive, 0)
+        self.thr_wide[...] = jnp.dot(self.thr_buf[:, 0, :], self.spread_ref[:, self.lanes(self.core)],
+                                     precision=HIGHEST, preferred_element_type=jnp.float32)
+
+        def hop(i, state):
+            j = self.chips - 1 - i if self.reverse else i
+
+            @pl.when(j != self.chip)
+            def _():
+                self.chunk_copy(self.chip, j).wait_recv()
+
+            self.stage[j] = state
+
+            @pl.when(j != self.chip)
+            def _():
+                self.back_copy(j, self.chip).start()
+
+            return self.thr_wide[pl.ds(j, 1), :] * state + self.recv[j]
+
+        lax.fori_loop(0, self.chips, hop, jnp.zeros((self.rows, self.half), jnp.float32))
+        self.back[self.chip] = self.stage[self.chip]
+
+    def deliver(self):
+        mine_first = self.core == (1 if self.reverse else 0)
+
+        def one(i, _):
+            k = lax.rem(self.chip + i, self.chips)
+
+            @pl.when(k != self.chip)
+            def _():
+                self.back_copy(self.chip, k).wait_recv()
+
+            early = self.back[k]
+            own = self.s_ref[self.band(k), self.lanes(self.core)]
+            late = self.first_wide[...] * early + jnp.where(mine_first, own, self.pair[k])
+            self.out_ref[self.band(k), self.lanes(self.core)] = jnp.where(mine_first, early, late)
+            self.give[k] = jnp.where(mine_first, late, early)
+            self.give_copy(k, self.core).start()
+            return 0
+
+        lax.fori_loop(0, self.chips, one, 0)
+
+        def got(k, _):
+            self.give_copy(k, 1 - self.core).wait_recv()
+            return 0
+
+        lax.fori_loop(0, self.chips, got, 0)
+
+    def finish(self):
+        self.thr_pair_copy().wait_send()
+
+        def one(i, _):
+            k = lax.rem(self.chip + 1 + i, self.chips)
+            self.pair_copy(k).wait_send()
+            self.give_copy(k, self.core).wait_send()
+
+            @pl.when(k != self.chip)
+            def _():
+                self.thr_copy(k, self.chip).wait_send()
+                self.chunk_copy(k, self.chip).wait_send()
+                self.back_copy(k, self.chip).wait_send()
+
+            return 0
+
+        lax.fori_loop(0, self.chips, one, 0)
+
+
+def scan_scratch(n, ns, width):
+    chips = n // 2
+    chunk = pltpu.VMEM((chips, ns // chips, width // 2), jnp.float32)
+    tile = pltpu.VMEM((8, 128), jnp.float32)
+    return [chunk] * 6 + [
+        tile,
+        tile,
+        pltpu.VMEM((chips, 8, 128), jnp.float32),
+        pltpu.VMEM((chips, width // 2), jnp.float32),
+        pltpu.VMEM((8, width // 2), jnp.float32),
+    ] + [pltpu.SemaphoreType.DMA((chips,))] * 10 + [pltpu.SemaphoreType.DMA] * 2
+
+
+SCAN_SCRATCH = 11 + 12
+
+
+def make_scan(n, reverse, s_ref, thr_ref, spread_ref, out_ref, scratch):
+    return Scan(n, reverse, s_ref, thr_ref, spread_ref, out_ref, *scratch[:11], scratch[11:])
+
+
+def scan_kernel(n, reverse, s_ref, thr_ref, spread_ref, out_ref, *scratch):
+    scan = make_scan(n, reverse, s_ref, thr_ref, spread_ref, out_ref, scratch)
     barrier = pltpu.get_barrier_semaphore()
-
-    def greet(i, _):
-        peer = lax.rem(me + 1 + i, n)
-        pl.semaphore_signal(barrier, inc=1, device_id={"seq": peer}, device_id_type=MESH)
-        return 0
-
-    lax.fori_loop(0, n - 1, greet, 0)
-    pl.semaphore_wait(barrier, n - 1)
-
-    def thr_copy(k, slot):
-        return pltpu.make_async_remote_copy(
-            src_ref=thr_ref, dst_ref=thr_buf.at[slot], send_sem=t_send.at[k],
-            recv_sem=t_recv.at[slot], device_id={"seq": k}, device_id_type=MESH)
-
-    def s_copy(k, slot):
-        r, l = place(k)
-        return pltpu.make_async_remote_copy(
-            src_ref=s_ref.at[r, l], dst_ref=recv.at[slot], send_sem=s_send.at[k],
-            recv_sem=s_recv.at[slot], device_id={"seq": k}, device_id_type=MESH)
-
-    def o_copy(k, owner):
-        r, l = place(owner)
-        return pltpu.make_async_remote_copy(
-            src_ref=stage.at[k], dst_ref=out_ref.at[r, l], send_sem=o_send.at[k],
-            recv_sem=o_recv.at[owner], device_id={"seq": k}, device_id_type=MESH)
-
-    def send(i, _):
-        k = lax.rem(me + 1 + i, n)
-        thr_copy(k, me).start()
-        s_copy(k, me).start()
-        return 0
-
-    lax.fori_loop(0, n - 1, send, 0)
-    my_r, my_l = place(me)
-    recv[me] = s_ref[my_r, my_l]
-    thr_buf[me] = thr_ref[...]
-
-    def arrive(i, _):
-        thr_copy(me, lax.rem(me + 1 + i, n)).wait_recv()
-        return 0
-
-    lax.fori_loop(0, n - 1, arrive, 0)
-    thr_wide[...] = jnp.dot(thr_buf[:, 0, :], spread_ref[:, my_l], precision=HIGHEST,
-                            preferred_element_type=jnp.float32)
-
-    def hop(i, state):
-        j = n - 1 - i if reverse else i
-
-        @pl.when(j != me)
-        def _():
-            s_copy(me, j).wait_recv()
-
-        stage[j] = state
-
-        @pl.when(j != me)
-        def _():
-            o_copy(j, me).start()
-
-        return thr_wide[pl.ds(j, 1), :] * state + recv[j]
-
-    lax.fori_loop(0, n, hop, jnp.zeros((rows, half), jnp.float32))
-    out_ref[my_r, my_l] = stage[me]
-
-    def finish(i, _):
-        k = lax.rem(me + 1 + i, n)
-        o_copy(me, k).wait_recv()
-        thr_copy(k, me).wait_send()
-        s_copy(k, me).wait_send()
-        o_copy(k, me).wait_send()
-        return 0
-
-    lax.fori_loop(0, n - 1, finish, 0)
+    pl.semaphore_wait(barrier, scan.greet(barrier))
+    scan.begin()
+    scan.exchange()
+    scan.hops()
+    scan.deliver()
+    scan.finish()
 
 
 def state_scan(n, state, thr, spread, reverse):
     ns, width = state.shape
-    rows, half = ns // (n // 2), width // 2
     vmem = pl.BlockSpec(memory_space=pltpu.VMEM)
     return pl.pallas_call(
         functools.partial(scan_kernel, n, reverse),
         out_shape=jax.ShapeDtypeStruct((ns, width), jnp.float32),
         in_specs=[vmem] * 3,
         out_specs=vmem,
-        scratch_shapes=[
-            pltpu.VMEM((n, rows, half), jnp.float32),
-            pltpu.VMEM((n, rows, half), jnp.float32),
-            pltpu.VMEM((n, 8, 128), jnp.float32),
-            pltpu.VMEM((n, half), jnp.float32),
-        ] + [pltpu.SemaphoreType.DMA((n,))] * 6,
+        scratch_shapes=scan_scratch(n, ns, width),
         compiler_params=pltpu.CompilerParams(
             collective_id=2 if reverse else 1, has_side_effects=True,
             vmem_limit_bytes=VMEM_LIMIT),
@@ -436,9 +554,9 @@
 
     dfx = dot2(gm2, du2, 0, 0) + dot2(b_keep, ds2, 1, 0)
     dx = (f * dfx + skip * dy).astype(bf16)
-    dgm2 = split(jnp.where(mask, bdot(du, fx, 1, 1), 0.0))
-    dc = dot2(dgm2, bmap, 1, 0) + jnp.where(opened, bdot(du, s_in, 1, 1), 0.0)
-    db = dot2(dgm2, cmap, 0, 0) + jnp.where(keep, bdot(fx, ds, 1, 1), 0.0)
+    dgm2 = split(jnp.where(mask, dot2(du2, fx, 1, 1), 0.0))
+    dc = dot2(dgm2, bmap, 1, 0) + jnp.where(opened, dot2(du2, s_in, 1, 1), 0.0)
+    db = dot2(dgm2, cmap, 0, 0) + jnp.where(keep, dot2(fx, ds2, 1, 1), 0.0)
     skip_row = jnp.sum(dy * xf, axis=0, keepdims=True)
     end_row = jnp.sum(ds_f * s_own + through_wide * later * incoming, axis=0, keepdims=True)
     a_wide = fx_f * dfx

time: 298 us -> 250 us (0.84)
  Pallas kernels: 195 us -> 146 us
    pallas_call x2, Pallas kernels: 125 us -> 75.2 us  [state_scan(): pl.pallas_call(functools.partial(scan_kernel, n, reverse), out_shape=jax....]
    dot_general x24 -> x27, matrix products: 49.9 us -> 52.3 us  [bdot(): lax.dot_general(a, b, (((ca,), (cb,)), ((), ())), preferred_element_type=...]
    unnamed x49 -> x47, local copies, waits for them, and re-layouts: 9.9 us -> 9.27 us
where the time goes in v2:
time: 250 us
  Pallas kernels  146 us (58%)
  matrix products  62.8 us (25%)
  other arithmetic  20.5 us (8%)
  local copies, waits for them, and re-layouts  18.1 us (7%)
    pallas_call x2, Pallas kernels, state_scan(): pl.pallas_call(functools.partial(scan_kernel, n, reverse), out_shape=jax....  75.2 us
    pallas_call x1, Pallas kernels, reduce_weight(): pl.pallas_call(reduce_kernel, out_shape=(jax.ShapeDtypeStruct((4, quarter...  71.3 us
    dot_general x27, matrix products, bdot(): lax.dot_general(a, b, (((ca,), (cb,)), ((), ())), preferred_element_type=...  52.3 us
    dot_general x4, matrix products, exact(): return jnp.dot(a, b, precision=HIGHEST, preferred_element_type=jnp.float32)  10.5 us
    unnamed x47, local copies, waits for them, and re-layouts  9.27 us

profile of v2, /device:TPU:0, one launch (start us, length us, event | category | flops | bytes accessed | tf_op | source)
XLA Modules:
  0.0 249.6 jit_solution(6091200881345986975)
XLA Ops:
  0.7 0.6 compare_reduce_fusion
  1.3 0.7 neg.16
  2.0 1.4 fusion.102
  3.3 3.2 %fusion.75 = f32[]{:T(128)} fusion(s32[]{:T(128)} %bitcast.5, s32[]{:T(128)} %bitcast.4, s32[]{:T(128)} %bitcast.3, s32[]{:T(128)} %bitcast.2, s32[]{:T(128)S(6)} %mul.182), kind=kLoop, calls=%fused_computation.147 | loop fusion | flops 2559 | bytes 24 | tf_op jit(solution)/shard_map/reduce_sum | solution.py:490
  7.2 2.6 %compare_or_fusion = pred[256]{0:T(512)(128)(4,1)S(1)} fusion(s32[]{:T(128)} %bitcast.5, s32[]{:T(128)} %bitcast.4, s32[]{:T(128)} %bitcast.3, s32[]{:T(128)} %bitcast.2, s32[]{:T(128)S(6)} %mul.182), kind=kLoop, calls=%fused_computation.145 | loop fusion | flops 2048 | bytes 276 | tf_op jit(solution)/shard_map/or | solution.py:487
  10.0 0.7 broadcast_compare_fusion.1
  10.6 0.7 copy.27
  11.4 1.0 fusion.46
  12.4 0.8 select_reduce_fusion.2
  13.9 0.9 exponential_multiply_fusion
  14.9 1.1 convolution_select_fusion
  16.0 1.3 pad_convert_fusion.spread_ref
  17.3 1.4 bitcast_convert_fusion.og_ref
  18.7 2.7 %fusion.91 = f32[516,3072]{1,0:T(8,128)S(1)} fusion(f32[516,48]{0,1:T(8,128)S(1)} %concatenate.13, s32[3072]{0:T(1024)S(1)} %get-tuple-element.85, s32[3072]{0:T(1024)S(1)} %get-tuple-element.86, pred[3072]{0:T(1024)(128)(4,1)S(1)} %fusion.74), kind=kOutput, calls=%fused_computation.166 | convolution fusion | flops 913342464 | bytes 6467328 | tf_op jit(solution)/shard_map/dot_general | solution.py:37
  21.5 0.6 subtract_convert_fusion.1
  22.1 2.0 copy-done
  24.6 2.2 broadcast_multiply_fusion
  26.8 34.2 %scan_ahead.1 = f32[128,3072]{1,0:T(8,128)} custom-call(f32[128,3072]{1,0:T(8,128)} %get-tuple-element.81.s_ref, f32[8,128]{1,0:T(8,128)} %scatter.15.thr_ref, f32[128,3072]{1,0:T(8,128)} %pad_convert_fusion.spread_ref), custom_call_target="tpu_custom_call" | custom-call | tf_op jit(solution)/shard_map/scan_ahead/pallas_call | solution.py:254
  61.0 2.1 fusion.85
  63.2 0.6 fusion.48
  64.4 0.6 fusion.11
  65.0 0.9 slice-done
  66.0 0.9 slice-done.1
  67.2 3.6 %multiply_reduce_fusion.2 = (f32[256]{0:T(256)S(1)}, f32[256,3072]{1,0:T(8,128)S(1)}, f32[256,3072]{1,0:T(8,128)}) fusion(bf16[1,256,3072]{2,1,0:T(8,128)(2,1)S(1)} %copy-done.12, bf16[1,256,3072]{2,1,0:T(8,128)(2,1)S(1)} %copy-done.7, f32[3072]{0:T(1024)S(1)} %bitcast.149, f32[516,3072]{1,0:T(8,128)S(1)} %bitcast.135, f32[256,3072]{1,0:T(8,128)S(1)} %fusion.11, ...), kind=kOutput, calls=%fused_computation.42 | convolution fusion | flops 214335232 | bytes 20538624 | tf_op jit(solution)/shard_map/dot_general | solution.py:16
  70.8 8.4 %fusion.22 = bf16[1,256,1536]{2,1,0:T(8,128)(2,1)} fusion(bf16[3072,1536]{1,0:T(8,128)(2,1)} %param.25, f32[256,3072]{1,0:T(8,128)S(1)} %get-tuple-element.54, f32[3072]{0:T(1024)S(1)} %copy-done.17, f32[256]{0:T(256)S(1)} %add_rsqrt_fusion), kind=kOutput, calls=%fused_computation.46 | convolution fusion | flops 2418671616 | bytes 13382656 | tf_op jit(solution)/shard_map/dot_general | solution.py:16
  79.2 8.1 %multiply_reduce_fusion = (f32[3072]{0:T(1024)S(1)}, f32[256]{0:T(256)S(1)}, f32[256,3072]{1,0:T(8,128)}) fusion(f32[256,3072]{1,0:T(8,128)S(1)} %get-tuple-element.54, f32[256]{0:T(256)S(1)} %add_rsqrt_fusion, f32[3072]{0:T(1024)S(1)} %copy-done.17, bf16[3072,1536]{1,0:T(8,128)(2,1)} %param.25, bf16[1,256,1536]{2,1,0:T(8,128)(2,1)S(1)} %copy-done.16), kind=kOutput, calls=%fused_computation.35 | convolution fusion | flops 2420634368 | bytes 16541696 | tf_op jit(solution)/shard_map/dot_general | solution.py:16
  87.3 4.0 %fusion.14 = (f32[3072]{0:T(1024)S(1)}, f32[256,3072]{1,0:T(8,128)S(1)}) fusion(bf16[1,256,3072]{2,1,0:T(8,128)(2,1)S(1)} %copy-done.7, bf16[1,256,3072]{2,1,0:T(8,128)(2,1)S(1)} %copy-done.12, f32[256]{0:T(256)S(1)} %broadcast_multiply_fusion.1, f32[256,3072]{1,0:T(8,128)S(1)} %get-tuple-element.54, f32[256,3072]{1,0:T(8,128)} %get-tuple-element.84, ...), kind=kLoop, calls=%fused_computation.26 | loop fusion | flops 11006976 | bytes 12609536 | tf_op jit(solution)/shard_map/reduce_sum | solution.py:560
  91.3 0.6 subtract_convert_fusion
  91.9 1.0 copy-done.3
  94.1 0.6 fusion.27
  95.1 1.2 fusion.34
  97.3 1.7 fusion.12.s_ref
  99.0 41.0 %scan_back.1 = f32[128,3072]{1,0:T(8,128)} custom-call(f32[128,3072]{1,0:T(8,128)} %fusion.12.s_ref, f32[8,128]{1,0:T(8,128)} %scatter.15.thr_ref, f32[128,3072]{1,0:T(8,128)} %pad_convert_fusion.spread_ref), custom_call_target="tpu_custom_call" | custom-call | tf_op jit(solution)/shard_map/scan_back/pallas_call | solution.py:254
  139.9 2.9 %add_reduce_fusion = f32[3072]{0:T(1024)S(1)} fusion(f32[128,3072]{1,0:T(8,128)} %scan_ahead.1, f32[128,3072]{1,0:T(8,128)} %scan_back.1, f32[128,3072]{1,0:T(8,128)} %get-tuple-element.82, f32[3072]{0:T(1024)S(1)} %bitcast.151, f32[3072]{0:T(1024)S(1)} %bitcast.138), kind=kLoop, calls=%fused_computation.48 | loop fusion | flops 2356224 | bytes 4755456 | tf_op jit(solution)/shard_map/reduce_sum | solution.py:561
  143.5 1.2 fusion.35
  145.3 2.3 fusion.42
  148.2 2.3 fusion.9
  150.6 1.1 copy-done.8
  151.6 1.0 copy-done.11
  152.6 11.0 %multiply_subtract_fusion = (f32[256,3072]{1,0:T(8,128)}, f32[256,3072]{1,0:T(8,128)}, bf16[1,256,3072]{2,1,0:T(8,128)(2,1)}, bf16[1,256,3072]{2,1,0:T(8,128)(2,1)}, f32[3072,256]{0,1:T(8,128)S(1)}) fusion(f32[256,3072]{1,0:T(8,128)} %get-tuple-element.83, f32[256,3072]{1,0:T(8,128)S(1)} %copy-done.4, f32[516,3072]{1,0:T(8,128)} %copy-done, ...), kind=kOutput, calls=%fused_computation.36 | convolution fusion | flops 230064128 | bytes 42572032 | tf_op jit(solution)/shard_map/dot_general | solution.py:16
  163.7 5.8 %fusion = f32[514,48]{0,1:T(8,128)S(1)} fusion(f32[1,3072]{1,0:T(1,128)S(1)} %bitcast.153, f32[1,3072]{1,0:T(1,128)S(1)} %bitcast.152, f32[256,3072]{1,0:T(8,128)} %get-tuple-element.47, f32[256,3072]{1,0:T(8,128)} %get-tuple-element.48, s32[3072]{0:T(1024)S(1)} %get-tuple-element.85, s32[3072]{0:T(1024)S(1)} %get-tuple-element.86, pred[3072]{0:T(1024)(128)(4,1)S(1)} %fusion.74), kind=kOutput, calls=%fused_computation | convolution fusion | flops 914540544 | bytes 6442368 | tf_op jit(solution)/shard_map/dot_general | solution.py:37
  169.7 1.0 fusion.93
  170.8 0.6 pad_bitcast_fusion.small_ref
  171.4 2.4 copy.28
  173.7 71.3 %reduce_weight.1 = (f32[4,24,1536]{2,1,0:T(8,128)}, f32[32,128]{1,0:T(8,128)}) custom-call(f32[16,2,96,256]{3,2,1,0:T(8,128)} %bitcast.136, f32[256,1536]{1,0:T(8,128)} %bitcast_convert_fusion.og_ref, f32[32,128]{1,0:T(8,128)} %pad_bitcast_fusion.small_ref), custom_call_target="tpu_custom_call" | custom-call | tf_op jit(solution)/shard_map/reduce_weight/pallas_call | solution.py:434
  245.0 1.4 fusion.101
  246.4 1.3 slice_bitcast_fusion
  247.7 1.9 copy.30
  (65 shorter events, 7.2 us)
Async XLA Ops:
  0.6 16.6 %copy-start.15 = (bf16[1,256,1536]{2,1,0:T(8,128)(2,1)S(1)}, bf16[1,256,1536]{2,1,0:T(8,128)(2,1)}, u32[]{:S(2)}) copy-start(bf16[1,256,1536]{2,1,0:T(8,128)(2,1)} %param.27) | copy-start | bytes 2359300
  18.7 2.8 %copy-start.7 = (bf16[1,256,3072]{2,1,0:T(8,128)(2,1)S(1)}, bf16[1,256,3072]{2,1,0:T(8,128)(2,1)}, u32[]{:S(2)}) copy-start(bf16[1,256,3072]{2,1,0:T(8,128)(2,1)} %param.16) | copy-start | bytes 4718596
  21.4 2.7 %copy-start = (f32[516,3072]{1,0:T(8,128)}, f32[516,3072]{1,0:T(8,128)S(1)}, u32[]{:S(2)}) copy-start(f32[516,3072]{1,0:T(8,128)S(1)} %fusion.91) | copy-start | bytes 19021828
  21.5 2.6 %copy-start.13 = (bf16[1,256,128]{2,1,0:T(8,128)(2,1)S(1)}, bf16[1,256,128]{2,1,0:T(8,128)(2,1)}, u32[]{:S(2)}) copy-start(bf16[1,256,128]{2,1,0:T(8,128)(2,1)} %param.18) | copy-start | bytes 196612
  24.1 2.7 %copy-start.9 = (bf16[256,3072]{1,0:T(8,128)(2,1)}, bf16[256,3072]{1,0:T(8,128)(2,1)S(1)}, u32[]{:S(2)}) copy-start(bf16[256,3072]{1,0:T(8,128)(2,1)S(1)} %get-tuple-element.57) | copy-start | bytes 4718596
  61.0 2.1 copy-start.2
  61.0 2.1 copy-start.14
  63.8 2.2 slice-start
  64.4 2.5 slice-start.1
  64.4 2.9 %copy-start.12 = (bf16[1,256,3072]{2,1,0:T(8,128)(2,1)S(1)}, bf16[1,256,3072]{2,1,0:T(8,128)(2,1)}, u32[]{:S(2)}) copy-start(bf16[1,256,3072]{2,1,0:T(8,128)(2,1)} %param.17) | copy-start | bytes 4718596
  67.2 3.6 %copy-start.17 = (f32[3072]{0:T(1024)S(1)}, f32[3072]{0:T(1024)}, u32[]{:S(2)}) copy-start(f32[3072]{0:T(1024)} %param.24) | copy-start | bytes 36868
  70.8 16.5 %copy-start.10 = (f32[256,3072]{1,0:T(8,128)}, f32[256,3072]{1,0:T(8,128)S(1)}, u32[]{:S(2)}) copy-start(f32[256,3072]{1,0:T(8,128)S(1)} %get-tuple-element.54) | copy-start | bytes 9437188
  70.8 8.4 %copy-start.16 = (bf16[1,256,1536]{2,1,0:T(8,128)(2,1)S(1)}, bf16[1,256,1536]{2,1,0:T(8,128)(2,1)}, u32[]{:S(2)}) copy-start(bf16[1,256,1536]{2,1,0:T(8,128)(2,1)} %param.27) | copy-start | bytes 2359300
  91.3 1.7 copy-start.3
  92.9 4.4 %copy-start.5 = (bf16[256,3072]{1,0:T(8,128)(2,1)}, bf16[256,3072]{1,0:T(8,128)(2,1)S(1)}, u32[]{:S(2)}) copy-start(bf16[256,3072]{1,0:T(8,128)(2,1)S(1)} %get-tuple-element.51) | copy-start | bytes 4718596
  139.9 2.9 %copy-start.1 = (f32[128,3072]{1,0:T(8,128)S(1)}, f32[128,3072]{1,0:T(8,128)}, u32[]{:S(2)}) copy-start(f32[128,3072]{1,0:T(8,128)} %scan_back.1) | copy-start | bytes 4718596
  142.9 1.8 copy-start.6
  148.1 2.4 copy-start.4
  148.2 3.5 %copy-start.8 = (bf16[1,256,3072]{2,1,0:T(8,128)(2,1)S(1)}, bf16[1,256,3072]{2,1,0:T(8,128)(2,1)}, u32[]{:S(2)}) copy-start(bf16[1,256,3072]{2,1,0:T(8,128)(2,1)} %param.16) | copy-start | bytes 4718596
  148.2 4.4 %copy-start.11 = (f32[256,3072]{1,0:T(8,128)S(1)}, f32[256,3072]{1,0:T(8,128)}, u32[]{:S(2)}) copy-start(f32[256,3072]{1,0:T(8,128)} %copy-done.10) | copy-start | bytes 9437188
  163.6 6.0 %copy-start.18 = (bf16[1,256,48]{1,2,0:T(8,128)(2,1)S(1)}, bf16[1,256,48]{1,2,0:T(8,128)(2,1)}, u32[]{:S(2)}) copy-start(bf16[1,256,48]{1,2,0:T(8,128)(2,1)} %param.20) | copy-start | bytes 73732
  163.7 6.0 %copy-start.19 = (f32[48]{0:T(128)S(1)}, f32[48]{0:T(128)}, u32[]{:S(2)}) copy-start(f32[48]{0:T(128)} %param.21) | copy-start | bytes 580
  163.7 6.0 %copy-start.20 = (f32[48]{0:T(128)S(1)}, f32[48]{0:T(128)}, u32[]{:S(2)}) copy-start(f32[48]{0:T(128)} %param.22) | copy-start | bytes 580

commit v3 on v2

--- a/solution.py
+++ b/solution.py
@@ -16,6 +16,11 @@
     return lax.dot_general(
         a, b, (((ca,), (cb,)), ((), ())), preferred_element_type=jnp.float32
     )
+
+
+def split_wide(v):
+    hi = lax.reduce_precision(v, exponent_bits=8, mantissa_bits=7)
+    return hi.astype(jnp.bfloat16), (v - hi).astype(jnp.bfloat16)
 
 
 def split(v):
@@ -267,205 +272,343 @@
 ORDERS = ((2, 1, 0), (1, 0, 2), (0, 2, 1))
 
 
-def reduce_kernel(nt_ref, og_ref, small_ref, out_ref, small_out, part, nt_got, og_got,
-                  agg1, full1, agg2, full2, agg3, full3, slots_c, slots_a, total,
-                  c_send, c_recv, r_send, r_recv, x_send, x_recv, m_send, m_recv):
-    xi = lax.axis_index("dp")
-    s = lax.axis_index("seq")
-    zi, yi, core = lax.div(s, 8), lax.rem(lax.div(s, 2), 4), lax.rem(s, 2)
-    here = (zi, yi, xi)
-    cols = part.shape[-1]
-    third = cols // 3
-    half = third // 2
-
-    def at(axis, index):
+class Ring:
+    def __init__(self, nt_ref, og_ref, out_ref, small, small_out, part, nt_got, og_got, agg1, full1, agg2, full2,
+                 agg3, full3, slots_c, slots_a, total, sems):
+        (self.cs, self.cr, self.rs, self.rr, self.xs, self.xr, self.ms, self.mr) = sems
+        self.xi = lax.axis_index("dp")
+        s = lax.axis_index("seq")
+        self.core = lax.rem(s, 2)
+        self.here = (lax.div(s, 8), lax.rem(lax.div(s, 2), 4), self.xi)
+        self.sibling = {"seq": s + 1 - 2 * self.core}
+        self.nt_ref, self.og_ref, self.out_ref = nt_ref, og_ref, out_ref
+        self.small, self.small_out = small, small_out
+        self.part, self.nt_got, self.og_got = part, nt_got, og_got
+        self.bufs = ((agg1, full1), (agg2, full2), (agg3, full3))
+        self.slots_c, self.slots_a, self.total = slots_c, slots_a, total
+        self.third = part.shape[-1] // 3
+        self.half = self.third // 2
+        self.started = []
+        self.steps = {}
+
+    def at(self, axis, index):
         if axis == 2:
             return {"dp": index}
-        z, y = (index, yi) if axis == 0 else (zi, index)
-        return {"seq": (z * 4 + y) * 2 + core}
-
-    sibling = {"seq": s + 1 - 2 * core}
-    barrier = pltpu.get_barrier_semaphore()
-    pl.semaphore_signal(barrier, inc=1, device_id=sibling, device_id_type=MESH)
-    for axis in range(3):
-        for d in range(1, 4):
-            pl.semaphore_signal(barrier, inc=1, device_id=at(axis, lax.rem(here[axis] + d, 4)),
-                                device_id_type=MESH)
-    pl.semaphore_wait(barrier, 10)
-
-    def remote(src, dst, ss, rs, to):
+        z, y = (index, self.here[1]) if axis == 0 else (self.here[0], index)
+        return {"seq": (z * 4 + y) * 2 + self.core}
+
+    def remote(self, src, dst, ss, rs, to):
         return pltpu.make_async_remote_copy(src_ref=src, dst_ref=dst, send_sem=ss, recv_sem=rs,
                                             device_id=to, device_id_type=MESH)
 
-    started = []
-
-    copies = [
-        remote(og_ref, og_got, c_send.at[0], c_recv.at[0], sibling),
-        remote(nt_ref.at[:, 1 - core], nt_got, c_send.at[1], c_recv.at[1], sibling),
-        remote(small_ref, slots_c.at[core], c_send.at[2], c_recv.at[2], sibling),
-    ]
-    for c in copies:
-        c.start()
-    slots_c[core] = small_ref[...]
-    og = og_ref[...].astype(jnp.bfloat16)
-
-    def own(b, _):
-        z, y = lax.div(b, 4), lax.rem(b, 4)
-        lhs = nt_ref[b, core].astype(jnp.bfloat16)
-        part[z, y] = bdot(lhs, og, 1, 0).reshape(part.shape[2:])
-        return 0
-
-    lax.fori_loop(0, 16, own, 0)
-    for c in copies:
-        c.wait_recv()
-    og2 = og_got[...].astype(jnp.bfloat16)
-
-    def theirs(b, _):
-        z, y = lax.div(b, 4), lax.rem(b, 4)
-        lhs = nt_got[b].astype(jnp.bfloat16)
-        part[z, y] += bdot(lhs, og2, 1, 0).reshape(part.shape[2:])
-        return 0
-
-    lax.fori_loop(0, 16, theirs, 0)
-    total[...] = slots_c[0] + slots_c[1]
-
-    bufs = ((agg1, full1), (agg2, full2), (agg3, full3))
-    small_axes = (2, 1, 0)
-    for step in range(3):
-        agg, full = bufs[step]
-
-        def small_copy(d):
-            axis = small_axes[step]
-            return remote(total, slots_a.at[step, here[axis]], m_send.at[step, d - 1],
-                          m_recv.at[step, d - 1], at(axis, lax.rem(here[axis] + d, 4)))
-
-        smalls = [small_copy(d) for d in (1, 2, 3)]
-        for c in smalls:
+    def start(self, copies):
+        for c in copies:
             c.start()
-        slots_a[step, here[small_axes[step]]] = total[...]
-
-        def region(p, t, h=None):
-            order = ORDERS[p]
-            index = [slice(None)] * 3
-            for done in order[:step]:
-                index[done] = here[done]
-            index[order[step]] = t
-            lo = p * third + (0 if h in (None, 0) else half)
-            return (*index, slice(None), pl.ds(lo, third if h is None else half))
-
-        def sem(p, k):
-            return r_send.at[step, p, k], r_recv.at[step, p, k]
-
+        self.started += copies
+        return copies
+
+    def pair_begin(self):
+        self.pair = self.start([
+            self.remote(self.og_ref, self.og_got, self.cs.at[0], self.cr.at[0], self.sibling),
+            self.remote(self.nt_ref.at[:, 1 - self.core], self.nt_got, self.cs.at[1], self.cr.at[1], self.sibling),
+        ])
+
+    def own(self):
+        og = self.og_ref[...].astype(jnp.bfloat16)
+
+        def one(b, _):
+            z, y = lax.div(b, 4), lax.rem(b, 4)
+            lhs = self.nt_ref[b, self.core].astype(jnp.bfloat16)
+            self.part[z, y] = bdot(lhs, og, 1, 0).reshape(self.part.shape[2:])
+            return 0
+
+        lax.fori_loop(0, 16, one, 0)
+
+    def theirs(self):
+        for c in self.pair:
+            c.wait_recv()
+        og = self.og_got[...].astype(jnp.bfloat16)
+
+        def one(b, _):
+            z, y = lax.div(b, 4), lax.rem(b, 4)
+            lhs = self.nt_got[b].astype(jnp.bfloat16)
+            self.part[z, y] += bdot(lhs, og, 1, 0).reshape(self.part.shape[2:])
+            return 0
+
+        lax.fori_loop(0, 16, one, 0)
+
+    def region(self, step, p, t, h=None):
+        order = ORDERS[p]
+        index = [slice(None)] * 3
+        for done in order[:step]:
+            index[done] = self.here[done]
+        index[order[step]] = t
+        lo = p * self.third + (0 if h in (None, 0) else self.half)
+        return (*index, slice(None), pl.ds(lo, self.third if h is None else self.half))
+
+    def ways(self, step, p):
+        axis = ORDERS[p][step]
+        me = self.here[axis]
+        return axis, lax.rem(me + 1, 4), lax.rem(me + 3, 4), lax.rem(me + 2, 4)
+
+    def begin(self, step):
+        agg, full = self.bufs[step]
         first, second, last = [], [], []
+        lo, hi = pl.ds(0, self.half), pl.ds(self.half, self.half)
         for p in range(3):
-            axis = ORDERS[p][step]
-            me = here[axis]
-            up, down, far = lax.rem(me + 1, 4), lax.rem(me + 3, 4), lax.rem(me + 2, 4)
-            a = [
-                remote(part.at[region(p, far, 0)], agg.at[p, 0], *sem(p, 0), at(axis, up)),
-                remote(part.at[region(p, far, 1)], agg.at[p, 1], *sem(p, 1), at(axis, down)),
-            ]
-            b = [
-                remote(part.at[region(p, up, 1)], full.at[p, 0, ..., pl.ds(half, half)], *sem(p, 2), at(axis, up)),
-                remote(part.at[region(p, down, 0)], full.at[p, 1, ..., pl.ds(0, half)], *sem(p, 3), at(axis, down)),
-            ]
-            c = [
-                remote(part.at[region(p, up, 0)], full.at[p, 0, ..., pl.ds(0, half)], *sem(p, 4), at(axis, up)),
-                remote(part.at[region(p, down, 1)], full.at[p, 1, ..., pl.ds(half, half)], *sem(p, 5), at(axis, down)),
-            ]
-            first.append(a)
-            second.append(b)
-            last.append(c)
+            axis, up, down, far = self.ways(step, p)
+
+            def go(t, h, dst, k, to):
+                return self.remote(self.part.at[self.region(step, p, t, h)], dst, self.rs.at[step, p, k],
+                                   self.rr.at[step, p, k], self.at(axis, to))
+
+            first.append([go(far, 0, agg.at[p, 0], 0, up), go(far, 1, agg.at[p, 1], 1, down)])
+            second.append([go(up, 1, full.at[p, 0, ..., hi], 2, up), go(down, 0, full.at[p, 1, ..., lo], 3, down)])
+            last.append([go(up, 0, full.at[p, 0, ..., lo], 4, up), go(down, 1, full.at[p, 1, ..., hi], 5, down)])
         for p in range(3):
-            for c in first[p]:
-                c.start()
+            self.start(first[p])
         for p in range(3):
-            for c in second[p]:
-                c.start()
+            self.start(second[p])
+        self.steps[step] = (first, second, last)
+
+    def middle(self, step):
+        agg, _ = self.bufs[step]
+        first, _, last = self.steps[step]
         for p in range(3):
-            axis = ORDERS[p][step]
-            me = here[axis]
-            up, down = lax.rem(me + 1, 4), lax.rem(me + 3, 4)
+            _, up, down, _ = self.ways(step, p)
             first[p][0].wait_recv()
-            part[region(p, up, 0)] += agg[p, 0]
-            last[p][0].start()
+            self.part[self.region(step, p, up, 0)] += agg[p, 0]
+            self.start([last[p][0]])
             first[p][1].wait_recv()
-            part[region(p, down, 1)] += agg[p, 1]
-            last[p][1].start()
+            self.part[self.region(step, p, down, 1)] += agg[p, 1]
+            self.start([last[p][1]])
+
+    def end(self, step):
+        _, full = self.bufs[step]
+        _, second, last = self.steps[step]
         for p in range(3):
-            axis = ORDERS[p][step]
             for c in second[p] + last[p]:
                 c.wait_recv()
-            part[region(p, here[axis])] += full[p, 0] + full[p, 1]
-        for c in smalls:
+            here = self.region(step, p, self.here[ORDERS[p][step]])
+            self.part[here] += full[p, 0] + full[p, 1]
+
+    def small_pair_begin(self):
+        self.small_pair = self.start([
+            self.remote(self.small, self.slots_c.at[self.core], self.cs.at[2], self.cr.at[2], self.sibling)])
+        self.slots_c[self.core] = self.small[...]
+
+    def small_pair_end(self):
+        self.small_pair[0].wait_recv()
+        self.total[0] = self.slots_c[0] + self.slots_c[1]
+
+    def small_begin(self, k):
+        axis = (2, 1, 0)[k]
+        me = self.here[axis]
+        self.smalls = self.start([
+            self.remote(self.total.at[k], self.slots_a.at[k, me], self.ms.at[k, d - 1], self.mr.at[k, d - 1],
+                        self.at(axis, lax.rem(me + d, 4)))
+            for d in (1, 2, 3)])
+        self.slots_a[k, me] = self.total[k]
+
+    def small_end(self, k):
+        for c in self.smalls:
             c.wait_recv()
+        now = (self.slots_a[k, 0] + self.slots_a[k, 1]) + (self.slots_a[k, 2] + self.slots_a[k, 3])
+        if k < 2:
+            self.total[k + 1] = now
+        else:
+            self.small_out[...] = now
+
+    def share_begin(self):
+        z, y, x = self.here
+        self.out_ref[x] = self.part[z, y, x]
+        self.start([
+            self.remote(self.out_ref.at[x], self.out_ref.at[x], self.xs.at[d - 1], self.xr.at[d - 1],
+                        {"dp": lax.rem(x + d, 4)})
+            for d in (1, 2, 3)])
+
+    def share_end(self):
+        for d in (1, 2, 3):
+            came = lax.rem(self.xi + 4 - d, 4)
+            self.remote(self.out_ref.at[came], self.out_ref.at[came], self.xs.at[d - 1], self.xr.at[d - 1],
+                        {"dp": came}).wait_recv()
+
+    def finish(self):
+        for c in self.started:
             c.wait_send()
-        for p in range(3):
-            started += first[p] + second[p] + last[p]
-        total_now = (slots_a[step, 0] + slots_a[step, 1]) + (slots_a[step, 2] + slots_a[step, 3])
-        if step < 2:
-            total[...] = total_now
-        else:
-            small_out[...] = total_now
-
-    mine = part[zi, yi, xi]
-    out_ref[xi] = mine
-    spread = []
+
+
+def ring_scratch(rows, cols, span, lines):
+    f32 = jnp.float32
+    quarter, third, half = rows // 4, cols // 3, cols // 6
+    return [
+        pltpu.VMEM((4, 4, 4, quarter, cols), f32),
+        pltpu.VMEM((16, rows, span), f32),
+        pltpu.VMEM((span, cols), f32),
+        pltpu.VMEM((3, 2, 4, 4, quarter, half), f32),
+        pltpu.VMEM((3, 2, 4, 4, quarter, third), f32),
+        pltpu.VMEM((3, 2, 4, quarter, half), f32),
+        pltpu.VMEM((3, 2, 4, quarter, third), f32),
+        pltpu.VMEM((3, 2, quarter, half), f32),
+        pltpu.VMEM((3, 2, quarter, third), f32),
+        pltpu.VMEM((2, lines, 128), f32),
+        pltpu.VMEM((3, 4, lines, 128), f32),
+        pltpu.VMEM((3, lines, 128), f32),
+        pltpu.SemaphoreType.DMA((3,)),
+        pltpu.SemaphoreType.DMA((3,)),
+        pltpu.SemaphoreType.DMA((3, 3, 6)),
+        pltpu.SemaphoreType.DMA((3, 3, 6)),
+        pltpu.SemaphoreType.DMA((3,)),
+        pltpu.SemaphoreType.DMA((3,)),
+        pltpu.SemaphoreType.DMA((3, 3)),
+        pltpu.SemaphoreType.DMA((3, 3)),
+    ]
+
+
+BLOCK = 512
+
+
+def backward_kernel(n, sg_ref, thr_ref, spread_ref, nt_ref, og_ref, dy_ref, u_ref, x_ref, e_ref, f_ref, gt_hi, gt_lo,
+                    s_in_ref, s_end_ref, lanes_ref, b_ref, c_ref, mask_ref, keep_ref, open_ref, step_ref, sig_ref,
+                    rate_ref, gain_ref, w_out, small_out, dx_out, db_out, dc_out, dlogit_out, *scratch):
+    later, dfx, dg_acc, dc_acc, db_acc, a_acc, b_acc, skip_acc, end_acc, small = scratch[:10]
+    scan = make_scan(n, True, sg_ref, thr_ref, spread_ref, later, scratch[10 : 10 + SCAN_SCRATCH])
+    rest = scratch[10 + SCAN_SCRATCH :]
+    ring = Ring(nt_ref, og_ref, w_out, small, small_out, *rest[:12], rest[12:])
+    f32, bf16 = jnp.float32, jnp.bfloat16
+    span, width = x_ref.shape
+
+    barrier = pltpu.get_barrier_semaphore()
+    count = scan.greet(barrier)
     for d in (1, 2, 3):
-        c = remote(out_ref.at[xi], out_ref.at[xi], x_send.at[d - 1], x_recv.at[d - 1],
-                   {"dp": lax.rem(xi + d, 4)})
-        c.start()
-        spread.append(c)
-    for d in (1, 2, 3):
-        came = lax.rem(xi + 4 - d, 4)
-        remote(out_ref.at[came], out_ref.at[came], x_send.at[d - 1], x_recv.at[d - 1],
-               {"dp": came}).wait_recv()
-    for c in spread + copies + started:
-        c.wait_send()
-
-
-def reduce_weight(nt, og, small):
+        pl.semaphore_signal(barrier, inc=1, device_id={"dp": lax.rem(ring.xi + d, 4)}, device_id_type=MESH)
+    pl.semaphore_wait(barrier, count + 3)
+
+    def block(i):
+        return pl.ds(pl.multiple_of(i * BLOCK, BLOCK), BLOCK)
+
+    def pass_one(i, _):
+        at = block(i)
+        sp = spread_ref[:, at].astype(bf16)
+        dy, xb = dy_ref[:, at], x_ref[:, at].astype(f32)
+        du = dot2(split(e_ref[...]), sp, 1, 0) * dy
+        fx = (dot2(split(f_ref[...]), sp, 1, 0) * xb).astype(bf16)
+        du2 = split(du)
+        dfx[:, at] = dot2((gt_hi[...], gt_lo[...]), du2, 1, 0)
+        dg_acc[...] += dot2(du2, fx, 1, 1)
+        dc_acc[...] += dot2(du2, s_in_ref[:, at], 1, 1)
+        b_acc[...] += dot2(split(du * u_ref[:, at]), sp, 1, 1)
+        row = jnp.broadcast_to(jnp.sum(dy * xb, axis=0, keepdims=True), (8, BLOCK))
+        skip_acc[...] += dot2(split(row), sp, 1, 1)
+        return 0
+
+    def pass_two(i, _):
+        at = block(i)
+        sp = spread_ref[:, at].astype(bf16)
+        f = dot2(split(f_ref[...]), sp, 1, 0)
+        fx = f * x_ref[:, at].astype(f32)
+        late = later[:, at]
+        ds2 = split(lanes_ref[0:1, at] * late)
+        d = dfx[:, at] + dot2(b_ref[...] * keep_ref[...].astype(bf16), ds2, 1, 0)
+        dx_out[:, at] = (f * d + lanes_ref[1:2, at] * dy_ref[:, at]).astype(bf16)
+        a_acc[...] += dot2(split(fx * d), sp, 1, 1)
+        db_acc[...] += dot2(fx.astype(bf16), ds2, 1, 1)
+        row = jnp.broadcast_to(jnp.sum(late * s_end_ref[:, at], axis=0, keepdims=True), (8, BLOCK))
+        end_acc[...] += dot2(split(row), sp, 1, 1)
+        return 0
+
+    scan.begin()
+    ring.pair_begin()
+    scan.exchange()
+    ring.own()
+    scan.hops()
+    ring.theirs()
+    ring.begin(0)
+    for acc in (dg_acc, dc_acc, db_acc, a_acc, b_acc, skip_acc, end_acc):
+        acc[...] = jnp.zeros_like(acc)
+    lax.fori_loop(0, width // BLOCK, pass_one, 0)
+    scan.deliver()
+    ring.middle(0)
+    lax.fori_loop(0, width // BLOCK, pass_two, 0)
+
+    a = a_acc[...]
+    rows = lax.broadcasted_iota(jnp.int32, (span, span), 0)
+    cols = lax.broadcasted_iota(jnp.int32, (span, span), 1)
+    upper = jnp.where(rows <= cols, 1.0, 0.0).astype(f32)
+    d_decay = jnp.dot(upper, b_acc[...] - a, precision=HIGHEST, preferred_element_type=f32) + end_acc[0:1]
+    dlogit = (a / step_ref[...] - rate_ref[0:1] * d_decay) * sig_ref[...]
+    heads = dlogit_out.shape[1]
+    dlogit_out[...] = dlogit[:, :heads].astype(bf16)
+    small[...] = jnp.zeros_like(small)
+    lines = width // 128
+    small[0:lines] = gain_ref[...]
+    small[lines : lines + 1] = jnp.sum(dlogit, axis=0, keepdims=True)
+    small[lines + 1 : lines + 2] = jnp.sum(-step_ref[...] * d_decay, axis=0, keepdims=True)
+    small[lines + 2 : lines + 3] = skip_acc[0:1]
+    ring.small_pair_begin()
+    ring.end(0)
+    ring.begin(1)
+    ring.small_pair_end()
+    ring.small_begin(0)
+    dg = dg_acc[...] * mask_ref[...]
+    dc_out[...] = (dot2(split(dg), b_ref[...], 1, 0) + open_ref[...] * dc_acc[...]).astype(bf16)
+    db_out[...] = (dot2(split(dg.T), c_ref[...], 1, 0) + keep_ref[...] * db_acc[...]).astype(bf16)
+    ring.middle(1)
+    ring.small_end(0)
+    ring.small_begin(1)
+    ring.end(1)
+    ring.begin(2)
+    ring.small_end(1)
+    ring.small_begin(2)
+    ring.middle(2)
+    ring.end(2)
+    ring.share_begin()
+    ring.small_end(2)
+    ring.share_end()
+    ring.finish()
+    scan.finish()
+
+
+def backward(n, heads, sg, thr, spread, nt, og, dy, *rest):
+    f32, bf16 = jnp.float32, jnp.bfloat16
+    ns, width = sg.shape
+    span, cols = og.shape
     rows = nt.shape[2]
-    cols = og.shape[1]
-    quarter = rows // 4
-    third, half = cols // 3, cols // 6
+    lines = -(-(width // 128 + 3) // 8) * 8
     vmem = pl.BlockSpec(memory_space=pltpu.VMEM)
-    f32 = jnp.float32
-    out, sums = pl.pallas_call(
-        reduce_kernel,
-        out_shape=(jax.ShapeDtypeStruct((4, quarter, cols), f32), jax.ShapeDtypeStruct(small.shape, f32)),
-        in_specs=[vmem] * 3,
-        out_specs=(vmem, vmem),
+    wide = pltpu.VMEM((span, 128), f32)
+    out = pl.pallas_call(
+        functools.partial(backward_kernel, n),
+        out_shape=(
+            jax.ShapeDtypeStruct((4, rows // 4, cols), f32),
+            jax.ShapeDtypeStruct((lines, 128), f32),
+            jax.ShapeDtypeStruct((span, width), bf16),
+            jax.ShapeDtypeStruct((span, ns), bf16),
+            jax.ShapeDtypeStruct((span, ns), bf16),
+            jax.ShapeDtypeStruct((span, heads), bf16),
+        ),
+        in_specs=[vmem] * (6 + len(rest)),
+        out_specs=(vmem,) * 6,
         scratch_shapes=[
-            pltpu.VMEM((4, 4, 4, quarter, cols), f32),
-            pltpu.VMEM((16, rows, nt.shape[3]), f32),
-            pltpu.VMEM(og.shape, f32),
-            pltpu.VMEM((3, 2, 4, 4, quarter, half), f32),
-            pltpu.VMEM((3, 2, 4, 4, quarter, third), f32),
-            pltpu.VMEM((3, 2, 4, quarter, half), f32),
-            pltpu.VMEM((3, 2, 4, quarter, third), f32),
-            pltpu.VMEM((3, 2, quarter, half), f32),
-            pltpu.VMEM((3, 2, quarter, third), f32),
-            pltpu.VMEM((2, *small.shape), f32),
-            pltpu.VMEM((3, 4, *small.shape), f32),
-            pltpu.VMEM(small.shape, f32),
-            pltpu.SemaphoreType.DMA((3,)),
-            pltpu.SemaphoreType.DMA((3,)),
-            pltpu.SemaphoreType.DMA((3, 3, 6)),
-            pltpu.SemaphoreType.DMA((3, 3, 6)),
-            pltpu.SemaphoreType.DMA((3,)),
-            pltpu.SemaphoreType.DMA((3,)),
-            pltpu.SemaphoreType.DMA((3, 3)),
-            pltpu.SemaphoreType.DMA((3, 3)),
-        ],
+            pltpu.VMEM((ns, width), f32),
+            pltpu.VMEM((span, width), f32),
+            pltpu.VMEM((span, span), f32),
+            pltpu.VMEM((span, ns), f32),
+            pltpu.VMEM((span, ns), f32),
+            wide,
+            wide,
+            pltpu.VMEM((8, 128), f32),
+            pltpu.VMEM((8, 128), f32),
+            pltpu.VMEM((lines, 128), f32),
+        ] + scan_scratch(n, ns, width) + ring_scratch(rows, cols, span, lines),
         compiler_params=pltpu.CompilerParams(
-            collective_id=3, has_side_effects=True, vmem_limit_bytes=VMEM_LIMIT),
-        name="reduce_weight",
-    )(nt, og, small)
-    return out.reshape(rows, cols), sums
-
-
-def per_device(scan, reduce_all, ssm_input, gate_input, input_map, output_map, step_logit, step_bias,
+            collective_id=2, has_side_effects=True, vmem_limit_bytes=VMEM_LIMIT),
+        name="backward",
+    )(sg, thr, spread, nt, og, dy, *rest)
+    return out
+
+
+def per_device(scan, back, ssm_input, gate_input, input_map, output_map, step_logit, step_bias,
                decay_rate, skip_gain, norm_gain, out_weight, resets, out_grad):
     f32, bf16 = jnp.float32, jnp.bfloat16
     x, z, bmap, cmap, og = ssm_input[0], gate_input[0], input_map[0], output_map[0], out_grad[0]
@@ -496,7 +639,6 @@
         lax.broadcasted_iota(jnp.int32, (heads, width), 0)
         == lax.broadcasted_iota(jnp.int32, (heads, width), 1) // per_head
     ).astype(f32)
-    gather = spread.T
 
     raw = step_logit[0].astype(f32) + step_bias
     step = jax.nn.softplus(raw)
@@ -515,9 +657,9 @@
 
     xf = x.astype(f32)
     fx_f = f * xf
-    fx2 = split(fx_f)
+    fx2 = split_wide(fx_f)
     fx = fx2[0]
-    gm2 = split(jnp.where(mask, bdot(cmap, bmap, 1, 1), 0.0))
+    gm2 = split_wide(jnp.where(mask, bdot(cmap, bmap, 1, 1), 0.0))
     gm = gm2[0]
     b_keep = jnp.where(keep, bmap, jnp.zeros_like(bmap))
     c_open = jnp.where(opened, cmap, jnp.zeros_like(cmap))
@@ -525,7 +667,7 @@
     thr = jnp.zeros((8, 128), f32).at[:, :heads].set(jnp.broadcast_to(through, (8, heads)))
     spread_pad = jnp.zeros((128, width), f32).at[:heads].set(spread)
     incoming = scan(tail * s_own, thr, spread_pad, False)
-    s_in2 = split(lead * incoming)
+    s_in2 = split_wide(lead * incoming)
     s_in = s_in2[0]
 
     u = dot2(gm2, fx2, 1, 0) + dot2(c_open, s_in2, 1, 0)
@@ -545,54 +687,36 @@
     dy = dg * silu
     dz = (dg * y * (sig * (1.0 + zf * (1.0 - sig)))).astype(bf16)
     du_f = e * dy
-    du2 = split(du_f)
-    du = du2[0]
-    later = scan(lead * dot2(c_open, du2, 0, 0), thr, spread_pad, True)
-    ds_f = tail * later
-    ds2 = split(ds_f)
-    ds = ds2[0]
-
-    dfx = dot2(gm2, du2, 0, 0) + dot2(b_keep, ds2, 1, 0)
-    dx = (f * dfx + skip * dy).astype(bf16)
-    dgm2 = split(jnp.where(mask, dot2(du2, fx, 1, 1), 0.0))
-    dc = dot2(dgm2, bmap, 1, 0) + jnp.where(opened, dot2(du2, s_in, 1, 1), 0.0)
-    db = dot2(dgm2, cmap, 0, 0) + jnp.where(keep, dot2(fx, ds2, 1, 1), 0.0)
-    skip_row = jnp.sum(dy * xf, axis=0, keepdims=True)
-    end_row = jnp.sum(ds_f * s_own + through_wide * later * incoming, axis=0, keepdims=True)
-    a_wide = fx_f * dfx
-    per = exact(jnp.concatenate([a_wide, du_f * u - a_wide, skip_row, end_row], axis=0), gather)
-    a, ba = per[:rows], per[rows : 2 * rows]
-    skip_grad, end = per[2 * rows], per[2 * rows + 1 :]
-    d_decay = exact((ri <= ci).astype(f32), ba) + end
-    dlogit = (a / step - decay_rate * d_decay) * jax.nn.sigmoid(raw)
-    bias_grad = jnp.sum(dlogit, axis=0)
-    rate_grad = jnp.sum(-step * d_decay, axis=0)
-
-    small = jnp.concatenate([gain_grad, bias_grad, rate_grad, skip_grad])
-    size = small.shape[0]
-    lines = -(-size // 1024) * 8
-    small = jnp.pad(small, (0, lines * 128 - size)).reshape(lines, 128)
-    weight_grad, sums = reduce_all(normed, og, small)
-    sums = sums.reshape(-1)
-    gain_sum = sums[:width]
-    bias_sum, rate_sum, skip_sum = (sums[width + k * heads : width + (k + 1) * heads] for k in range(3))
+    du2 = split_wide(du_f)
+    sg = lead * dot2(c_open, du2, 0, 0)
+
+    def padded(values, fill=0.0):
+        return jnp.pad(values, ((0, 0), (0, 128 - heads)), constant_values=fill)
+
+    gt2 = split_wide(jnp.where((ri <= ci) & (count_col == count_row), bdot(bmap, cmap, 1, 1), 0.0))
+    nt = normed.T.astype(f32).reshape(16, 2, width // 32, rows)
+    s_end = through_wide * incoming + tail * s_own
+    lanes = jnp.concatenate([tail, skip, jnp.zeros((6, width), f32)], axis=0)
+    weight_grad, sums, dx, db, dc, dlogit = back(
+        heads, sg, thr, spread_pad, nt, og.astype(f32), dy, u, x, padded(e_head), padded(f_head), *gt2, s_in, s_end, lanes,
+        bmap, cmap, mask.astype(f32), keep.astype(f32), opened.astype(f32), padded(step, 1.0),
+        padded(jax.nn.sigmoid(raw)), jnp.broadcast_to(padded(decay_rate[None]), (8, 128)), gain_grad.reshape(-1, 128))
+    lines = width // 128
+    gain_sum = sums[:lines].reshape(-1)
+    bias_sum, rate_sum, skip_sum = (sums[lines + k, :heads] for k in range(3))
     return (
         mixed[None],
         dx[None],
         dz[None],
-        dc_cast(db)[None],
-        dc_cast(dc)[None],
-        dc_cast(dlogit)[None],
+        db[None],
+        dc[None],
+        dlogit[None],
         bias_sum,
         rate_sum,
         skip_sum,
         gain_sum,
-        weight_grad,
+        weight_grad.reshape(-1, weight_grad.shape[-1]),
     )
-
-
-def dc_cast(values):
-    return values.astype(jnp.bfloat16)
 
 
 def solution(mesh):
@@ -601,14 +725,12 @@
     def scan(state, thr, spread, reverse):
         return state_scan(n, state, thr, spread, reverse)
 
-    def reduce_all(normed, og, small):
-        rows, width = normed.shape
-        nt = normed.T.astype(jnp.float32).reshape(16, 2, width // 32, rows)
-        return reduce_weight(nt, og.astype(jnp.float32), small)
+    def back(heads, *operands):
+        return backward(n, heads, *operands)
 
     by_rows = P("dp", "seq", None)
     return jax.shard_map(
-        functools.partial(per_device, scan, reduce_all),
+        functools.partial(per_device, scan, back),
         mesh=mesh,
         in_specs=(by_rows,) * 5 + (P(),) * 5 + (P("dp", None), by_rows),
         out_specs=(by_rows,) * 6 + (P(),) * 4 + (P("seq", None),),

time: 250 us -> 223 us (0.89)
  matrix products: 62.8 us -> 36.3 us
  Pallas kernels: 146 us -> 132 us
  local copies, waits for them, and re-layouts: 18.1 us -> 25.9 us
  other arithmetic: 20.5 us -> 26.3 us
    pallas_call x2 -> x1, Pallas kernels: 75.2 us -> 34.2 us  [state_scan(): pl.pallas_call(functools.partial(scan_kernel, n, reverse), out_shape=jax....]
    pallas_call x1, Pallas kernels: 71.3 us -> 97.9 us  [backward(): pl.pallas_call(functools.partial(backward_kernel, n), out_shape=(jax.Shap...]
    dot_general x27 -> x13, matrix products: 52.3 us -> 32.6 us  [bdot(): lax.dot_general(a, b, (((ca,), (cb,)), ((), ())), preferred_element_type=...]
    reduce_sum x2 -> x0, other arithmetic: 6.89 us -> none  [the longest x1 3.98 us: per_device(): skip_row = jnp.sum(dy * xf, axis=0, keepdims=True)]
    dot_general x4 -> x2, matrix products: 10.5 us -> 3.73 us  [exact(): return jnp.dot(a, b, precision=HIGHEST, preferred_element_type=jnp.float32)]
    broadcast_in_dim x0 -> x1, other arithmetic: none -> 5.33 us  [per_device(): dz[None]]
    pad x0 -> x4, local copies, waits for them, and re-layouts: none -> 4.48 us  [padded(): return jnp.pad(values, ((0, 0), (0, 128 - heads)), constant_values=fill)]
    add x0 -> x1, other arithmetic: none -> 3.49 us  [per_device(): s_end = through_wide * incoming + tail * s_own]
where the time goes in v3:
time: 223 us; the launch traced here: 222 us
  Pallas kernels  132 us (59%)
  matrix products  36.3 us (16%)
  other arithmetic  26.3 us (12%)
  local copies, waits for them, and re-layouts  25.9 us (12%)
    pallas_call x1, Pallas kernels, backward(): pl.pallas_call(functools.partial(backward_kernel, n), out_shape=(jax.Shap...  97.9 us
    pallas_call x1, Pallas kernels, state_scan(): pl.pallas_call(functools.partial(scan_kernel, n, reverse), out_shape=jax....  34.2 us
    dot_general x13, matrix products, bdot(): lax.dot_general(a, b, (((ca,), (cb,)), ((), ())), preferred_element_type=...  32.6 us
    unnamed x72, local copies, waits for them, and re-layouts  7.41 us
    broadcast_in_dim x1, other arithmetic, per_device(): dz[None]  5.33 us
    reshape x1, local copies, waits for them, and re-layouts, per_device(): nt = normed.T.astype(f32).reshape(16, 2, width // 32, rows)  4.68 us
    pad x4, local copies, waits for them, and re-layouts, padded(): return jnp.pad(values, ((0, 0), (0, 128 - heads)), constant_values=fill)  4.48 us

profile of v3, /device:TPU:0, one launch (start us, length us, event | category | flops | bytes accessed | tf_op | source)
XLA Modules:
  0.0 222.3 jit_solution(13375967654666295092)
XLA Ops:
  0.6 1.4 fusion.67
  2.0 3.2 %fusion.50 = f32[]{:T(128)} fusion(s32[]{:T(128)} %bitcast.5, s32[]{:T(128)} %bitcast.4, s32[]{:T(128)} %bitcast.3, s32[]{:T(128)} %bitcast.2, s32[]{:T(128)S(6)} %mul.142), kind=kLoop, calls=%fused_computation.107 | loop fusion | flops 2559 | bytes 24 | tf_op jit(solution)/shard_map/reduce_sum | solution.py:633
  5.9 0.9 copy.69
  6.7 0.7 neg.13
  7.4 1.0 fusion.29
  8.4 0.6 compare_reduce_fusion
  9.0 0.8 select_reduce_fusion.2
  10.0 1.5 exponential_multiply_fusion
  11.6 0.7 copy.76
  12.5 2.7 %fusion.60 = f32[516,3072]{1,0:T(8,128)S(1)} fusion(f32[516,48]{0,1:T(8,128)S(1)} %concatenate.10, s32[3072]{0:T(1024)S(1)} %get-tuple-element.154, s32[3072]{0:T(1024)S(1)} %get-tuple-element.155, pred[3072]{0:T(1024)(128)(4,1)S(1)} %fusion.49), kind=kOutput, calls=%fused_computation.124 | convolution fusion | flops 913342464 | bytes 6467328 | tf_op jit(solution)/shard_map/dot_general | solution.py:42
  15.8 2.7 %compare_or_fusion = pred[256]{0:T(512)(128)(4,1)S(1)} fusion(s32[]{:T(128)} %bitcast.5, s32[]{:T(128)} %bitcast.4, s32[]{:T(128)} %bitcast.3, s32[]{:T(128)} %bitcast.2, s32[]{:T(128)S(6)} %mul.142), kind=kLoop, calls=%fused_computation.105 | loop fusion | flops 2048 | bytes 276 | tf_op jit(solution)/shard_map/or | solution.py:630
  18.7 1.2 fusion.63
  20.5 2.0 fusion.2.s_ref
  22.5 0.6 scatter.15.thr_ref
  23.2 1.3 pad_convert_fusion.spread_ref
  24.5 34.2 %scan_ahead.1 = f32[128,3072]{1,0:T(8,128)} custom-call(f32[128,3072]{1,0:T(8,128)} %fusion.2.s_ref, f32[8,128]{1,0:T(8,128)} %scatter.15.thr_ref, f32[128,3072]{1,0:T(8,128)} %pad_convert_fusion.spread_ref), custom_call_target="tpu_custom_call" | custom-call | tf_op jit(solution)/shard_map/scan_ahead/pallas_call | solution.py:259
  58.7 3.5 %multiply_add_fusion = (f32[128,3072]{1,0:T(8,128)}, bf16[128,3072]{1,0:T(8,128)(2,1)S(1)}) fusion(f32[128,3072]{1,0:T(8,128)} %fusion.2.s_ref, f32[128,3072]{1,0:T(8,128)} %scan_ahead.1, f32[3072]{0:T(1024)S(1)} %bitcast.122, f32[3072]{0:T(1024)S(1)} %bitcast.116), kind=kLoop, calls=%fused_computation.40 | loop fusion | flops 1966080 | bytes 5529600 | tf_op jit(solution)/shard_map/add | solution.py:698
  62.2 0.6 fusion.59
  63.3 0.6 fusion.45
  64.1 0.7 fusion.44
  64.9 0.7 fusion.1
  65.5 0.7 copy-done.6
  66.7 3.6 %multiply_reduce_fusion.2 = (f32[256]{0:T(256)S(1)}, f32[256,3072]{1,0:T(8,128)}, f32[256,3072]{1,0:T(8,128)S(1)}) fusion(bf16[1,256,3072]{2,1,0:T(8,128)(2,1)S(1)} %copy-done.9, bf16[1,256,3072]{2,1,0:T(8,128)(2,1)S(1)} %copy-done.2, f32[3072]{0:T(1024)S(1)} %bitcast.113, f32[516,3072]{1,0:T(8,128)S(1)} %bitcast.106, f32[256,3072]{1,0:T(8,128)S(1)} %fusion.1, ...), kind=kOutput, calls=%fused_computation.32 | convolution fusion | flops 213942016 | bytes 20538624 | tf_op jit(solution)/shard_map/dot_general | solution.py:16
  70.4 9.2 %multiply_reduce_fusion = (f32[3072]{0:T(1024)}, f32[256]{0:T(256)S(1)}, f32[256,3072]{1,0:T(8,128)S(1)}) fusion(f32[256,3072]{1,0:T(8,128)} %get-tuple-element.122, f32[256]{0:T(256)S(1)} %add_rsqrt_fusion, f32[3072]{0:T(1024)S(1)} %copy-done.21, bf16[3072,1536]{1,0:T(8,128)(2,1)} %param.25, bf16[1,256,1536]{2,1,0:T(8,128)(2,1)S(1)} %copy-done.12), kind=kOutput, calls=%fused_computation.28 | convolution fusion | flops 2420634368 | bytes 16541696 | tf_op jit(solution)/shard_map/dot_general | solution.py:16
  79.6 5.3 %fusion.19 = (bf16[1,256,3072]{2,1,0:T(8,128)(2,1)}, f32[256,3072]{1,0:T(8,128)S(1)}, f32[3072,256]{0,1:T(8,128)}) fusion(bf16[1,256,3072]{2,1,0:T(8,128)(2,1)} %param.17, f32[256]{0:T(256)S(1)} %broadcast_multiply_fusion, f32[256,3072]{1,0:T(8,128)S(1)} %copy-done.7, f32[256,3072]{1,0:T(8,128)S(1)} %get-tuple-element.153, f32[3072]{0:T(1024)S(1)} %copy-done.22, ...), kind=kLoop, calls=%fused_computation.43 | loop fusion | flops 19660800 | bytes 23619584 | tf_op jit(solution)/shard_map/broadcast_in_dim | solution.py:710
  85.0 4.7 %copy.77 = f32[3072,256]{1,0:T(8,128)} copy(f32[3072,256]{0,1:T(8,128)} %get-tuple-element.131) | data formatting | bytes 6291456 | tf_op jit(solution)/shard_map/reshape | solution.py:697
  89.6 2.5 %fusion.17 = f32[128,3072]{1,0:T(8,128)S(1)} fusion(f32[256,3072]{1,0:T(8,128)S(1)} %get-tuple-element.126.dy_ref, f32[516,3072]{1,0:T(8,128)} %copy-done, pred[256]{0:T(512)(128)(4,1)} %copy-done.24, bf16[1,256,128]{2,1,0:T(8,128)(2,1)S(1)} %copy-done.11), kind=kOutput, calls=%fused_computation.39 | convolution fusion | flops 203718656 | bytes 7930368 | tf_op jit(solution)/shard_map/dot_general | solution.py:16
  92.2 3.8 %fusion.3.sg_ref = f32[128,3072]{1,0:T(8,128)} fusion(f32[128,3072]{1,0:T(8,128)S(1)} %fusion.17, f32[256,3072]{1,0:T(8,128)S(1)} %get-tuple-element.126.dy_ref, f32[516,3072]{1,0:T(8,128)} %copy-done, f32[3072]{0:T(1024)S(1)} %bitcast.118, pred[256]{0:T(512)(128)(4,1)S(1)} %copy-done.25, bf16[1,256,128]{2,1,0:T(8,128)(2,1)S(1)} %copy-done.11), kind=kOutput, calls=%fused_computation.16 | convolution fusion | flops 205291520 | bytes 9515264 | tf_op jit(solution)/shard_map/dot_general | solution.py:16
  96.0 0.7 maximum_maximum_fusion.lanes_ref
  96.7 0.9 fusion.26
  97.7 1.5 copy.78.keep_ref
  99.1 1.5 copy.79.open_ref
  100.6 1.5 fusion.30.mask_ref
  102.1 0.7 pad.24.e_ref
  102.8 0.7 pad.25.f_ref
  103.4 1.6 pad.26.step_ref
  105.0 1.6 pad.27.sig_ref
  106.6 2.5 %bitcast_convert_fusion.og_ref = f32[256,1536]{1,0:T(8,128)} fusion(bf16[1,256,1536]{2,1,0:T(8,128)(2,1)} %param.27), kind=kLoop, calls=%fused_computation.47 | loop fusion | flops 393216 | bytes 2359296 | tf_op jit(solution)/shard_map/convert_element_type | solution.py:701
  109.0 0.6 broadcast_in_dim.87.rate_ref
  109.6 97.9 %backward.1 = (f32[4,24,1536]{2,1,0:T(8,128)}, f32[32,128]{1,0:T(8,128)}, bf16[256,3072]{1,0:T(8,128)(2,1)}, bf16[256,128]{1,0:T(8,128)(2,1)}, bf16[256,128]{1,0:T(8,128)(2,1)}, /*index=5*/bf16[256,48]{1,0:T(8,128)(2,1)}) custom-call(f32[128,3072]{1,0:T(8,128)} %fusion.3.sg_ref, f32[8,128]{1,0:T(8,128)} %scatter.15.thr_ref, ...), custom_call_target="tpu_custom_call" | custom-call | tf_op jit(solution)/shard_map/backward/pallas_call | solution.py:580
  207.5 1.5 copy.80
  209.0 1.3 slice_bitcast_fusion
  210.3 1.3 slice_bitcast_fusion.1
  211.7 7.3 %fusion.14 = bf16[1,256,1536]{2,1,0:T(8,128)(2,1)} fusion(bf16[3072,1536]{1,0:T(8,128)(2,1)} %param.25, f32[256,3072]{1,0:T(8,128)S(1)} %copy-done.8, f32[3072]{0:T(1024)S(1)} %copy-done.23, f32[256]{0:T(256)S(1)} %copy-done.29), kind=kOutput, calls=%fused_computation.35 | convolution fusion | flops 2418671616 | bytes 13382656 | tf_op jit(solution)/shard_map/dot_general | solution.py:16
  219.0 1.1 copy.85
  220.2 0.6 copy.86
  220.8 0.6 copy.87
  221.4 0.8 copy.88
  (84 shorter events, 3.0 us)
Async XLA Ops:
  12.5 2.8 %copy-start.2 = (bf16[1,256,3072]{2,1,0:T(8,128)(2,1)S(1)}, bf16[1,256,3072]{2,1,0:T(8,128)(2,1)}, u32[]{:S(2)}) copy-start(bf16[1,256,3072]{2,1,0:T(8,128)(2,1)} %param.16) | copy-start | bytes 4718596
  15.3 5.2 %copy-start = (f32[516,3072]{1,0:T(8,128)}, f32[516,3072]{1,0:T(8,128)S(1)}, u32[]{:S(2)}) copy-start(f32[516,3072]{1,0:T(8,128)S(1)} %fusion.60) | copy-start | bytes 19021828
  15.3 4.7 %copy-start.13 = (bf16[1,256,128]{2,1,0:T(8,128)(2,1)S(1)}, bf16[1,256,128]{2,1,0:T(8,128)(2,1)}, u32[]{:S(2)}) copy-start(bf16[1,256,128]{2,1,0:T(8,128)(2,1)} %param.18) | copy-start | bytes 196612
  18.7 44.2 %copy-start.26 = (f32[256]{0:T(256)}, f32[256]{0:T(256)S(1)}, u32[]{:S(2)}) copy-start(f32[256]{0:T(256)S(1)} %get-tuple-element.116) | copy-start | bytes 3076
  19.9 45.6 %copy-start.24 = (pred[256]{0:T(512)(128)(4,1)}, pred[256]{0:T(512)(128)(4,1)S(1)}, u32[]{:S(2)}) copy-start(pred[256]{0:T(512)(128)(4,1)S(1)} %get-tuple-element.118) | copy-start | bytes 772
  20.5 2.1 copy-start.15
  20.5 45.1 %copy-start.17 = (f32[1,3072]{1,0:T(1,128)}, f32[1,3072]{1,0:T(1,128)S(1)}, u32[]{:S(2)}) copy-start(f32[1,3072]{1,0:T(1,128)S(1)} %get-tuple-element.130) | copy-start | bytes 36868
  58.7 3.5 %copy-start.11 = (bf16[1,256,128]{2,1,0:T(8,128)(2,1)S(1)}, bf16[1,256,128]{2,1,0:T(8,128)(2,1)}, u32[]{:S(2)}) copy-start(bf16[1,256,128]{2,1,0:T(8,128)(2,1)} %param.19) | copy-start | bytes 196612
  58.7 5.2 %slice-start = ((s8[6389760]{0:T(1024)(128)(4,1)}), s8[4194304]{0:T(1024)(128)(4,1)S(1)}, s32[]{:S(2)}) async-start(s8[6389760]{0:T(1024)(128)(4,1)} %bitcast.105), calls=%async_computation | async-start | bytes 8388608
  62.2 0.9 copy-start.5
  62.2 1.9 slice-start.1
  64.8 1.4 copy-start.6
  64.8 1.9 copy-start.9
  66.7 3.7 %copy-start.12 = (bf16[1,256,1536]{2,1,0:T(8,128)(2,1)S(1)}, bf16[1,256,1536]{2,1,0:T(8,128)(2,1)}, u32[]{:S(2)}) copy-start(bf16[1,256,1536]{2,1,0:T(8,128)(2,1)} %param.27) | copy-start | bytes 2359300
  66.7 3.7 %copy-start.21 = (f32[3072]{0:T(1024)S(1)}, f32[3072]{0:T(1024)}, u32[]{:S(2)}) copy-start(f32[3072]{0:T(1024)} %param.24) | copy-start | bytes 36868
  70.4 9.2 %copy-start.4 = (f32[256,3072]{1,0:T(8,128)}, f32[256,3072]{1,0:T(8,128)S(1)}, u32[]{:S(2)}) copy-start(f32[256,3072]{1,0:T(8,128)S(1)} %get-tuple-element.152.u_ref) | copy-start | bytes 9437188
  70.4 9.2 %copy-start.28 = (f32[256]{0:T(256)}, f32[256]{0:T(256)S(1)}, u32[]{:S(2)}) copy-start(f32[256]{0:T(256)S(1)} %add_rsqrt_fusion) | copy-start | bytes 3076
  70.4 9.2 %copy-start.3 = (bf16[1,256,3072]{2,1,0:T(8,128)(2,1)S(1)}, bf16[1,256,3072]{2,1,0:T(8,128)(2,1)}, u32[]{:S(2)}) copy-start(bf16[1,256,3072]{2,1,0:T(8,128)(2,1)} %param.16) | copy-start | bytes 4718596
  70.4 9.2 %copy-start.7 = (f32[256,3072]{1,0:T(8,128)S(1)}, f32[256,3072]{1,0:T(8,128)}, u32[]{:S(2)}) copy-start(f32[256,3072]{1,0:T(8,128)} %get-tuple-element.122) | copy-start | bytes 9437188
  70.4 9.2 %copy-start.22 = (f32[3072]{0:T(1024)S(1)}, f32[3072]{0:T(1024)}, u32[]{:S(2)}) copy-start(f32[3072]{0:T(1024)} %param.24) | copy-start | bytes 36868
  85.0 7.2 %copy-start.1 = (f32[256,3072]{1,0:T(8,128)}, f32[256,3072]{1,0:T(8,128)S(1)}, u32[]{:S(2)}) copy-start(f32[256,3072]{1,0:T(8,128)S(1)} %get-tuple-element.126.dy_ref) | copy-start | bytes 9437188
  89.6 2.5 %copy-start.18 = (f32[1,3072]{1,0:T(1,128)S(1)}, f32[1,3072]{1,0:T(1,128)}, u32[]{:S(2)}) copy-start(f32[1,3072]{1,0:T(1,128)} %copy-done.17) | copy-start | bytes 36868
  89.6 2.5 %copy-start.25 = (pred[256]{0:T(512)(128)(4,1)S(1)}, pred[256]{0:T(512)(128)(4,1)}, u32[]{:S(2)}) copy-start(pred[256]{0:T(512)(128)(4,1)} %copy-done.24) | copy-start | bytes 772
  92.1 3.9 %copy-start.16 = (f32[1,3072]{1,0:T(1,128)S(1)}, f32[1,3072]{1,0:T(1,128)}, u32[]{:S(2)}) copy-start(f32[1,3072]{1,0:T(1,128)} %copy-done.15) | copy-start | bytes 36868
  92.2 4.6 %copy-start.27 = (f32[256]{0:T(256)S(1)}, f32[256]{0:T(256)}, u32[]{:S(2)}) copy-start(f32[256]{0:T(256)} %copy-done.26) | copy-start | bytes 3076
  95.9 13.1 %copy-start.30 = (f32[48]{0:T(128)S(1)}, f32[48]{0:T(128)}, u32[]{:S(2)}) copy-start(f32[48]{0:T(128)} %param.22) | copy-start | bytes 580
  109.6 102.0 %copy-start.8 = (f32[256,3072]{1,0:T(8,128)S(1)}, f32[256,3072]{1,0:T(8,128)}, u32[]{:S(2)}) copy-start(f32[256,3072]{1,0:T(8,128)} %get-tuple-element.122) | copy-start | bytes 9437188
  109.6 102.0 %copy-start.23 = (f32[3072]{0:T(1024)S(1)}, f32[3072]{0:T(1024)}, u32[]{:S(2)}) copy-start(f32[3072]{0:T(1024)} %param.24) | copy-start | bytes 36868
  109.6 102.0 %copy-start.29 = (f32[256]{0:T(256)S(1)}, f32[256]{0:T(256)}, u32[]{:S(2)}) copy-start(f32[256]{0:T(256)} %copy-done.28) | copy-start | bytes 3076
  211.7 7.3 %copy-start.10 = (bf16[256,3072]{1,0:T(8,128)(2,1)S(1)}, bf16[256,3072]{1,0:T(8,128)(2,1)}, u32[]{:S(2)}) copy-start(bf16[256,3072]{1,0:T(8,128)(2,1)} %get-tuple-element.41) | copy-start | bytes 4718596
  219.0 1.2 copy-start.20
  219.0 1.8 copy-start.19
  219.0 2.4 %copy-start.14 = (f32[4,24,1536]{2,1,0:T(8,128)S(1)}, f32[4,24,1536]{2,1,0:T(8,128)}, u32[]{:S(2)}) copy-start(f32[4,24,1536]{2,1,0:T(8,128)} %get-tuple-element.46) | copy-start | bytes 1769476

commit v4 on v3

--- a/solution.py
+++ b/solution.py
@@ -9,18 +9,13 @@
 
 MESH = pl.DeviceIdType.MESH
 HIGHEST = lax.Precision.HIGHEST
-VMEM_LIMIT = 60 * 1024 * 1024
+VMEM_LIMIT = 63 * 1024 * 1024
 
 
 def bdot(a, b, ca, cb):
     return lax.dot_general(
         a, b, (((ca,), (cb,)), ((), ())), preferred_element_type=jnp.float32
     )
-
-
-def split_wide(v):
-    hi = lax.reduce_precision(v, exponent_bits=8, mantissa_bits=7)
-    return hi.astype(jnp.bfloat16), (v - hi).astype(jnp.bfloat16)
 
 
 def split(v):
@@ -36,10 +31,6 @@
     if isinstance(b, tuple):
         return bdot(a, b[0], ca, cb) + bdot(a, b[1], ca, cb)
     return bdot(a, b, ca, cb)
-
-
-def exact(a, b):
-    return jnp.dot(a, b, precision=HIGHEST, preferred_element_type=jnp.float32)
 
 
 class Scan:
@@ -127,7 +118,7 @@
 
         lax.fori_loop(0, self.chips - 1, tell, 0)
         both = jnp.concatenate([thr_first, thr_second], axis=0)
-        wide = jnp.dot(both, self.spread_ref[:, self.lanes(self.core)], precision=HIGHEST,
+        wide = jnp.dot(both, self.spread_ref[:, self.lanes(self.core)].astype(jnp.float32), precision=HIGHEST,
                        preferred_element_type=jnp.float32)
         self.first_wide[...] = wide[0:8]
         second_wide = wide[8:16]
@@ -156,7 +147,7 @@
             return 0
 
         lax.fori_loop(0, self.chips - 1, arrive, 0)
-        self.thr_wide[...] = jnp.dot(self.thr_buf[:, 0, :], self.spread_ref[:, self.lanes(self.core)],
+        self.thr_wide[...] = jnp.dot(self.thr_buf[:, 0, :], self.spread_ref[:, self.lanes(self.core)].astype(jnp.float32),
                                      precision=HIGHEST, preferred_element_type=jnp.float32)
 
         def hop(i, state):
@@ -226,7 +217,8 @@
     chips = n // 2
     chunk = pltpu.VMEM((chips, ns // chips, width // 2), jnp.float32)
     tile = pltpu.VMEM((8, 128), jnp.float32)
-    return [chunk] * 6 + [
+    return [chunk] * 3 + [
+        tile,
         tile,
         tile,
         pltpu.VMEM((chips, 8, 128), jnp.float32),
@@ -235,53 +227,30 @@
     ] + [pltpu.SemaphoreType.DMA((chips,))] * 10 + [pltpu.SemaphoreType.DMA] * 2
 
 
-SCAN_SCRATCH = 11 + 12
-
-
-def make_scan(n, reverse, s_ref, thr_ref, spread_ref, out_ref, scratch):
-    return Scan(n, reverse, s_ref, thr_ref, spread_ref, out_ref, *scratch[:11], scratch[11:])
-
-
-def scan_kernel(n, reverse, s_ref, thr_ref, spread_ref, out_ref, *scratch):
-    scan = make_scan(n, reverse, s_ref, thr_ref, spread_ref, out_ref, scratch)
-    barrier = pltpu.get_barrier_semaphore()
-    pl.semaphore_wait(barrier, scan.greet(barrier))
-    scan.begin()
-    scan.exchange()
-    scan.hops()
-    scan.deliver()
-    scan.finish()
-
-
-def state_scan(n, state, thr, spread, reverse):
-    ns, width = state.shape
-    vmem = pl.BlockSpec(memory_space=pltpu.VMEM)
-    return pl.pallas_call(
-        functools.partial(scan_kernel, n, reverse),
-        out_shape=jax.ShapeDtypeStruct((ns, width), jnp.float32),
-        in_specs=[vmem] * 3,
-        out_specs=vmem,
-        scratch_shapes=scan_scratch(n, ns, width),
-        compiler_params=pltpu.CompilerParams(
-            collective_id=2 if reverse else 1, has_side_effects=True,
-            vmem_limit_bytes=VMEM_LIMIT),
-        name="scan_back" if reverse else "scan_ahead",
-    )(state, thr, spread)
+SCAN_SCRATCH = 9 + 12
+
+
+def make_scan(n, reverse, s_ref, spread_ref, out_ref, shared, scratch):
+    mine, stage, give = shared
+    pair, recv, back, thr_ref = scratch[:4]
+    return Scan(n, reverse, s_ref, thr_ref, spread_ref, out_ref, pair, mine, recv, stage, back, give,
+                *scratch[4:9], scratch[9:])
 
 
 ORDERS = ((2, 1, 0), (1, 0, 2), (0, 2, 1))
 
 
 class Ring:
-    def __init__(self, nt_ref, og_ref, out_ref, small, small_out, part, nt_got, og_got, agg1, full1, agg2, full2,
+    def __init__(self, og_ref, og_wide, nt_own, nt_send, out_ref, small, small_out, part, nt_got, og_got, agg1, full1, agg2, full2,
                  agg3, full3, slots_c, slots_a, total, sems):
-        (self.cs, self.cr, self.rs, self.rr, self.xs, self.xr, self.ms, self.mr) = sems
+        (self.cs, self.cr, self.ns, self.nr, self.rs, self.rr, self.xs, self.xr, self.ms, self.mr) = sems
         self.xi = lax.axis_index("dp")
         s = lax.axis_index("seq")
         self.core = lax.rem(s, 2)
         self.here = (lax.div(s, 8), lax.rem(lax.div(s, 2), 4), self.xi)
         self.sibling = {"seq": s + 1 - 2 * self.core}
-        self.nt_ref, self.og_ref, self.out_ref = nt_ref, og_ref, out_ref
+        self.og_ref, self.og_wide, self.nt_own, self.nt_send = og_ref, og_wide, nt_own, nt_send
+        self.out_ref = out_ref
         self.small, self.small_out = small, small_out
         self.part, self.nt_got, self.og_got = part, nt_got, og_got
         self.bufs = ((agg1, full1), (agg2, full2), (agg3, full3))
@@ -307,27 +276,32 @@
         self.started += copies
         return copies
 
-    def pair_begin(self):
-        self.pair = self.start([
-            self.remote(self.og_ref, self.og_got, self.cs.at[0], self.cr.at[0], self.sibling),
-            self.remote(self.nt_ref.at[:, 1 - self.core], self.nt_got, self.cs.at[1], self.cr.at[1], self.sibling),
-        ])
+    def og_begin(self):
+        self.og_wide[...] = self.og_ref[...].astype(jnp.float32)
+        self.og_copy = self.remote(self.og_wide, self.og_got, self.cs.at[0], self.cr.at[0], self.sibling)
+        self.og_copy.start()
+
+    def nt_copy(self, i, count):
+        here = pl.ds(i * count, count)
+        return self.remote(self.nt_send.at[here], self.nt_got.at[here], self.ns.at[i], self.nr.at[i], self.sibling)
 
     def own(self):
-        og = self.og_ref[...].astype(jnp.bfloat16)
-
         def one(b, _):
             z, y = lax.div(b, 4), lax.rem(b, 4)
-            lhs = self.nt_ref[b, self.core].astype(jnp.bfloat16)
-            self.part[z, y] = bdot(lhs, og, 1, 0).reshape(self.part.shape[2:])
+            self.part[z, y] = bdot(self.nt_own[b], self.og_ref[...], 1, 0).reshape(self.part.shape[2:])
             return 0
 
         lax.fori_loop(0, 16, one, 0)
 
-    def theirs(self):
-        for c in self.pair:
-            c.wait_recv()
+    def theirs(self, parts):
+        self.og_copy.wait_recv()
         og = self.og_got[...].astype(jnp.bfloat16)
+
+        def got(i, _):
+            self.nt_copy(i, 16 // parts).wait_recv()
+            return 0
+
+        lax.fori_loop(0, parts, got, 0)
 
         def one(b, _):
             z, y = lax.div(b, 4), lax.rem(b, 4)
@@ -456,6 +430,8 @@
         pltpu.VMEM((3, lines, 128), f32),
         pltpu.SemaphoreType.DMA((3,)),
         pltpu.SemaphoreType.DMA((3,)),
+        pltpu.SemaphoreType.DMA((8,)),
+        pltpu.SemaphoreType.DMA((8,)),
         pltpu.SemaphoreType.DMA((3, 3, 6)),
         pltpu.SemaphoreType.DMA((3, 3, 6)),
         pltpu.SemaphoreType.DMA((3,)),
@@ -465,94 +441,246 @@
     ]
 
 
-BLOCK = 512
-
-
-def backward_kernel(n, sg_ref, thr_ref, spread_ref, nt_ref, og_ref, dy_ref, u_ref, x_ref, e_ref, f_ref, gt_hi, gt_lo,
-                    s_in_ref, s_end_ref, lanes_ref, b_ref, c_ref, mask_ref, keep_ref, open_ref, step_ref, sig_ref,
-                    rate_ref, gain_ref, w_out, small_out, dx_out, db_out, dc_out, dlogit_out, *scratch):
-    later, dfx, dg_acc, dc_acc, db_acc, a_acc, b_acc, skip_acc, end_acc, small = scratch[:10]
-    scan = make_scan(n, True, sg_ref, thr_ref, spread_ref, later, scratch[10 : 10 + SCAN_SCRATCH])
-    rest = scratch[10 + SCAN_SCRATCH :]
-    ring = Ring(nt_ref, og_ref, w_out, small, small_out, *rest[:12], rest[12:])
+BLOCK = 384
+TAIL, LEAD, SKIP, THROUGH = range(4)
+
+
+def softplus(v):
+    return jnp.maximum(v, 0.0) + jnp.log1p(jnp.exp(-jnp.abs(v)))
+
+
+def mixer_kernel(n, x_ref, z_ref, b_ref, c_ref, logit_ref, og_ref, par_ref, gain_ref, resets_ref, w_hbm,
+                 w_out, small_out, dx_out, dz_out, db_out, dc_out, dlogit_out, mixed_out, *scratch):
+    (dn, u, normed, s_buf, inc, sg, s_in, spread, lanes, w_buf, gm_hi, gm_lo, gt_hi, gt_lo, mask_ref, bk, bkt, co, cot,
+     e_ref, f_ref, step_ref, sig_ref, keep_ref, open_ref, ms_acc, m2_acc, dg_acc, dc_acc, db_acc, a_acc, b_acc,
+     skip_acc, end_acc, small, nt_own, nt_send, og_wide, mine, stage, give, w_sem) = scratch[:42]
+    rest = scratch[42:]
+    ahead = make_scan(n, False, s_buf, spread, inc, (mine, stage, give), rest[:SCAN_SCRATCH])
+    behind = make_scan(n, True, sg, spread, inc, (mine, stage, give), rest[SCAN_SCRATCH : 2 * SCAN_SCRATCH])
+    rest = rest[2 * SCAN_SCRATCH :]
+    ring = Ring(og_ref, og_wide, nt_own, nt_send, w_out, small, small_out, *rest[:12], rest[12:])
     f32, bf16 = jnp.float32, jnp.bfloat16
     span, width = x_ref.shape
+    blocks = width // BLOCK
+
+    def w_copy(i):
+        slot = lax.rem(i, 2)
+        return pltpu.make_async_copy(w_hbm.at[pl.ds(i * BLOCK, BLOCK)], w_buf.at[slot], w_sem.at[slot])
 
     barrier = pltpu.get_barrier_semaphore()
-    count = scan.greet(barrier)
+    count = ahead.greet(barrier)
     for d in (1, 2, 3):
         pl.semaphore_signal(barrier, inc=1, device_id={"dp": lax.rem(ring.xi + d, 4)}, device_id_type=MESH)
-    pl.semaphore_wait(barrier, count + 3)
+    w_copy(0).start()
+
+    start = lax.axis_index("seq") * span
+    ri = lax.broadcasted_iota(jnp.int32, (span, span), 0)
+    ci = lax.broadcasted_iota(jnp.int32, (span, span), 1)
+    flag_c = jnp.zeros((span, span), f32)
+    flag_r = jnp.zeros((span, span), f32)
+    for k in range(resets_ref.shape[0]):
+        at_reset = resets_ref[k, 0:1, :] - start
+        flag_c = jnp.where(ci == at_reset, 1.0, flag_c)
+        flag_r = jnp.where(ri == at_reset, 1.0, flag_r)
+    count_col = jnp.sum(jnp.where(ri >= ci, flag_c, 0.0), axis=1, keepdims=True)
+    count_row = jnp.sum(jnp.where(ri <= ci, flag_r, 0.0), axis=0, keepdims=True)
+    all_col = jnp.sum(flag_c, axis=1, keepdims=True)
+    all_row = jnp.sum(flag_r, axis=0, keepdims=True)
+    below = jnp.where(ri >= ci, 1.0, 0.0)
+    mask = jnp.where((ri >= ci) & (count_col == count_row), 1.0, 0.0)
+    mask_ref[...] = mask
+    keep = jnp.where(count_col == all_col, 1.0, 0.0)
+    opened = jnp.where(count_col == 0.0, 1.0, 0.0)
+    keep_ref[...] = jnp.broadcast_to(keep, keep_ref.shape)
+    open_ref[...] = jnp.broadcast_to(opened, open_ref.shape)
+    b_keep = b_ref[...].astype(f32) * keep
+    c_open = c_ref[...].astype(f32) * opened
+    bk[...] = b_keep.astype(bf16)
+    bkt[...] = b_keep.T.astype(bf16)
+    co[...] = c_open.astype(bf16)
+    cot[...] = c_open.T.astype(bf16)
+    gm = bdot(c_ref[...], b_ref[...], 1, 1) * mask
+    gm_hi[...], gm_lo[...] = split(gm)
+    gt_hi[...], gt_lo[...] = split(gm.T)
+    raw = logit_ref[...].astype(f32) + par_ref[0:1]
+    step = softplus(raw)
+    step_ref[...] = step
+    sig_ref[...] = jax.nn.sigmoid(raw)
+    cum = jnp.dot(below, -par_ref[1:2] * step, precision=HIGHEST, preferred_element_type=f32)
+    last = cum[span - 1 : span]
+    mid = cum[span // 2 : span // 2 + 1]
+    through = jnp.where(all_row[:, :128] == 0.0, jnp.exp(last), 0.0)
+    e_ref[...] = jnp.exp(cum - mid)
+    f_ref[...] = step * jnp.exp(mid - cum)
+    thr = jnp.broadcast_to(through, (8, 128))
+    ahead.thr_ref[...] = thr
+    behind.thr_ref[...] = thr
+    head_of = lax.broadcasted_iota(jnp.int32, spread.shape, 1) >> 6
+    spread[...] = jnp.where(lax.broadcasted_iota(jnp.int32, spread.shape, 0) == head_of, 1.0, 0.0).astype(bf16)
+    per_head = jnp.concatenate(
+        [jnp.exp(last - mid), jnp.exp(mid), par_ref[2:3], through, jnp.zeros((4, 128), f32)], axis=0)
+    lanes[...] = jnp.dot(per_head, spread[...].astype(f32), precision=HIGHEST, preferred_element_type=f32)
+    for acc in (ms_acc, m2_acc, dg_acc, dc_acc, db_acc, a_acc, b_acc, skip_acc, end_acc, small):
+        acc[...] = jnp.zeros_like(acc)
 
     def block(i):
-        return pl.ds(pl.multiple_of(i * BLOCK, BLOCK), BLOCK)
-
-    def pass_one(i, _):
-        at = block(i)
-        sp = spread_ref[:, at].astype(bf16)
-        dy, xb = dy_ref[:, at], x_ref[:, at].astype(f32)
-        du = dot2(split(e_ref[...]), sp, 1, 0) * dy
-        fx = (dot2(split(f_ref[...]), sp, 1, 0) * xb).astype(bf16)
+        return pl.ds(pl.multiple_of(i * BLOCK, 128), BLOCK)
+
+    def every(body):
+        def one(i, _):
+            body(i, block(i))
+            return 0
+
+        lax.fori_loop(0, blocks, one, 0)
+
+    def e_of(at):
+        return dot2(split(e_ref[...]), spread[:, at], 1, 0)
+
+    def f_of(at):
+        return dot2(split(f_ref[...]), spread[:, at], 1, 0)
+
+    def row(k, at):
+        return lanes[k : k + 1, at]
+
+    def own_state(i, at):
+        fx2 = split(f_of(at) * x_ref[:, at].astype(f32))
+        s_buf[:, at] = row(TAIL, at) * dot2(bkt[...], fx2, 1, 0)
+
+    def in_span(i, at):
+        fx2 = split(f_of(at) * x_ref[:, at].astype(f32))
+        u[:, at] = dot2((gm_hi[...], gm_lo[...]), fx2, 1, 0)
+
+    def project_back(i, at):
+        w_copy(i).wait()
+
+        @pl.when(i + 1 < blocks)
+        def _():
+            w_copy(i + 1).start()
+
+        dn[:, at] = bdot(og_ref[...], w_buf[lax.rem(i, 2)], 1, 1)
+
+    def read_out(i, at):
+        before = inc[:, at]
+        s2 = split(row(LEAD, at) * before)
+        s_in[:, at] = s2[0]
+        s_buf[:, at] = row(THROUGH, at) * before + s_buf[:, at]
+        now = u[:, at] + dot2(co[...], s2, 1, 0)
+        u[:, at] = now
+        y = e_of(at) * now + row(SKIP, at) * x_ref[:, at].astype(f32)
+        zf = z_ref[:, at].astype(f32)
+        g = y * (zf * jax.nn.sigmoid(zf))
+        ms_acc[...] += jnp.broadcast_to(jnp.sum(g * g, axis=1, keepdims=True), ms_acc.shape)
+        m2_acc[...] += jnp.broadcast_to(
+            jnp.sum(dn[:, at] * gain_ref[0:1, at] * g, axis=1, keepdims=True), m2_acc.shape)
+
+    def norm(i, at):
+        e = e_of(at)
+        y = e * u[:, at] + row(SKIP, at) * x_ref[:, at].astype(f32)
+        zf = z_ref[:, at].astype(f32)
+        sig = jax.nn.sigmoid(zf)
+        silu = zf * sig
+        r = lax.rsqrt(ms_acc[:, 0:1] * (1.0 / width) + 1e-05)
+        ghat = y * silu * r
+        gain = gain_ref[0:1, at]
+        out = ghat * gain
+        out_low = out.astype(bf16)
+        normed[:, at] = out_low
+        up = out_low.astype(f32).T.reshape(BLOCK // 192, 2, 96, span)
+        here = pl.ds(i * (BLOCK // 192), BLOCK // 192)
+        even = ring.core == 0
+        nt_own[here] = jnp.where(even, up[:, 0], up[:, 1]).astype(bf16)
+        nt_send[here] = jnp.where(even, up[:, 1], up[:, 0])
+        ring.nt_copy(i, BLOCK // 192).start()
+        d = dn[:, at]
+        sums = jnp.sum(d * ghat, axis=0, keepdims=True)
+        for k in range(BLOCK // 128):
+            small[pl.ds(i * (BLOCK // 128) + k, 1)] = sums[:, k * 128 : (k + 1) * 128]
+        dg = r * (d * gain - ghat * (r * m2_acc[:, 0:1] * (1.0 / width)))
+        dy = dg * silu
+        dz_out[:, at] = (dg * y * (sig * (1.0 + zf * (1.0 - sig)))).astype(bf16)
+        dn[:, at] = dy
+        sg[:, at] = row(LEAD, at) * dot2(cot[...], split(e * dy), 1, 0)
+
+    def pass_one(i, at):
+        sp = spread[:, at]
+        dy, xb = dn[:, at], x_ref[:, at].astype(f32)
+        du = e_of(at) * dy
+        fx = (f_of(at) * xb).astype(bf16)
         du2 = split(du)
-        dfx[:, at] = dot2((gt_hi[...], gt_lo[...]), du2, 1, 0)
+        b_acc[...] += dot2(split(du * u[:, at]), sp, 1, 1)
+        u[:, at] = dot2((gt_hi[...], gt_lo[...]), du2, 1, 0)
         dg_acc[...] += dot2(du2, fx, 1, 1)
-        dc_acc[...] += dot2(du2, s_in_ref[:, at], 1, 1)
-        b_acc[...] += dot2(split(du * u_ref[:, at]), sp, 1, 1)
-        row = jnp.broadcast_to(jnp.sum(dy * xb, axis=0, keepdims=True), (8, BLOCK))
-        skip_acc[...] += dot2(split(row), sp, 1, 1)
-        return 0
-
-    def pass_two(i, _):
-        at = block(i)
-        sp = spread_ref[:, at].astype(bf16)
-        f = dot2(split(f_ref[...]), sp, 1, 0)
+        dc_acc[...] += dot2(du2, s_in[:, at], 1, 1)
+        line = jnp.broadcast_to(jnp.sum(dy * xb, axis=0, keepdims=True), (8, BLOCK))
+        skip_acc[...] += dot2(split(line), sp, 1, 1)
+
+    def pass_two(i, at):
+        sp = spread[:, at]
+        f = f_of(at)
         fx = f * x_ref[:, at].astype(f32)
-        late = later[:, at]
-        ds2 = split(lanes_ref[0:1, at] * late)
-        d = dfx[:, at] + dot2(b_ref[...] * keep_ref[...].astype(bf16), ds2, 1, 0)
-        dx_out[:, at] = (f * d + lanes_ref[1:2, at] * dy_ref[:, at]).astype(bf16)
+        late = inc[:, at]
+        ds2 = split(row(TAIL, at) * late)
+        d = u[:, at] + dot2(bk[...], ds2, 1, 0)
+        dx_out[:, at] = (f * d + row(SKIP, at) * dn[:, at]).astype(bf16)
         a_acc[...] += dot2(split(fx * d), sp, 1, 1)
         db_acc[...] += dot2(fx.astype(bf16), ds2, 1, 1)
-        row = jnp.broadcast_to(jnp.sum(late * s_end_ref[:, at], axis=0, keepdims=True), (8, BLOCK))
-        end_acc[...] += dot2(split(row), sp, 1, 1)
-        return 0
-
-    scan.begin()
-    ring.pair_begin()
-    scan.exchange()
+        line = jnp.broadcast_to(jnp.sum(late * s_buf[:, at], axis=0, keepdims=True), (8, BLOCK))
+        end_acc[...] += dot2(split(line), sp, 1, 1)
+
+    def project(i, at):
+        w_copy(i).wait()
+
+        @pl.when(i + 1 < blocks)
+        def _():
+            w_copy(i + 1).start()
+
+        og_wide[...] += bdot(normed[:, at], w_buf[lax.rem(i, 2)], 1, 0)
+
+    every(own_state)
+    pl.semaphore_wait(barrier, count + 3)
+    ahead.begin()
+    every(in_span)
+    ahead.exchange()
+    ring.og_begin()
+    every(project_back)
+    ahead.hops()
+    ahead.deliver()
+    ahead.finish()
+    every(read_out)
+    every(norm)
+    behind.begin()
     ring.own()
-    scan.hops()
-    ring.theirs()
+    behind.exchange()
+    ring.theirs(blocks)
     ring.begin(0)
-    for acc in (dg_acc, dc_acc, db_acc, a_acc, b_acc, skip_acc, end_acc):
-        acc[...] = jnp.zeros_like(acc)
-    lax.fori_loop(0, width // BLOCK, pass_one, 0)
-    scan.deliver()
+    behind.hops()
+    every(pass_one)
+    behind.deliver()
     ring.middle(0)
-    lax.fori_loop(0, width // BLOCK, pass_two, 0)
+    w_copy(0).start()
+    every(pass_two)
 
     a = a_acc[...]
-    rows = lax.broadcasted_iota(jnp.int32, (span, span), 0)
-    cols = lax.broadcasted_iota(jnp.int32, (span, span), 1)
-    upper = jnp.where(rows <= cols, 1.0, 0.0).astype(f32)
+    upper = jnp.where(ri <= ci, 1.0, 0.0)
     d_decay = jnp.dot(upper, b_acc[...] - a, precision=HIGHEST, preferred_element_type=f32) + end_acc[0:1]
-    dlogit = (a / step_ref[...] - rate_ref[0:1] * d_decay) * sig_ref[...]
-    heads = dlogit_out.shape[1]
-    dlogit_out[...] = dlogit[:, :heads].astype(bf16)
-    small[...] = jnp.zeros_like(small)
+    dlogit = (a / step_ref[...] - par_ref[1:2] * d_decay) * sig_ref[...]
+    dlogit_out[...] = dlogit[:, : dlogit_out.shape[1]].astype(bf16)
     lines = width // 128
-    small[0:lines] = gain_ref[...]
     small[lines : lines + 1] = jnp.sum(dlogit, axis=0, keepdims=True)
     small[lines + 1 : lines + 2] = jnp.sum(-step_ref[...] * d_decay, axis=0, keepdims=True)
     small[lines + 2 : lines + 3] = skip_acc[0:1]
     ring.small_pair_begin()
+    dg = dg_acc[...] * mask_ref[...]
+    dc_out[...] = (dot2(split(dg), b_ref[...], 1, 0) + open_ref[...] * dc_acc[...]).astype(bf16)
+    db_out[...] = (dot2(split(dg.T), c_ref[...], 1, 0) + keep_ref[...] * db_acc[...]).astype(bf16)
     ring.end(0)
     ring.begin(1)
     ring.small_pair_end()
     ring.small_begin(0)
-    dg = dg_acc[...] * mask_ref[...]
-    dc_out[...] = (dot2(split(dg), b_ref[...], 1, 0) + open_ref[...] * dc_acc[...]).astype(bf16)
-    db_out[...] = (dot2(split(dg.T), c_ref[...], 1, 0) + keep_ref[...] * db_acc[...]).astype(bf16)
+    ring.og_copy.wait_send()
+    og_wide[...] = jnp.zeros_like(og_wide)
+    every(project)
+    mixed_out[...] = og_wide[...].astype(bf16)
     ring.middle(1)
     ring.small_end(0)
     ring.small_begin(1)
@@ -566,144 +694,65 @@
     ring.small_end(2)
     ring.share_end()
     ring.finish()
-    scan.finish()
-
-
-def backward(n, heads, sg, thr, spread, nt, og, dy, *rest):
+
+    def sent(i, _):
+        ring.nt_copy(i, BLOCK // 192).wait_send()
+        return 0
+
+    lax.fori_loop(0, blocks, sent, 0)
+    behind.finish()
+
+
+def per_device(n, ssm_input, gate_input, input_map, output_map, step_logit, step_bias, decay_rate, skip_gain,
+               norm_gain, out_weight, resets, out_grad):
     f32, bf16 = jnp.float32, jnp.bfloat16
-    ns, width = sg.shape
-    span, cols = og.shape
-    rows = nt.shape[2]
-    lines = -(-(width // 128 + 3) // 8) * 8
+    _, span, width = ssm_input.shape
+    ns, heads, cols = input_map.shape[2], step_bias.shape[0], out_weight.shape[1]
+    rows, lines = width // 32, width // 128 + 8
+    logit = jnp.pad(step_logit[0], ((0, 0), (0, 128 - heads)))
+    params = jnp.pad(jnp.stack([step_bias, decay_rate, skip_gain]), ((0, 5), (0, 128 - heads)))
+    starts = jnp.broadcast_to(resets[0][:, None, None], (resets.shape[1], 8, span))
     vmem = pl.BlockSpec(memory_space=pltpu.VMEM)
-    wide = pltpu.VMEM((span, 128), f32)
-    out = pl.pallas_call(
-        functools.partial(backward_kernel, n),
+
+    def wide(*shape):
+        return pltpu.VMEM(shape, f32)
+
+    def low(*shape):
+        return pltpu.VMEM(shape, bf16)
+
+    chunk = wide(n // 2, ns // (n // 2), width // 2)
+    weight_grad, sums, dx, dz, db, dc, dlogit, mixed = pl.pallas_call(
+        functools.partial(mixer_kernel, n),
         out_shape=(
             jax.ShapeDtypeStruct((4, rows // 4, cols), f32),
             jax.ShapeDtypeStruct((lines, 128), f32),
             jax.ShapeDtypeStruct((span, width), bf16),
+            jax.ShapeDtypeStruct((span, width), bf16),
             jax.ShapeDtypeStruct((span, ns), bf16),
             jax.ShapeDtypeStruct((span, ns), bf16),
             jax.ShapeDtypeStruct((span, heads), bf16),
+            jax.ShapeDtypeStruct((span, cols), bf16),
         ),
-        in_specs=[vmem] * (6 + len(rest)),
-        out_specs=(vmem,) * 6,
+        in_specs=[vmem] * 9 + [pl.BlockSpec(memory_space=pl.ANY)],
+        out_specs=(vmem,) * 8,
         scratch_shapes=[
-            pltpu.VMEM((ns, width), f32),
-            pltpu.VMEM((span, width), f32),
-            pltpu.VMEM((span, span), f32),
-            pltpu.VMEM((span, ns), f32),
-            pltpu.VMEM((span, ns), f32),
-            wide,
-            wide,
-            pltpu.VMEM((8, 128), f32),
-            pltpu.VMEM((8, 128), f32),
-            pltpu.VMEM((lines, 128), f32),
-        ] + scan_scratch(n, ns, width) + ring_scratch(rows, cols, span, lines),
+            wide(span, width), wide(span, width), low(span, width), wide(ns, width), wide(ns, width), wide(ns, width),
+            low(ns, width), low(128, width), wide(8, width), low(2, BLOCK, cols),
+            low(span, span), low(span, span), low(span, span), low(span, span), wide(span, span),
+            low(span, ns), low(ns, span), low(span, ns), low(ns, span),
+            wide(span, 128), wide(span, 128), wide(span, 128), wide(span, 128), wide(span, ns), wide(span, ns),
+            wide(span, 128), wide(span, 128), wide(span, span), wide(span, ns), wide(span, ns),
+            wide(span, 128), wide(span, 128), wide(8, 128), wide(8, 128), wide(lines, 128),
+            low(16, rows, span), wide(16, rows, span), wide(span, cols), chunk, chunk, chunk,
+            pltpu.SemaphoreType.DMA((2,)),
+        ] + scan_scratch(n, ns, width) * 2 + ring_scratch(rows, cols, span, lines),
         compiler_params=pltpu.CompilerParams(
-            collective_id=2, has_side_effects=True, vmem_limit_bytes=VMEM_LIMIT),
-        name="backward",
-    )(sg, thr, spread, nt, og, dy, *rest)
-    return out
-
-
-def per_device(scan, back, ssm_input, gate_input, input_map, output_map, step_logit, step_bias,
-               decay_rate, skip_gain, norm_gain, out_weight, resets, out_grad):
-    f32, bf16 = jnp.float32, jnp.bfloat16
-    x, z, bmap, cmap, og = ssm_input[0], gate_input[0], input_map[0], output_map[0], out_grad[0]
-    rows, width = x.shape
-    heads = step_bias.shape[0]
-    per_head = width // heads
-
-    start = lax.axis_index("seq") * rows
-    ri = lax.broadcasted_iota(jnp.int32, (rows, rows), 0)
-    ci = lax.broadcasted_iota(jnp.int32, (rows, rows), 1)
-    below = ri >= ci
-    tri = below.astype(f32)
-    at_col = start + lax.broadcasted_iota(jnp.int32, (rows, 1), 0)
-    at_row = start + lax.broadcasted_iota(jnp.int32, (1, rows), 1)
-    flag_col = jnp.zeros((rows, 1), jnp.bool_)
-    flag_row = jnp.zeros((1, rows), jnp.bool_)
-    for k in range(resets.shape[1]):
-        flag_col |= at_col == resets[0, k]
-        flag_row |= at_row == resets[0, k]
-    count_col = jnp.sum(jnp.where(below & flag_row, 1.0, 0.0), axis=1, keepdims=True)
-    count_row = jnp.sum(jnp.where((ri <= ci) & flag_col, 1.0, 0.0), axis=0, keepdims=True)
-    count_all = jnp.sum(flag_row.astype(f32))
-    mask = below & (count_col == count_row)
-    opened = count_col == 0
-    keep = count_col == count_all
-
-    spread = (
-        lax.broadcasted_iota(jnp.int32, (heads, width), 0)
-        == lax.broadcasted_iota(jnp.int32, (heads, width), 1) // per_head
-    ).astype(f32)
-
-    raw = step_logit[0].astype(f32) + step_bias
-    step = jax.nn.softplus(raw)
-    cum = exact(tri, -decay_rate * step)
-    last = cum[rows - 1 :]
-    mid = cum[rows // 2 : rows // 2 + 1]
-    through = jnp.where(count_all == 0, jnp.exp(last), 0.0)
-    e_head = jnp.exp(cum - mid)
-    f_head = step * jnp.exp(mid - cum)
-    wide = exact(
-        jnp.concatenate([e_head, f_head, jnp.exp(last - mid), jnp.exp(mid), skip_gain[None], through], axis=0),
-        spread,
-    )
-    e, f = wide[:rows], wide[rows : 2 * rows]
-    tail, lead, skip, through_wide = (wide[2 * rows + k : 2 * rows + k + 1] for k in range(4))
-
-    xf = x.astype(f32)
-    fx_f = f * xf
-    fx2 = split_wide(fx_f)
-    fx = fx2[0]
-    gm2 = split_wide(jnp.where(mask, bdot(cmap, bmap, 1, 1), 0.0))
-    gm = gm2[0]
-    b_keep = jnp.where(keep, bmap, jnp.zeros_like(bmap))
-    c_open = jnp.where(opened, cmap, jnp.zeros_like(cmap))
-    s_own = dot2(b_keep, fx2, 0, 0)
-    thr = jnp.zeros((8, 128), f32).at[:, :heads].set(jnp.broadcast_to(through, (8, heads)))
-    spread_pad = jnp.zeros((128, width), f32).at[:heads].set(spread)
-    incoming = scan(tail * s_own, thr, spread_pad, False)
-    s_in2 = split_wide(lead * incoming)
-    s_in = s_in2[0]
-
-    u = dot2(gm2, fx2, 1, 0) + dot2(c_open, s_in2, 1, 0)
-    y = e * u + skip * xf
-    zf = z.astype(f32)
-    sig = jax.nn.sigmoid(zf)
-    silu = zf * sig
-    g = y * silu
-    r = lax.rsqrt(jnp.mean(g * g, axis=1, keepdims=True) + 1e-05)
-    ghat = g * r
-    normed = (ghat * norm_gain).astype(bf16)
-    mixed = bdot(normed, out_weight, 1, 0).astype(bf16)
-    dn = bdot(og, out_weight, 1, 1)
-    gain_grad = jnp.sum(dn * ghat, axis=0)
-    q = dn * norm_gain
-    dg = r * (q - ghat * jnp.mean(q * ghat, axis=1, keepdims=True))
-    dy = dg * silu
-    dz = (dg * y * (sig * (1.0 + zf * (1.0 - sig)))).astype(bf16)
-    du_f = e * dy
-    du2 = split_wide(du_f)
-    sg = lead * dot2(c_open, du2, 0, 0)
-
-    def padded(values, fill=0.0):
-        return jnp.pad(values, ((0, 0), (0, 128 - heads)), constant_values=fill)
-
-    gt2 = split_wide(jnp.where((ri <= ci) & (count_col == count_row), bdot(bmap, cmap, 1, 1), 0.0))
-    nt = normed.T.astype(f32).reshape(16, 2, width // 32, rows)
-    s_end = through_wide * incoming + tail * s_own
-    lanes = jnp.concatenate([tail, skip, jnp.zeros((6, width), f32)], axis=0)
-    weight_grad, sums, dx, db, dc, dlogit = back(
-        heads, sg, thr, spread_pad, nt, og.astype(f32), dy, u, x, padded(e_head), padded(f_head), *gt2, s_in, s_end, lanes,
-        bmap, cmap, mask.astype(f32), keep.astype(f32), opened.astype(f32), padded(step, 1.0),
-        padded(jax.nn.sigmoid(raw)), jnp.broadcast_to(padded(decay_rate[None]), (8, 128)), gain_grad.reshape(-1, 128))
-    lines = width // 128
-    gain_sum = sums[:lines].reshape(-1)
-    bias_sum, rate_sum, skip_sum = (sums[lines + k, :heads] for k in range(3))
+            collective_id=1, has_side_effects=True, vmem_limit_bytes=VMEM_LIMIT),
+        name="mixer",
+    )(ssm_input[0], gate_input[0], input_map[0], output_map[0], logit, out_grad[0], params, norm_gain[None], starts,
+      out_weight)
+    first = width // 128
+    bias_sum, rate_sum, skip_sum = (sums[first + k, :heads] for k in range(3))
     return (
         mixed[None],
         dx[None],
@@ -714,23 +763,15 @@
         bias_sum,
         rate_sum,
         skip_sum,
-        gain_sum,
-        weight_grad.reshape(-1, weight_grad.shape[-1]),
+        sums[:first].reshape(-1),
+        weight_grad.reshape(rows, cols),
     )
 
 
 def solution(mesh):
-    n = mesh.shape["seq"]
-
-    def scan(state, thr, spread, reverse):
-        return state_scan(n, state, thr, spread, reverse)
-
-    def back(heads, *operands):
-        return backward(n, heads, *operands)
-
     by_rows = P("dp", "seq", None)
     return jax.shard_map(
-        functools.partial(per_device, scan, back),
+        functools.partial(per_device, mesh.shape["seq"]),
         mesh=mesh,
         in_specs=(by_rows,) * 5 + (P(),) * 5 + (P("dp", None), by_rows),
         out_specs=(by_rows,) * 6 + (P(),) * 4 + (P("seq", None),),

time: 223 us -> 168 us (0.75)
  matrix products: 36.3 us -> 0 us
  other arithmetic: 26.3 us -> 1.29 us
  Pallas kernels: 132 us -> 151 us
  local copies, waits for them, and re-layouts: 25.9 us -> 14.3 us
    dot_general x15 -> x0, matrix products: 36.3 us -> none  [the longest x13 32.6 us: bdot(): lax.dot_general(a, b, (((ca,), (cb,)), ((), ())), preferred_element_type=...]
    pallas_call x2 -> x1, Pallas kernels: 132 us -> 151 us  [per_device(): pl.pallas_call(functools.partial(mixer_kernel, n), out_shape=(jax.ShapeDt...]
    convert_element_type x4 -> x0, other arithmetic: 5.68 us -> none  [the longest x1 2.48 us: per_device(): og.astype(f32)]
    broadcast_in_dim x1 -> x0, other arithmetic: 5.33 us -> none  [per_device(): dz[None]]
    reshape x2 -> x1, local copies, waits for them, and re-layouts: 5.98 us -> 1.31 us  [per_device(): sums[:first].reshape(-1)]
    pad x4 -> x1, local copies, waits for them, and re-layouts: 4.48 us -> 0.65 us  [per_device(): logit = jnp.pad(step_logit[0], ((0, 0), (0, 128 - heads)))]
    add x1 -> x0, other arithmetic: 3.49 us -> none  [per_device(): s_end = through_wide * incoming + tail * s_own]
    reduce_sum x2 -> x0, other arithmetic: 3.36 us -> none  [the longest x1 3.19 us: per_device(): count_all = jnp.sum(flag_row.astype(f32))]
where the time goes in v4:
time: 168 us; the launch traced here: 167 us
  Pallas kernels  151 us (90%)
  local copies, waits for them, and re-layouts  14.3 us (9%)
    pallas_call x1, Pallas kernels, per_device(): pl.pallas_call(functools.partial(mixer_kernel, n), out_shape=(jax.ShapeDt...  151 us
    unnamed x18, local copies, waits for them, and re-layouts  9.65 us

profile of v4, /device:TPU:0, one launch (start us, length us, event | category | flops | bytes accessed | tf_op | source)
XLA Modules:
  0.0 167.4 jit_solution(4615611791281359153)
XLA Ops:
  0.6 0.9 copy.23
  1.5 0.7 pad.8.logit_ref
  2.1 1.3 broadcast_in_dim.30.resets_ref
  3.5 1.3 select_maximum_fusion.par_ref
  4.8 151.2 %mixer.1 = (f32[4,24,1536]{2,1,0:T(8,128)}, f32[32,128]{1,0:T(8,128)}, bf16[256,3072]{1,0:T(8,128)(2,1)}, bf16[256,3072]{1,0:T(8,128)(2,1)}, bf16[256,128]{1,0:T...) custom-call(bf16[256,3072]{1,0:T(8,128)(2,1)} %bitcast.28, ...), custom_call_target="tpu_custom_call" | custom-call | tf_op jit(solution)/shard_map/mixer/pallas_call | solution.py:724
  156.0 0.0 copy-start.1
  156.0 1.3 slice_bitcast_fusion.1
  157.3 1.3 slice_bitcast_fusion
  158.6 1.5 copy.24
  160.1 2.1 %copy.31 = bf16[1,256,1536]{2,1,0:T(8,128)(2,1)} copy(bf16[1,256,1536]{2,1,0:T(8,128)(2,1)} %bitcast.30) | data formatting | bytes 1572864
  162.2 0.0 copy-done.1
  162.2 0.0 copy-start
  162.2 1.1 copy.32
  163.3 0.8 copy-done
  164.2 0.0 copy-start.4
  164.2 0.0 copy-start.3
  164.2 0.0 copy-start.2
  164.2 1.1 copy.33
  165.3 0.0 copy-done.4
  165.3 0.6 copy.34
  166.0 0.0 copy-done.3
  166.0 0.6 copy.35
  166.6 0.0 copy-done.2
  166.6 0.8 copy.36
Async XLA Ops:
  156.0 6.2 %copy-start.1 = (bf16[256,3072]{1,0:T(8,128)(2,1)S(1)}, bf16[256,3072]{1,0:T(8,128)(2,1)}, u32[]{:S(2)}) copy-start(bf16[256,3072]{1,0:T(8,128)(2,1)} %get-tuple-element.20) | copy-start | bytes 4718596
  162.2 2.0 %copy-start = (bf16[256,3072]{1,0:T(8,128)(2,1)S(1)}, bf16[256,3072]{1,0:T(8,128)(2,1)}, u32[]{:S(2)}) copy-start(bf16[256,3072]{1,0:T(8,128)(2,1)} %get-tuple-element.21) | copy-start | bytes 4718596
  164.2 1.2 copy-start.4
  164.2 1.8 %copy-start.3 = (bf16[256,128]{1,0:T(8,128)(2,1)S(1)}, bf16[256,128]{1,0:T(8,128)(2,1)}, u32[]{:S(2)}) copy-start(bf16[256,128]{1,0:T(8,128)(2,1)} %get-tuple-element.23) | copy-start | bytes 196612
  164.2 2.4 %copy-start.2 = (f32[4,24,1536]{2,1,0:T(8,128)S(1)}, f32[4,24,1536]{2,1,0:T(8,128)}, u32[]{:S(2)}) copy-start(f32[4,24,1536]{2,1,0:T(8,128)} %get-tuple-element.26) | copy-start | bytes 1769476

commit v5 on v4

--- a/solution.py
+++ b/solution.py
@@ -177,6 +177,7 @@
             @pl.when(k != self.chip)
             def _():
                 self.back_copy(self.chip, k).wait_recv()
+                self.chunk_copy(k, self.chip).wait_send()
 
             early = self.back[k]
             own = self.s_ref[self.band(k), self.lanes(self.core)]
@@ -205,7 +206,6 @@
             @pl.when(k != self.chip)
             def _():
                 self.thr_copy(k, self.chip).wait_send()
-                self.chunk_copy(k, self.chip).wait_send()
                 self.back_copy(k, self.chip).wait_send()
 
             return 0
@@ -231,7 +231,8 @@
 
 
 def make_scan(n, reverse, s_ref, spread_ref, out_ref, shared, scratch):
-    mine, stage, give = shared
+    mine, stage = shared
+    give = mine
     pair, recv, back, thr_ref = scratch[:4]
     return Scan(n, reverse, s_ref, thr_ref, spread_ref, out_ref, pair, mine, recv, stage, back, give,
                 *scratch[4:9], scratch[9:])
@@ -241,7 +242,7 @@
 
 
 class Ring:
-    def __init__(self, og_ref, og_wide, nt_own, nt_send, out_ref, small, small_out, part, nt_got, og_got, agg1, full1, agg2, full2,
+    def __init__(self, og_ref, og_wide, nt_own, nt_send, out_ref, small, small_out, part, nt_got, og_got, og_theirs, agg1, full1, agg2, full2,
                  agg3, full3, slots_c, slots_a, total, sems):
         (self.cs, self.cr, self.ns, self.nr, self.rs, self.rr, self.xs, self.xr, self.ms, self.mr) = sems
         self.xi = lax.axis_index("dp")
@@ -252,7 +253,7 @@
         self.og_ref, self.og_wide, self.nt_own, self.nt_send = og_ref, og_wide, nt_own, nt_send
         self.out_ref = out_ref
         self.small, self.small_out = small, small_out
-        self.part, self.nt_got, self.og_got = part, nt_got, og_got
+        self.part, self.nt_got, self.og_got, self.og_theirs = part, nt_got, og_got, og_theirs
         self.bufs = ((agg1, full1), (agg2, full2), (agg3, full3))
         self.slots_c, self.slots_a, self.total = slots_c, slots_a, total
         self.third = part.shape[-1] // 3
@@ -285,28 +286,22 @@
         here = pl.ds(i * count, count)
         return self.remote(self.nt_send.at[here], self.nt_got.at[here], self.ns.at[i], self.nr.at[i], self.sibling)
 
-    def own(self):
+    def og_end(self):
+        self.og_copy.wait_recv()
+        self.og_theirs[...] = self.og_got[...].astype(jnp.bfloat16)
+
+    def product(self, parts):
+        def got(i, _):
+            self.nt_copy(i, 16 // parts).wait_recv()
+            return 0
+
+        lax.fori_loop(0, parts, got, 0)
+
         def one(b, _):
             z, y = lax.div(b, 4), lax.rem(b, 4)
-            self.part[z, y] = bdot(self.nt_own[b], self.og_ref[...], 1, 0).reshape(self.part.shape[2:])
-            return 0
-
-        lax.fori_loop(0, 16, one, 0)
-
-    def theirs(self, parts):
-        self.og_copy.wait_recv()
-        og = self.og_got[...].astype(jnp.bfloat16)
-
-        def got(i, _):
-            self.nt_copy(i, 16 // parts).wait_recv()
-            return 0
-
-        lax.fori_loop(0, parts, got, 0)
-
-        def one(b, _):
-            z, y = lax.div(b, 4), lax.rem(b, 4)
-            lhs = self.nt_got[b].astype(jnp.bfloat16)
-            self.part[z, y] += bdot(lhs, og, 1, 0).reshape(self.part.shape[2:])
+            sums = bdot(self.nt_own[b], self.og_ref[...], 1, 0)
+            sums += bdot(self.nt_got[b].astype(jnp.bfloat16), self.og_theirs[...], 1, 0)
+            self.part[z, y] = sums.reshape(self.part.shape[2:])
             return 0
 
         lax.fori_loop(0, 16, one, 0)
@@ -419,6 +414,7 @@
         pltpu.VMEM((4, 4, 4, quarter, cols), f32),
         pltpu.VMEM((16, rows, span), f32),
         pltpu.VMEM((span, cols), f32),
+        pltpu.VMEM((span, cols), jnp.bfloat16),
         pltpu.VMEM((3, 2, 4, 4, quarter, half), f32),
         pltpu.VMEM((3, 2, 4, 4, quarter, third), f32),
         pltpu.VMEM((3, 2, 4, quarter, half), f32),
@@ -449,16 +445,17 @@
     return jnp.maximum(v, 0.0) + jnp.log1p(jnp.exp(-jnp.abs(v)))
 
 
-def mixer_kernel(n, x_ref, z_ref, b_ref, c_ref, logit_ref, og_ref, par_ref, gain_ref, resets_ref, w_hbm,
+def mixer_kernel(n, x_ref, z_ref, b_ref, c_ref, logit_in, og_ref, bias_in, rate_in, skip_in, gain_ref,
+                 resets_ref, w_hbm,
                  w_out, small_out, dx_out, dz_out, db_out, dc_out, dlogit_out, mixed_out, *scratch):
     (dn, u, normed, s_buf, inc, sg, s_in, spread, lanes, w_buf, gm_hi, gm_lo, gt_hi, gt_lo, mask_ref, bk, bkt, co, cot,
      e_ref, f_ref, step_ref, sig_ref, keep_ref, open_ref, ms_acc, m2_acc, dg_acc, dc_acc, db_acc, a_acc, b_acc,
-     skip_acc, end_acc, small, nt_own, nt_send, og_wide, mine, stage, give, w_sem) = scratch[:42]
+     skip_acc, end_acc, small, nt_own, nt_send, og_wide, mine, stage, par_ref, w_sem) = scratch[:42]
     rest = scratch[42:]
-    ahead = make_scan(n, False, s_buf, spread, inc, (mine, stage, give), rest[:SCAN_SCRATCH])
-    behind = make_scan(n, True, sg, spread, inc, (mine, stage, give), rest[SCAN_SCRATCH : 2 * SCAN_SCRATCH])
+    ahead = make_scan(n, False, s_buf, spread, inc, (mine, stage), rest[:SCAN_SCRATCH])
+    behind = make_scan(n, True, sg, spread, inc, (mine, stage), rest[SCAN_SCRATCH : 2 * SCAN_SCRATCH])
     rest = rest[2 * SCAN_SCRATCH :]
-    ring = Ring(og_ref, og_wide, nt_own, nt_send, w_out, small, small_out, *rest[:12], rest[12:])
+    ring = Ring(og_ref, og_wide, nt_own, nt_send, w_out, small, small_out, *rest[:13], rest[13:])
     f32, bf16 = jnp.float32, jnp.bfloat16
     span, width = x_ref.shape
     blocks = width // BLOCK
@@ -478,8 +475,8 @@
     ci = lax.broadcasted_iota(jnp.int32, (span, span), 1)
     flag_c = jnp.zeros((span, span), f32)
     flag_r = jnp.zeros((span, span), f32)
-    for k in range(resets_ref.shape[0]):
-        at_reset = resets_ref[k, 0:1, :] - start
+    for k in range(resets_ref.shape[1]):
+        at_reset = resets_ref[0:1, k : k + 1] - start
         flag_c = jnp.where(ci == at_reset, 1.0, flag_c)
         flag_r = jnp.where(ri == at_reset, 1.0, flag_r)
     count_col = jnp.sum(jnp.where(ri >= ci, flag_c, 0.0), axis=1, keepdims=True)
@@ -502,7 +499,14 @@
     gm = bdot(c_ref[...], b_ref[...], 1, 1) * mask
     gm_hi[...], gm_lo[...] = split(gm)
     gt_hi[...], gt_lo[...] = split(gm.T)
-    raw = logit_ref[...].astype(f32) + par_ref[0:1]
+    heads = logit_in.shape[1]
+    sig_ref[...] = jnp.zeros_like(sig_ref)
+    sig_ref[:, 0:heads] = logit_in[...].astype(f32)
+    par_ref[...] = jnp.zeros_like(par_ref)
+    par_ref[0:1, 0:heads] = bias_in[...]
+    par_ref[1:2, 0:heads] = rate_in[...]
+    par_ref[2:3, 0:heads] = skip_in[...]
+    raw = sig_ref[...] + par_ref[0:1]
     step = softplus(raw)
     step_ref[...] = step
     sig_ref[...] = jax.nn.sigmoid(raw)
@@ -636,28 +640,45 @@
 
         og_wide[...] += bdot(normed[:, at], w_buf[lax.rem(i, 2)], 1, 0)
 
-    every(own_state)
+    half = blocks // 2
+    theirs_first = (1 - ring.core) * half
+
+    def part_of(body, lo):
+        def one(i, _):
+            k = lax.rem(theirs_first + lo + i, blocks)
+            body(k, block(k))
+            return 0
+
+        lax.fori_loop(0, half, one, 0)
+
+    part_of(own_state, 0)
     pl.semaphore_wait(barrier, count + 3)
     ahead.begin()
-    every(in_span)
+    part_of(own_state, half)
     ahead.exchange()
     ring.og_begin()
     every(project_back)
     ahead.hops()
+    every(in_span)
+    ring.og_end()
     ahead.deliver()
     ahead.finish()
     every(read_out)
-    every(norm)
+    part_of(norm, 0)
     behind.begin()
-    ring.own()
+    part_of(norm, half)
     behind.exchange()
-    ring.theirs(blocks)
+    ring.product(blocks)
     ring.begin(0)
     behind.hops()
+    w_copy(0).start()
+    ring.og_copy.wait_send()
+    og_wide[...] = jnp.zeros_like(og_wide)
     every(pass_one)
+    ring.middle(0)
+    every(project)
+    mixed_out[...] = og_wide[...].astype(bf16)
     behind.deliver()
-    ring.middle(0)
-    w_copy(0).start()
     every(pass_two)
 
     a = a_acc[...]
@@ -670,17 +691,13 @@
     small[lines + 1 : lines + 2] = jnp.sum(-step_ref[...] * d_decay, axis=0, keepdims=True)
     small[lines + 2 : lines + 3] = skip_acc[0:1]
     ring.small_pair_begin()
-    dg = dg_acc[...] * mask_ref[...]
-    dc_out[...] = (dot2(split(dg), b_ref[...], 1, 0) + open_ref[...] * dc_acc[...]).astype(bf16)
-    db_out[...] = (dot2(split(dg.T), c_ref[...], 1, 0) + keep_ref[...] * db_acc[...]).astype(bf16)
     ring.end(0)
     ring.begin(1)
     ring.small_pair_end()
     ring.small_begin(0)
-    ring.og_copy.wait_send()
-    og_wide[...] = jnp.zeros_like(og_wide)
-    every(project)
-    mixed_out[...] = og_wide[...].astype(bf16)
+    dg = dg_acc[...] * mask_ref[...]
+    dc_out[...] = (dot2(split(dg), b_ref[...], 1, 0) + open_ref[...] * dc_acc[...]).astype(bf16)
+    db_out[...] = (dot2(split(dg.T), c_ref[...], 1, 0) + keep_ref[...] * db_acc[...]).astype(bf16)
     ring.middle(1)
     ring.small_end(0)
     ring.small_begin(1)
@@ -703,15 +720,27 @@
     behind.finish()
 
 
+def results_kernel(w, sums, dx, dz, db, dc, dlogit, mixed, mixed_to, dx_to, dz_to, db_to, dc_to, dlogit_to,
+                   bias_to, rate_to, skip_to, gain_to, w_to, sems):
+    pairs = ((dx, dx_to), (dz, dz_to), (mixed, mixed_to), (w, w_to), (db, db_to), (dc, dc_to), (dlogit, dlogit_to))
+    copies = [pltpu.make_async_copy(a, b, sems.at[k]) for k, (a, b) in enumerate(pairs)]
+    for c in copies:
+        c.start()
+    lines, heads = gain_to.shape[0], bias_to.shape[1]
+    gain_to[...] = sums[0:lines]
+    bias_to[...] = sums[lines : lines + 1, 0:heads]
+    rate_to[...] = sums[lines + 1 : lines + 2, 0:heads]
+    skip_to[...] = sums[lines + 2 : lines + 3, 0:heads]
+    for c in copies:
+        c.wait()
+
+
 def per_device(n, ssm_input, gate_input, input_map, output_map, step_logit, step_bias, decay_rate, skip_gain,
                norm_gain, out_weight, resets, out_grad):
     f32, bf16 = jnp.float32, jnp.bfloat16
     _, span, width = ssm_input.shape
     ns, heads, cols = input_map.shape[2], step_bias.shape[0], out_weight.shape[1]
     rows, lines = width // 32, width // 128 + 8
-    logit = jnp.pad(step_logit[0], ((0, 0), (0, 128 - heads)))
-    params = jnp.pad(jnp.stack([step_bias, decay_rate, skip_gain]), ((0, 5), (0, 128 - heads)))
-    starts = jnp.broadcast_to(resets[0][:, None, None], (resets.shape[1], 8, span))
     vmem = pl.BlockSpec(memory_space=pltpu.VMEM)
 
     def wide(*shape):
@@ -733,7 +762,7 @@
             jax.ShapeDtypeStruct((span, heads), bf16),
             jax.ShapeDtypeStruct((span, cols), bf16),
         ),
-        in_specs=[vmem] * 9 + [pl.BlockSpec(memory_space=pl.ANY)],
+        in_specs=[vmem] * 11 + [pl.BlockSpec(memory_space=pl.ANY)],
         out_specs=(vmem,) * 8,
         scratch_shapes=[
             wide(span, width), wide(span, width), low(span, width), wide(ns, width), wide(ns, width), wide(ns, width),
@@ -743,28 +772,30 @@
             wide(span, 128), wide(span, 128), wide(span, 128), wide(span, 128), wide(span, ns), wide(span, ns),
             wide(span, 128), wide(span, 128), wide(span, span), wide(span, ns), wide(span, ns),
             wide(span, 128), wide(span, 128), wide(8, 128), wide(8, 128), wide(lines, 128),
-            low(16, rows, span), wide(16, rows, span), wide(span, cols), chunk, chunk, chunk,
+            low(16, rows, span), wide(16, rows, span), wide(span, cols), chunk, chunk,
+            wide(8, 128),
             pltpu.SemaphoreType.DMA((2,)),
         ] + scan_scratch(n, ns, width) * 2 + ring_scratch(rows, cols, span, lines),
         compiler_params=pltpu.CompilerParams(
             collective_id=1, has_side_effects=True, vmem_limit_bytes=VMEM_LIMIT),
         name="mixer",
-    )(ssm_input[0], gate_input[0], input_map[0], output_map[0], logit, out_grad[0], params, norm_gain[None], starts,
-      out_weight)
-    first = width // 128
-    bias_sum, rate_sum, skip_sum = (sums[first + k, :heads] for k in range(3))
+    )(ssm_input[0], gate_input[0], input_map[0], output_map[0], step_logit[0], out_grad[0], step_bias[None],
+      decay_rate[None], skip_gain[None], norm_gain[None], resets, out_weight)
+    anywhere = pl.BlockSpec(memory_space=pl.ANY)
+    shapes = [(v.shape, bf16) for v in (mixed, dx, dz, db, dc, dlogit)] + [((1, heads), f32)] * 3
+    shapes += [((width // 128, 128), f32), (weight_grad.shape, f32)]
+    out = pl.pallas_call(
+        results_kernel,
+        out_shape=tuple(jax.ShapeDtypeStruct(*v) for v in shapes),
+        in_specs=[anywhere, vmem] + [anywhere] * 6,
+        out_specs=(anywhere,) * 6 + (vmem,) * 4 + (anywhere,),
+        scratch_shapes=[pltpu.SemaphoreType.DMA((7,))],
+        name="results",
+    )(weight_grad, sums, dx, dz, db, dc, dlogit, mixed)
     return (
-        mixed[None],
-        dx[None],
-        dz[None],
-        db[None],
-        dc[None],
-        dlogit[None],
-        bias_sum,
-        rate_sum,
-        skip_sum,
-        sums[:first].reshape(-1),
-        weight_grad.reshape(rows, cols),
+        *(v[None] for v in out[:6]),
+        *(v.reshape(-1) for v in out[6:10]),
+        out[10].reshape(rows, cols),
     )
 
 

time: 168 us -> 283 us (1.68)
  Pallas kernels: 151 us -> 278 us
  local copies, waits for them, and re-layouts: 14.3 us -> 3 us
    pallas_call x0 -> x1, Pallas kernels: none -> 145 us  [per_device(): pl.pallas_call(results_kernel, out_shape=tuple((jax.ShapeDtypeStruct(*v)...]
    pallas_call x1, Pallas kernels: 151 us -> 133 us  [per_device(): pl.pallas_call(functools.partial(mixer_kernel, n), out_shape=(jax.ShapeDt...]
    unnamed x18 -> x2, local copies, waits for them, and re-layouts: 9.65 us -> 3 us
where the time goes in v5:
time: 283 us; the launch traced here: 282 us
  Pallas kernels  278 us (98%)
  local copies, waits for them, and re-layouts  3 us (1%)
    pallas_call x1, Pallas kernels, per_device(): pl.pallas_call(results_kernel, out_shape=tuple((jax.ShapeDtypeStruct(*v)...  145 us
    pallas_call x1, Pallas kernels, per_device(): pl.pallas_call(functools.partial(mixer_kernel, n), out_shape=(jax.ShapeDt...  133 us

profile of v5, /device:TPU:0, one launch (start us, length us, event | category | flops | bytes accessed | tf_op | source)
XLA Modules:
  0.0 281.8 jit_solution(6718061776268728052)
XLA Ops:
  0.6 1.5 copy.23
  2.1 132.7 %mixer.1 = (f32[4,24,1536]{2,1,0:T(8,128)}, f32[32,128]{1,0:T(8,128)}, bf16[256,3072]{1,0:T(8,128)(2,1)}, bf16[256,3072]{1,0:T(8,128)(2,1)}, bf16[256,128]{1,0:T...) custom-call(bf16[256,3072]{1,0:T(8,128)(2,1)} %bitcast.21, ...), custom_call_target="tpu_custom_call" | custom-call | tf_op jit(solution)/shard_map/mixer/pallas_call | solution.py:753
  134.8 145.4 %results.1 = (bf16[256,1536]{1,0:T(8,128)(2,1)}, bf16[256,3072]{1,0:T(8,128)(2,1)}, bf16[256,3072]{1,0:T(8,128)(2,1)}, bf16[256,128]{1,0:T(8,128)(2,1)}, bf16[25...) custom-call(f32[4,24,1536]{2,1,0:T(8,128)} %get-tuple-element.30.w, ...), custom_call_target="tpu_custom_call" | custom-call | tf_op jit(solution)/shard_map/results/pallas_call | solution.py:787
  280.2 1.5 copy.24

commit v6 on v5

--- a/solution.py
+++ b/solution.py
@@ -304,7 +304,7 @@
             self.part[z, y] = sums.reshape(self.part.shape[2:])
             return 0
 
-        lax.fori_loop(0, 16, one, 0)
+        lax.fori_loop(0, 16, one, 0, unroll=2)
 
     def region(self, step, p, t, h=None):
         order = ORDERS[p]
@@ -535,7 +535,7 @@
             body(i, block(i))
             return 0
 
-        lax.fori_loop(0, blocks, one, 0)
+        lax.fori_loop(0, blocks, one, 0, unroll=2)
 
     def e_of(at):
         return dot2(split(e_ref[...]), spread[:, at], 1, 0)
@@ -649,7 +649,7 @@
             body(k, block(k))
             return 0
 
-        lax.fori_loop(0, half, one, 0)
+        lax.fori_loop(0, half, one, 0, unroll=2)
 
     part_of(own_state, 0)
     pl.semaphore_wait(barrier, count + 3)
@@ -721,17 +721,22 @@
 
 
 def results_kernel(w, sums, dx, dz, db, dc, dlogit, mixed, mixed_to, dx_to, dz_to, db_to, dc_to, dlogit_to,
-                   bias_to, rate_to, skip_to, gain_to, w_to, sems):
+                   bias_to, rate_to, skip_to, gain_to, w_to, *scratch):
     pairs = ((dx, dx_to), (dz, dz_to), (mixed, mixed_to), (w, w_to), (db, db_to), (dc, dc_to), (dlogit, dlogit_to))
-    copies = [pltpu.make_async_copy(a, b, sems.at[k]) for k, (a, b) in enumerate(pairs)]
-    for c in copies:
+    held, (in_sem, out_sem) = scratch[:-2], scratch[-2:]
+    into = [pltpu.make_async_copy(a, v, in_sem.at[k]) for k, ((a, _), v) in enumerate(zip(pairs, held))]
+    out = [pltpu.make_async_copy(v, b, out_sem.at[k]) for k, ((_, b), v) in enumerate(zip(pairs, held))]
+    for c in into:
         c.start()
     lines, heads = gain_to.shape[0], bias_to.shape[1]
     gain_to[...] = sums[0:lines]
     bias_to[...] = sums[lines : lines + 1, 0:heads]
     rate_to[...] = sums[lines + 1 : lines + 2, 0:heads]
     skip_to[...] = sums[lines + 2 : lines + 3, 0:heads]
-    for c in copies:
+    for a, b in zip(into, out):
+        a.wait()
+        b.start()
+    for c in out:
         c.wait()
 
 
@@ -789,7 +794,9 @@
         out_shape=tuple(jax.ShapeDtypeStruct(*v) for v in shapes),
         in_specs=[anywhere, vmem] + [anywhere] * 6,
         out_specs=(anywhere,) * 6 + (vmem,) * 4 + (anywhere,),
-        scratch_shapes=[pltpu.SemaphoreType.DMA((7,))],
+        scratch_shapes=[pltpu.VMEM(v.shape, v.dtype) for v in (dx, dz, mixed, weight_grad, db, dc, dlogit)]
+        + [pltpu.SemaphoreType.DMA((7,))] * 2,
+        compiler_params=pltpu.CompilerParams(vmem_limit_bytes=16 * 1024 * 1024),
         name="results",
     )(weight_grad, sums, dx, dz, db, dc, dlogit, mixed)
     return (

time: 283 us -> 146 us (0.52)
  Pallas kernels: 278 us -> 134 us
  local copies, waits for them, and re-layouts: 3 us -> 10.4 us
    pallas_call x1, Pallas kernels: 145 us -> 3.52 us  [per_device(): pl.pallas_call(results_kernel, out_shape=tuple((jax.ShapeDtypeStruct(*v)...]
    unnamed x2 -> x18, local copies, waits for them, and re-layouts: 3 us -> 10.4 us
where the time goes in v6:
time: 146 us; the launch traced here: 145 us
  Pallas kernels  134 us (92%)
  local copies, waits for them, and re-layouts  10.4 us (7%)
    pallas_call x1, Pallas kernels, per_device(): pl.pallas_call(functools.partial(mixer_kernel, n), out_shape=(jax.ShapeDt...  130 us
    unnamed x18, local copies, waits for them, and re-layouts  10.4 us
    pallas_call x1, Pallas kernels, per_device(): pl.pallas_call(results_kernel, out_shape=tuple((jax.ShapeDtypeStruct(*v)...  3.52 us

profile of v6, /device:TPU:0, one launch (start us, length us, event | category | flops | bytes accessed | tf_op | source)
XLA Modules:
  0.0 144.6 jit_solution(12182031293309021946)
XLA Ops:
  0.6 1.5 %copy.23 = bf16[1,256,48]{2,1,0:T(8,128)(2,1)} copy(bf16[1,256,48]{1,2,0:T(8,128)(2,1)} %param.16) | data formatting | bytes 49152 | tf_op args[4]
  2.1 130.0 %mixer.1 = (f32[4,24,1536]{2,1,0:T(8,128)}, f32[32,128]{1,0:T(8,128)}, bf16[256,3072]{1,0:T(8,128)(2,1)}, bf16[256,3072]{1,0:T(8,128)(2,1)}, bf16[256,128]{1,0:T...) custom-call(bf16[256,3072]{1,0:T(8,128)(2,1)} %bitcast.22, ...), custom_call_target="tpu_custom_call" | custom-call | tf_op jit(solution)/shard_map/mixer/pallas_call | solution.py:758
  132.2 0.0 copy-start
  132.2 1.4 copy-done
  133.6 0.0 copy-start.1
  133.6 1.4 copy-done.1
  135.0 0.0 copy-start.2
  135.0 1.1 copy-done.2
  136.1 0.0 copy-start.3
  136.1 1.1 copy-done.3
  137.2 0.0 copy-start.4
  137.2 0.8 copy-done.4
  138.0 0.0 copy-start.5
  138.0 0.8 copy-done.5
  138.9 0.0 copy-start.6
  138.9 0.8 copy-done.6
  139.7 0.0 copy-start.7
  139.7 0.7 copy-done.7
  140.4 3.5 %results.1 = (bf16[256,1536]{1,0:T(8,128)(2,1)}, bf16[256,3072]{1,0:T(8,128)(2,1)}, bf16[256,3072]{1,0:T(8,128)(2,1)}, bf16[256,128]{1,0:T(8,128)(2,1)}, bf16[25...) custom-call(f32[4,24,1536]{2,1,0:T(8,128)S(1)} %copy-done.3, ...), custom_call_target="tpu_custom_call" | custom-call | tf_op jit(solution)/shard_map/results/pallas_call | solution.py:792
  143.9 0.7 copy.24
Async XLA Ops:
  132.2 1.4 copy-start
  133.6 1.4 copy-start.1
  135.0 1.1 copy-start.2
  136.1 1.1 copy-start.3
  137.2 0.8 copy-start.4
  138.0 0.8 copy-start.5
  138.9 0.8 copy-start.6
  139.7 0.7 copy-start.7

commit v7 on v6

--- a/solution.py
+++ b/solution.py
@@ -158,15 +158,16 @@
                 self.chunk_copy(self.chip, j).wait_recv()
 
             self.stage[j] = state
-
-            @pl.when(j != self.chip)
-            def _():
-                self.back_copy(j, self.chip).start()
-
             return self.thr_wide[pl.ds(j, 1), :] * state + self.recv[j]
 
         lax.fori_loop(0, self.chips, hop, jnp.zeros((self.rows, self.half), jnp.float32))
         self.back[self.chip] = self.stage[self.chip]
+
+        def give_back(i, _):
+            self.back_copy(lax.rem(self.chip + 1 + i, self.chips), self.chip).start()
+            return 0
+
+        lax.fori_loop(0, self.chips - 1, give_back, 0)
 
     def deliver(self):
         mine_first = self.core == (1 if self.reverse else 0)
@@ -320,46 +321,50 @@
         me = self.here[axis]
         return axis, lax.rem(me + 1, 4), lax.rem(me + 3, 4), lax.rem(me + 2, 4)
 
+    def copies_of(self, step, p):
+        agg, full = self.bufs[step]
+        lo, hi = pl.ds(0, self.half), pl.ds(self.half, self.half)
+        axis, up, down, far = self.ways(step, p)
+
+        def go(t, h, dst, k, to):
+            return self.remote(self.part.at[self.region(step, p, t, h)], dst, self.rs.at[step, p, k],
+                               self.rr.at[step, p, k], self.at(axis, to))
+
+        first = [go(far, 0, agg.at[p, 0], 0, up), go(far, 1, agg.at[p, 1], 1, down)]
+        second = [go(up, 1, full.at[p, 0, ..., hi], 2, up), go(down, 0, full.at[p, 1, ..., lo], 3, down)]
+        last = [go(up, 0, full.at[p, 0, ..., lo], 4, up), go(down, 1, full.at[p, 1, ..., hi], 5, down)]
+        return first, second, last
+
     def begin(self, step):
-        agg, full = self.bufs[step]
-        first, second, last = [], [], []
-        lo, hi = pl.ds(0, self.half), pl.ds(self.half, self.half)
         for p in range(3):
-            axis, up, down, far = self.ways(step, p)
-
-            def go(t, h, dst, k, to):
-                return self.remote(self.part.at[self.region(step, p, t, h)], dst, self.rs.at[step, p, k],
-                                   self.rr.at[step, p, k], self.at(axis, to))
-
-            first.append([go(far, 0, agg.at[p, 0], 0, up), go(far, 1, agg.at[p, 1], 1, down)])
-            second.append([go(up, 1, full.at[p, 0, ..., hi], 2, up), go(down, 0, full.at[p, 1, ..., lo], 3, down)])
-            last.append([go(up, 0, full.at[p, 0, ..., lo], 4, up), go(down, 1, full.at[p, 1, ..., hi], 5, down)])
+            self.steps[step, p] = self.copies_of(step, p)
+            self.start(self.steps[step, p][0])
         for p in range(3):
-            self.start(first[p])
-        for p in range(3):
-            self.start(second[p])
-        self.steps[step] = (first, second, last)
+            self.start(self.steps[step, p][1])
 
     def middle(self, step):
         agg, _ = self.bufs[step]
-        first, _, last = self.steps[step]
         for p in range(3):
+            first, _, last = self.steps[step, p]
             _, up, down, _ = self.ways(step, p)
-            first[p][0].wait_recv()
+            first[0].wait_recv()
             self.part[self.region(step, p, up, 0)] += agg[p, 0]
-            self.start([last[p][0]])
-            first[p][1].wait_recv()
+            self.start([last[0]])
+            first[1].wait_recv()
             self.part[self.region(step, p, down, 1)] += agg[p, 1]
-            self.start([last[p][1]])
+            self.start([last[1]])
 
     def end(self, step):
         _, full = self.bufs[step]
-        _, second, last = self.steps[step]
         for p in range(3):
-            for c in second[p] + last[p]:
+            _, second, last = self.steps[step, p]
+            for c in second + last:
                 c.wait_recv()
             here = self.region(step, p, self.here[ORDERS[p][step]])
             self.part[here] += full[p, 0] + full[p, 1]
+            if step < 2:
+                self.steps[step + 1, p] = self.copies_of(step + 1, p)
+                self.start(self.steps[step + 1, p][0] + self.steps[step + 1, p][1])
 
     def small_pair_begin(self):
         self.small_pair = self.start([
@@ -692,7 +697,6 @@
     small[lines + 2 : lines + 3] = skip_acc[0:1]
     ring.small_pair_begin()
     ring.end(0)
-    ring.begin(1)
     ring.small_pair_end()
     ring.small_begin(0)
     dg = dg_acc[...] * mask_ref[...]
@@ -702,7 +706,6 @@
     ring.small_end(0)
     ring.small_begin(1)
     ring.end(1)
-    ring.begin(2)
     ring.small_end(1)
     ring.small_begin(2)
     ring.middle(2)
@@ -796,7 +799,7 @@
         out_specs=(anywhere,) * 6 + (vmem,) * 4 + (anywhere,),
         scratch_shapes=[pltpu.VMEM(v.shape, v.dtype) for v in (dx, dz, mixed, weight_grad, db, dc, dlogit)]
         + [pltpu.SemaphoreType.DMA((7,))] * 2,
-        compiler_params=pltpu.CompilerParams(vmem_limit_bytes=16 * 1024 * 1024),
+        compiler_params=pltpu.CompilerParams(vmem_limit_bytes=VMEM_LIMIT),
         name="results",
     )(weight_grad, sums, dx, dz, db, dc, dlogit, mixed)
     return (

time: 146 us -> 138 us (0.945)
  local copies, waits for them, and re-layouts: 10.4 us -> 3 us
    unnamed x18 -> x2, local copies, waits for them, and re-layouts: 10.4 us -> 3 us
    pallas_call x1, Pallas kernels: 3.52 us -> 5.02 us  [per_device(): pl.pallas_call(results_kernel, out_shape=tuple((jax.ShapeDtypeStruct(*v)...]
where the time goes in v7:
time: 138 us; the launch traced here: 137 us
  Pallas kernels  134 us (97%)
  local copies, waits for them, and re-layouts  3 us (2%)
    pallas_call x1, Pallas kernels, per_device(): pl.pallas_call(functools.partial(mixer_kernel, n), out_shape=(jax.ShapeDt...  129 us
    pallas_call x1, Pallas kernels, per_device(): pl.pallas_call(results_kernel, out_shape=tuple((jax.ShapeDtypeStruct(*v)...  5.02 us
    unnamed x2, local copies, waits for them, and re-layouts  3 us

profile of v7, /device:TPU:0, one launch (start us, length us, event | category | flops | bytes accessed | tf_op | source)
XLA Modules:
  0.0 137.4 jit_solution(10840177965523436444)
XLA Ops:
  0.6 1.5 %copy.23 = bf16[1,256,48]{2,1,0:T(8,128)(2,1)} copy(bf16[1,256,48]{1,2,0:T(8,128)(2,1)} %param.16) | data formatting | bytes 49152 | tf_op args[4]
  2.1 128.7 %mixer.1 = (f32[4,24,1536]{2,1,0:T(8,128)}, f32[32,128]{1,0:T(8,128)}, bf16[256,3072]{1,0:T(8,128)(2,1)}, bf16[256,3072]{1,0:T(8,128)(2,1)}, bf16[256,128]{1,0:T...) custom-call(bf16[256,3072]{1,0:T(8,128)(2,1)} %bitcast.21, ...), custom_call_target="tpu_custom_call" | custom-call | tf_op jit(solution)/shard_map/mixer/pallas_call | solution.py:761
  130.8 5.0 %results.1 = (bf16[256,1536]{1,0:T(8,128)(2,1)}, bf16[256,3072]{1,0:T(8,128)(2,1)}, bf16[256,3072]{1,0:T(8,128)(2,1)}, bf16[256,128]{1,0:T(8,128)(2,1)}, bf16[25...) custom-call(f32[4,24,1536]{2,1,0:T(8,128)} %get-tuple-element.30.w, ...), custom_call_target="tpu_custom_call" | custom-call | tf_op jit(solution)/shard_map/results/pallas_call | solution.py:795
  135.9 1.5 %copy.24 = bf16[1,256,48]{1,2,0:T(8,128)(2,1)} copy(bf16[1,256,48]{2,1,0:T(8,128)(2,1)} %bitcast.27) | data formatting | bytes 49152

commit v8 on v7

--- a/solution.py
+++ b/solution.py
@@ -504,14 +504,14 @@
     gm = bdot(c_ref[...], b_ref[...], 1, 1) * mask
     gm_hi[...], gm_lo[...] = split(gm)
     gt_hi[...], gt_lo[...] = split(gm.T)
-    heads = logit_in.shape[1]
-    sig_ref[...] = jnp.zeros_like(sig_ref)
-    sig_ref[:, 0:heads] = logit_in[...].astype(f32)
+    heads = logit_in.shape[0]
+    u[0:128, 0:span] = jnp.zeros((128, span), f32)
+    u[0:heads, 0:span] = logit_in[...].astype(f32)
     par_ref[...] = jnp.zeros_like(par_ref)
     par_ref[0:1, 0:heads] = bias_in[...]
     par_ref[1:2, 0:heads] = rate_in[...]
     par_ref[2:3, 0:heads] = skip_in[...]
-    raw = sig_ref[...] + par_ref[0:1]
+    raw = u[0:128, 0:span].T + par_ref[0:1]
     step = softplus(raw)
     step_ref[...] = step
     sig_ref[...] = jax.nn.sigmoid(raw)
@@ -690,7 +690,7 @@
     upper = jnp.where(ri <= ci, 1.0, 0.0)
     d_decay = jnp.dot(upper, b_acc[...] - a, precision=HIGHEST, preferred_element_type=f32) + end_acc[0:1]
     dlogit = (a / step_ref[...] - par_ref[1:2] * d_decay) * sig_ref[...]
-    dlogit_out[...] = dlogit[:, : dlogit_out.shape[1]].astype(bf16)
+    dlogit_out[...] = dlogit.T[: dlogit_out.shape[0]].astype(bf16)
     lines = width // 128
     small[lines : lines + 1] = jnp.sum(dlogit, axis=0, keepdims=True)
     small[lines + 1 : lines + 2] = jnp.sum(-step_ref[...] * d_decay, axis=0, keepdims=True)
@@ -767,7 +767,7 @@
             jax.ShapeDtypeStruct((span, width), bf16),
             jax.ShapeDtypeStruct((span, ns), bf16),
             jax.ShapeDtypeStruct((span, ns), bf16),
-            jax.ShapeDtypeStruct((span, heads), bf16),
+            jax.ShapeDtypeStruct((heads, span), bf16),
             jax.ShapeDtypeStruct((span, cols), bf16),
         ),
         in_specs=[vmem] * 11 + [pl.BlockSpec(memory_space=pl.ANY)],
@@ -787,7 +787,7 @@
         compiler_params=pltpu.CompilerParams(
             collective_id=1, has_side_effects=True, vmem_limit_bytes=VMEM_LIMIT),
         name="mixer",
-    )(ssm_input[0], gate_input[0], input_map[0], output_map[0], step_logit[0], out_grad[0], step_bias[None],
+    )(ssm_input[0], gate_input[0], input_map[0], output_map[0], step_logit[0].T, out_grad[0], step_bias[None],
       decay_rate[None], skip_gain[None], norm_gain[None], resets, out_weight)
     anywhere = pl.BlockSpec(memory_space=pl.ANY)
     shapes = [(v.shape, bf16) for v in (mixed, dx, dz, db, dc, dlogit)] + [((1, heads), f32)] * 3
@@ -803,7 +803,8 @@
         name="results",
     )(weight_grad, sums, dx, dz, db, dc, dlogit, mixed)
     return (
-        *(v[None] for v in out[:6]),
+        *(v[None] for v in out[:5]),
+        out[5].T[None],
         *(v.reshape(-1) for v in out[6:10]),
         out[10].reshape(rows, cols),
     )

time: 138 us -> 135 us (0.978)
  local copies, waits for them, and re-layouts: 3 us -> 0 us
    unnamed x2 -> x0, local copies, waits for them, and re-layouts: 3 us -> none
where the time goes in v8:
time: 135 us
  Pallas kernels  134 us (99%)
    pallas_call x1, Pallas kernels, per_device(): pl.pallas_call(functools.partial(mixer_kernel, n), out_shape=(jax.ShapeDt...  129 us
    pallas_call x1, Pallas kernels, per_device(): pl.pallas_call(results_kernel, out_shape=tuple((jax.ShapeDtypeStruct(*v)...  5.01 us

profile of v8, /device:TPU:0, one launch (start us, length us, event | category | flops | bytes accessed | tf_op | source)
XLA Modules:
  0.0 134.6 jit_solution(10020187417024989931)
XLA Ops:
  0.6 128.7 %mixer.1 = (f32[4,24,1536]{2,1,0:T(8,128)}, f32[32,128]{1,0:T(8,128)}, bf16[256,3072]{1,0:T(8,128)(2,1)}, bf16[256,3072]{1,0:T(8,128)(2,1)}, bf16[256,128]{1,0:T...) custom-call(bf16[256,3072]{1,0:T(8,128)(2,1)} %bitcast.25, ...), custom_call_target="tpu_custom_call" | custom-call | tf_op jit(solution)/shard_map/mixer/pallas_call | solution.py:761
  129.4 5.0 %results.1 = (bf16[256,1536]{1,0:T(8,128)(2,1)}, bf16[256,3072]{1,0:T(8,128)(2,1)}, bf16[256,3072]{1,0:T(8,128)(2,1)}, bf16[256,128]{1,0:T(8,128)(2,1)}, bf16[25...) custom-call(f32[4,24,1536]{2,1,0:T(8,128)} %get-tuple-element.30.w, ...), custom_call_target="tpu_custom_call" | custom-call | tf_op jit(solution)/shard_map/results/pallas_call | solution.py:795

commit v9 on v8

--- a/solution.py
+++ b/solution.py
@@ -727,8 +727,15 @@
                    bias_to, rate_to, skip_to, gain_to, w_to, *scratch):
     pairs = ((dx, dx_to), (dz, dz_to), (mixed, mixed_to), (w, w_to), (db, db_to), (dc, dc_to), (dlogit, dlogit_to))
     held, (in_sem, out_sem) = scratch[:-2], scratch[-2:]
-    into = [pltpu.make_async_copy(a, v, in_sem.at[k]) for k, ((a, _), v) in enumerate(zip(pairs, held))]
-    out = [pltpu.make_async_copy(v, b, out_sem.at[k]) for k, ((_, b), v) in enumerate(zip(pairs, held))]
+    pieces = []
+    for (a, b), v in zip(pairs, held):
+        if len(v.shape) == 2 and v.shape[0] % 64 == 0 and v.shape[1] > 128:
+            cuts = [pl.ds(lo, 64) for lo in range(0, v.shape[0], 64)]
+            pieces += [(a.at[cut], v.at[cut], b.at[cut]) for cut in cuts]
+        else:
+            pieces.append((a, v, b))
+    into = [pltpu.make_async_copy(a, v, in_sem.at[k]) for k, (a, v, _) in enumerate(pieces)]
+    out = [pltpu.make_async_copy(v, b, out_sem.at[k]) for k, (_, v, b) in enumerate(pieces)]
     for c in into:
         c.start()
     lines, heads = gain_to.shape[0], bias_to.shape[1]
@@ -798,7 +805,7 @@
         in_specs=[anywhere, vmem] + [anywhere] * 6,
         out_specs=(anywhere,) * 6 + (vmem,) * 4 + (anywhere,),
         scratch_shapes=[pltpu.VMEM(v.shape, v.dtype) for v in (dx, dz, mixed, weight_grad, db, dc, dlogit)]
-        + [pltpu.SemaphoreType.DMA((7,))] * 2,
+        + [pltpu.SemaphoreType.DMA((16,))] * 2,
         compiler_params=pltpu.CompilerParams(vmem_limit_bytes=VMEM_LIMIT),
         name="results",
     )(weight_grad, sums, dx, dz, db, dc, dlogit, mixed)

time: 135 us -> 136 us (level)
  no operation moved by 1% of the time
where the time goes in v9:
time: 136 us; the launch traced here: 135 us
  Pallas kernels  134 us (99%)
    pallas_call x1, Pallas kernels, per_device(): pl.pallas_call(functools.partial(mixer_kernel, n), out_shape=(jax.ShapeDt...  129 us
    pallas_call x1, Pallas kernels, per_device(): pl.pallas_call(results_kernel, out_shape=tuple((jax.ShapeDtypeStruct(*v)...  5.57 us

profile of v9, /device:TPU:0, one launch (start us, length us, event | category | flops | bytes accessed | tf_op | source)
XLA Modules:
  0.0 135.1 jit_solution(14256472375222158197)
XLA Ops:
  0.6 128.7 %mixer.1 = (f32[4,24,1536]{2,1,0:T(8,128)}, f32[32,128]{1,0:T(8,128)}, bf16[256,3072]{1,0:T(8,128)(2,1)}, bf16[256,3072]{1,0:T(8,128)(2,1)}, bf16[256,128]{1,0:T...) custom-call(bf16[256,3072]{1,0:T(8,128)(2,1)} %bitcast.25, ...), custom_call_target="tpu_custom_call" | custom-call | tf_op jit(solution)/shard_map/mixer/pallas_call | solution.py:768
  129.4 5.6 %results.1 = (bf16[256,1536]{1,0:T(8,128)(2,1)}, bf16[256,3072]{1,0:T(8,128)(2,1)}, bf16[256,3072]{1,0:T(8,128)(2,1)}, bf16[256,128]{1,0:T(8,128)(2,1)}, bf16[25...) custom-call(f32[4,24,1536]{2,1,0:T(8,128)} %get-tuple-element.30.w, ...), custom_call_target="tpu_custom_call" | custom-call | tf_op jit(solution)/shard_map/results/pallas_call | solution.py:802
